TPU v7x, 32 devices: a whole 2x2x4 slice. The times are simulated.
32 devices in a mesh: gx: 8 (over z, x), gy: 2 (over y), gz: 2 (over core).
Axes of the slice: x: 2, y: 2, z: 4, core: 2. Of those that a mesh axis runs over, the one named last changes fastest.
Arguments:
- basis: float32 [32768, 256], P(('gx', 'gy', 'gz'))
- target: float32 [32768, 256], P(('gx', 'gy', 'gz'))
Outputs:
- tangent: float32 [32768, 256], P(('gx', 'gy', 'gz'))
All inputs are finite; a program needn't handle non-finite values.
Results may differ from a plain program's by a relative error of at most 0.0013.
Values sent between devices are 32-bit elements; how exact they have to be, the bound alone decides.
No kernel may reach another device: no remote copies, remote signals or barrier semaphores. Data moves between devices by JAX's collectives and lax.ppermute only.
A program may use at most 64 MiB of HBM per device.

v0:
```python
import functools

import jax
import jax.numpy as jnp
import numpy as np
from jax import lax
from jax.experimental import pallas as pl
from jax.experimental.pallas import tpu as pltpu
from jax.sharding import PartitionSpec as P

half_points = [
    0.0950125098376374,
    0.2816035507792589,
    0.4580167776572274,
    0.6178762444026438,
    0.755404408355003,
    0.8656312023878318,
    0.9445750230732326,
    0.9894009349916499,
]
half_weights = [
    0.1894506104550685,
    0.1826034150449236,
    0.1691565193950025,
    0.1495959888165767,
    0.1246289712555339,
    0.0951585116824928,
    0.0622535239386479,
    0.0271524594117541,
]
points = (np.array([-v for v in half_points[::-1]] + half_points) + 1.0) / 2.0
weights = np.array(half_weights[::-1] + half_weights) / 2.0
NODES = 8
STEP = 32
F32 = jnp.float32
BF16 = jnp.bfloat16
highest = lax.Precision.HIGHEST


def iota(shape, dim):
    return lax.broadcasted_iota(jnp.int32, shape, dim)


def split(x):
    high = x.astype(BF16).astype(F32)
    rest = x - high
    mid = rest.astype(BF16).astype(F32)
    return high, mid, rest - mid


def dot(a, b):
    return jnp.dot(a, b, precision=highest, preferred_element_type=F32)


def tdot(a, b):
    return lax.dot_general(
        a, b, (((0,), (0,)), ((), ())), precision=highest, preferred_element_type=F32
    )


def gram_kernel(b_ref, t_ref, out_ref):
    n = b_ref.shape[1]
    b, t = b_ref[...], t_ref[...]
    bt, tt = b.T, t.T
    out_ref[0:n, :] = dot(bt, t)
    tgram = dot(tt, t)
    bgram = dot(bt, b)
    row, col = iota((n, n), 0), iota((n, n), 1)
    out_ref[n : 2 * n, :] = jnp.where(row < col, tgram, bgram)
    diag = row == col
    tdiag = jnp.sum(jnp.where(diag, tgram, 0.0), axis=0, keepdims=True)
    bdiag = jnp.sum(jnp.where(diag, bgram, 0.0), axis=0, keepdims=True)
    out_ref[2 * n :, :] = jnp.concatenate([tdiag, bdiag, jnp.zeros((14, n), F32)], 0)


def invert_blocks(v):
    group = iota((8, 128), 1) // NODES
    node = iota((8, 128), 1) % NODES
    row = iota((8, 128), 0)
    for g in range(4):
        q, first = g // 2, g % 2 * 8
        pan = []
        for p in range(8):
            index = node + (first + p) * NODES
            pan.append([jnp.take_along_axis(x, index, axis=1) for x in v[q]])
        for p in range(8):
            recip = 1.0 / pan[p][g][p : p + 1, :]
            new = [x for x in pan[p]]
            new[g] = jnp.where(row == p, 1.0, new[g])
            new = [x * recip for x in new]
            pan[p] = new
            for o in range(8):
                if o != p:
                    factor = pan[o][g][p : p + 1, :]
                    old = [x for x in pan[o]]
                    old[g] = jnp.where(row == p, 0.0, old[g])
                    pan[o] = [x - factor * y for x, y in zip(old, new)]
        for o in range(2):
            acc = [x for x in v[o]]
            acc[g] = jnp.zeros((8, 128), F32)
            for p in range(8):
                factor = v[o][g][p : p + 1, :]
                acc = [x - factor * y for x, y in zip(acc, pan[p])]
            if o == q:
                for p in range(8):
                    acc = [jnp.where(group == first + p, y, x) for x, y in zip(acc, pan[p])]
            v[o] = acc
    return v


def resolvent_kernel(shift_ref, weight_ref, pay_ref, out_ref, mats, turned, inverses, news):
    n = out_ref.shape[1]
    row, col = iota((n, n), 0), iota((n, n), 1)
    cross = pay_ref[0:n, :]
    packed = pay_ref[n : 2 * n, :]
    tdiag = pay_ref[2 * n : 2 * n + 1, :]
    bdiag = pay_ref[2 * n + 1 : 2 * n + 2, :]
    upper = jnp.where(row < col, packed, 0.0)
    lower = jnp.where(row > col, packed, 0.0)
    tgram = upper + upper.T + jnp.where(row == col, tdiag, 0.0)
    bgram = lower + lower.T + jnp.where(row == col, bdiag, 0.0)
    crosst = cross.T
    square = dot(crosst, cross)
    normal = tgram - 2.0 * square + dot(crosst, dot(bgram, cross))
    for m in range(NODES):
        shifted = square + shift_ref[m] * normal
        mats[0, m * n : (m + 1) * n, :] = shifted[:, 0:128]
        mats[1, m * n : (m + 1) * n, :] = shifted[:, 128:256]

    def stack(x):
        h, m, l = split(x)
        return jnp.concatenate([h, m, h, l, h, m, l, m], 0).astype(BF16)

    def step(tile, part, carry):
        inner = pl.multiple_of(part * STEP, STEP)
        start = pl.multiple_of(tile * 128 + inner, STEP)
        v = []
        for q in range(2):
            rows = [mats[tile, pl.ds(start + 16 * q + i, NODES, stride=n), :] for i in range(16)]
            turned[q] = jnp.concatenate(rows, 0).T
            block = turned[q, pl.ds(inner, STEP), :]
            v.append([block[8 * g : 8 * g + 8] for g in range(4)])
        v = invert_blocks(v)
        for q in range(2):
            h, m, l = split(jnp.concatenate(v[q], 0))
            inverses[0, q * 128 : (q + 1) * 128, :] = jnp.concatenate([h, h, m, h], 0).T
            inverses[1, q * 128 : (q + 1) * 128, :] = jnp.concatenate([l, m, m, l], 0).T

        group = iota((n, 128), 1) // STEP
        index = iota((n, 128), 1) % STEP + inner
        local = iota((STEP, n), 1) - start
        inblock = (local >= 0) & (local < STEP)
        minus = jnp.where(local == iota((STEP, n), 0), -1.0, 0.0)
        for m in range(NODES):
            left = [inverses[c, pl.ds(m, STEP, stride=NODES), :] for c in range(2)]
            left = jnp.concatenate(left, 1).astype(BF16)
            here = pl.ds(pl.multiple_of(m * n + start, STEP), STEP)
            panel = jnp.concatenate([mats[0, here, :], mats[1, here, :]], 1)
            panel = jnp.where(inblock, minus, panel)
            news[m] = jnp.dot(left, stack(panel), preferred_element_type=F32)
        for m in range(NODES):
            rows = slice(m * n, (m + 1) * n)
            columns = jnp.take_along_axis(mats[tile, rows, :], index, axis=1)
            h, d, l = split(columns)
            one = jnp.where(group == 2, d, h)
            two = jnp.where((group == 0) | (group == 3), l, d)
            lhs = jnp.concatenate([one, two], 1).astype(BF16)
            change = jnp.dot(lhs, stack(news[m]), preferred_element_type=F32)
            for c in range(2):
                half = slice(c * 128, (c + 1) * 128)
                old = mats[c, rows, :]
                if c == tile:
                    old = jnp.where(inblock[0:1, half], 0.0, old)
                mats[c, rows, :] = old - change[:, half]
        for m in range(NODES):
            here = pl.ds(pl.multiple_of(m * n + start, STEP), STEP)
            mats[0, here, :] = news[m, :, 0:128]
            mats[1, here, :] = news[m, :, 128:256]
        return carry

    for tile in range(2):
        lax.fori_loop(0, 4, functools.partial(step, tile), 0)
    for c in range(2):
        half = weight_ref[0] * mats[c, 0:n, :]
        for m in range(1, NODES):
            half = half + weight_ref[m] * mats[c, m * n : (m + 1) * n, :]
        out_ref[:, c * 128 : (c + 1) * 128] = half


def residual_kernel(pay_ref, b_ref, t_ref, out_ref):
    n = b_ref.shape[1]
    out_ref[...] = t_ref[...] - dot(b_ref[...], pay_ref[0:n, :])


def lift_kernel(scale, mine_ref, other_ref, pay_ref, z_ref, out_ref):
    n = out_ref.shape[1]
    total = (mine_ref[...] + other_ref[...]) * -scale
    out_ref[...] = dot(z_ref[...], dot(total, pay_ref[0:n, :].T))


def reduced(x, mesh):
    sizes = dict(mesh.shape)
    if any(s & (s - 1) for s in sizes.values()) or sizes["gz"] != 2:
        return lax.psum(x, ("gx", "gy", "gz"))
    me = lax.axis_index("gz")
    half = x.shape[0] // 2
    mine = lax.dynamic_slice_in_dim(x, me * half, half, 0)
    other = lax.dynamic_slice_in_dim(x, (1 - me) * half, half, 0)
    mine = mine + lax.ppermute(other, "gz", [(0, 1), (1, 0)])
    for axis in ("gy", "gx"):
        bit = 1
        while bit < sizes[axis]:
            mine = mine + lax.ppermute(mine, axis, [(i, i ^ bit) for i in range(sizes[axis])])
            bit *= 2
    other = lax.ppermute(mine, "gz", [(0, 1), (1, 0)])
    return jnp.where(me == 0, jnp.concatenate([mine, other], 0), jnp.concatenate([other, mine], 0))


def on_device(basis, target, mesh):
    rows, n = basis.shape
    total_rows = rows * mesh.size
    vmem = pl.BlockSpec(memory_space=pltpu.VMEM)
    smem = pl.BlockSpec(memory_space=pltpu.SMEM)
    limit = pltpu.CompilerParams(vmem_limit_bytes=48 * 1024 * 1024)
    pay = pl.pallas_call(
        gram_kernel,
        out_shape=jax.ShapeDtypeStruct((2 * n + 16, n), F32),
        in_specs=[vmem, vmem],
        out_specs=vmem,
        compiler_params=limit,
    )(basis, target)
    pay = reduced(pay, mesh)
    first = lax.axis_index("gz") * NODES
    shifts = lax.dynamic_slice_in_dim(jnp.asarray(points**2, F32), first, NODES)
    node_wts = lax.dynamic_slice_in_dim(jnp.asarray(weights, F32), first, NODES)
    mine = pl.pallas_call(
        resolvent_kernel,
        out_shape=jax.ShapeDtypeStruct((n, n), F32),
        in_specs=[smem, smem, vmem],
        out_specs=vmem,
        scratch_shapes=[
            pltpu.VMEM((2, NODES * n, 128), F32),
            pltpu.VMEM((2, 128, 128), F32),
            pltpu.VMEM((2, 2 * 128, 128), F32),
            pltpu.VMEM((NODES, STEP, n), F32),
        ],
        compiler_params=limit,
        cost_estimate=pl.CostEstimate(flops=10**11, bytes_accessed=10**6, transcendentals=0),
    )(shifts, node_wts, pay)
    other = lax.ppermute(mine, "gz", [(0, 1), (1, 0)])
    residual = pl.pallas_call(
        residual_kernel,
        out_shape=jax.ShapeDtypeStruct((rows, n), F32),
        in_specs=[vmem, vmem, vmem],
        out_specs=vmem,
        compiler_params=limit,
        cost_estimate=pl.CostEstimate(flops=10**9, bytes_accessed=3 * 10**6, transcendentals=0),
    )(pay, basis, target)
    return pl.pallas_call(
        functools.partial(lift_kernel, float(np.sqrt(total_rows))),
        out_shape=jax.ShapeDtypeStruct((rows, n), F32),
        in_specs=[vmem] * 4,
        out_specs=vmem,
        compiler_params=limit,
    )(mine, other, pay, residual)


def solution(mesh):
    return jax.shard_map(
        functools.partial(on_device, mesh=mesh),
        mesh=mesh,
        in_specs=(P(("gx", "gy", "gz"), None), P(("gx", "gy", "gz"), None)),
        out_specs=P(("gx", "gy", "gz"), None),
        check_vma=False,
    )
```

profile of v0, /device:TPU:0, one launch (start us, length us, event | category | flops | bytes accessed | tf_op | source)
XLA Modules:
  0.0 67.6 jit_solution(16691887927833595830)
XLA Ops:
  0.0 1.2 %copy-done = f32[1024,256]{1,0:T(8,128)S(1)} copy-done((f32[1024,256]{1,0:T(8,128)S(1)}, f32[1024,256]{1,0:T(8,128)}, u32[]{:S(2)}) %copy-start) | copy-done | bytes 1048600
  1.2 1.2 %copy-done.2 = f32[1024,256]{1,0:T(8,128)S(1)} copy-done((f32[1024,256]{1,0:T(8,128)S(1)}, f32[1024,256]{1,0:T(8,128)}, u32[]{:S(2)}) %copy-start.2) | copy-done | bytes 1048600
  2.5 3.0 %shard_map.46 = f32[528,256]{1,0:T(8,128)S(1)} custom-call(f32[1024,256]{1,0:T(8,128)S(1)} %copy-done, f32[1024,256]{1,0:T(8,128)S(1)} %copy-done.2), custom_call_target="tpu_custom_call" | custom-call | tf_op jit(solution)/shard_map/pallas_call | solution.py:225
  5.5 0.5 collective-permute-start
  6.0 1.2 %collective-permute-done = f32[264,256]{1,0:T(8,128)S(1)} collective-permute-done((f32[264,256]{1,0:T(8,128)S(1)}, f32[264,256]{1,0:T(8,128)S(1)}, u32[]{:S(2)}, u32[]{:S(2)}) %collective-permute-start) | collective-permute-done | bytes 270368 | tf_op jit(solution)/shard_map/ppermute | solution.py:209
  7.2 3.0 %collective-permute-start.1 = (f32[264,256]{1,0:T(8,128)S(1)}, f32[264,256]{1,0:T(8,128)S(1)}, u32[]{:S(2)}, u32[]{:S(2)}) collective-permute-start(f32[264,256]{1,0:T(8,128)S(1)} %dynamic-slice_add_fusion), channel_id=1, source_target_pairs={{0,2},{2,0},{1,3},{3,1},{4,6},{6,4},{5,7},{7,5},{8,10},{10,8},{9,1... | collective-permute-start | bytes 811016 | tf_op jit(solution)/shard_map/ppermute | solution.py:213
  10.1 6.8 %collective-permute-done.1 = f32[264,256]{1,0:T(8,128)S(1)} collective-permute-done((f32[264,256]{1,0:T(8,128)S(1)}, f32[264,256]{1,0:T(8,128)S(1)}, u32[]{:S(2)}, u32[]{:S(2)}) %collective-permute-start.1) | collective-permute-done | bytes 270368 | tf_op jit(solution)/shard_map/ppermute | solution.py:213
  17.0 1.8 %collective-permute-start.2 = (f32[264,256]{1,0:T(8,128)S(1)}, f32[264,256]{1,0:T(8,128)S(1)}, u32[]{:S(2)}, u32[]{:S(2)}) collective-permute-start(f32[264,256]{1,0:T(8,128)S(1)} %add.29), channel_id=1, source_target_pairs={{0,4},{4,0},{8,12},{12,8},{16,20},{20,16},{24,28},{28,24},{1,5},{5... | collective-permute-start | bytes 811016 | tf_op jit(solution)/shard_map/ppermute | solution.py:213
  18.7 6.3 %collective-permute-done.2 = f32[264,256]{1,0:T(8,128)S(1)} collective-permute-done((f32[264,256]{1,0:T(8,128)S(1)}, f32[264,256]{1,0:T(8,128)S(1)}, u32[]{:S(2)}, u32[]{:S(2)}) %collective-permute-start.2) | collective-permute-done | bytes 270368 | tf_op jit(solution)/shard_map/ppermute | solution.py:213
  25.1 1.5 %collective-permute-start.3 = (f32[264,256]{1,0:T(8,128)S(1)}, f32[264,256]{1,0:T(8,128)S(1)}, u32[]{:S(2)}, u32[]{:S(2)}) collective-permute-start(f32[264,256]{1,0:T(8,128)S(1)} %add.30), channel_id=1, source_target_pairs={{0,8},{4,12},{8,0},{12,4},{16,24},{20,28},{24,16},{28,20},{1,9},{5... | collective-permute-start | bytes 811016 | tf_op jit(solution)/shard_map/ppermute | solution.py:213
  26.6 5.6 %collective-permute-done.3 = f32[264,256]{1,0:T(8,128)S(1)} collective-permute-done((f32[264,256]{1,0:T(8,128)S(1)}, f32[264,256]{1,0:T(8,128)S(1)}, u32[]{:S(2)}, u32[]{:S(2)}) %collective-permute-start.3) | collective-permute-done | bytes 270368 | tf_op jit(solution)/shard_map/ppermute | solution.py:213
  32.3 2.2 %collective-permute-start.4 = (f32[264,256]{1,0:T(8,128)S(1)}, f32[264,256]{1,0:T(8,128)S(1)}, u32[]{:S(2)}, u32[]{:S(2)}) collective-permute-start(f32[264,256]{1,0:T(8,128)S(1)} %add.31), channel_id=1, source_target_pairs={{0,16},{4,20},{8,24},{12,28},{16,0},{20,4},{24,8},{28,12},{1,17},{... | collective-permute-start | bytes 811016 | tf_op jit(solution)/shard_map/ppermute | solution.py:213
  34.5 10.7 %collective-permute-done.4 = f32[264,256]{1,0:T(8,128)S(1)} collective-permute-done((f32[264,256]{1,0:T(8,128)S(1)}, f32[264,256]{1,0:T(8,128)S(1)}, u32[]{:S(2)}, u32[]{:S(2)}) %collective-permute-start.4) | collective-permute-done | bytes 270368 | tf_op jit(solution)/shard_map/ppermute | solution.py:213
  45.3 0.1 collective-permute-start.5
  45.4 0.6 copy-done.5
  46.0 0.1 dynamic_slice.12.shift_ref
  46.1 0.6 copy-done.4
  46.7 0.1 dynamic_slice.13.weight_ref
  46.7 0.1 collective-permute-done.5
  47.0 16.3 %shard_map.47.mine_ref = f32[256,256]{1,0:T(8,128)S(1)} custom-call(f32[8]{0:T(128)S(1)} %dynamic_slice.12.shift_ref, f32[8]{0:T(128)S(1)} %dynamic_slice.13.weight_ref, f32[528,256]{1,0:T(8,128)S(1)} %maximum_select_fusion.pay_ref), custom_call_target="tpu_custom_call" | custom-call | flops 99999997952 | bytes 1000000 | tf_op jit(solution)/shard_map/pallas_call | solution.py:236
  63.2 0.4 collective-permute-start.6
  63.7 1.0 %shard_map.48.z_ref = f32[1024,256]{1,0:T(8,128)S(1)} custom-call(f32[528,256]{1,0:T(8,128)S(1)} %maximum_select_fusion.pay_ref, f32[1024,256]{1,0:T(8,128)S(1)} %copy-done.1, f32[1024,256]{1,0:T(8,128)S(1)} %copy-done.3), custom_call_target="tpu_custom_call" | custom-call | flops 1000000000 | bytes 3000000 | tf_op jit(solution)/shard_map/pallas_call | solution.py:251
  64.7 0.2 collective-permute-done.6.other_ref
  64.8 2.7 %shard_map.49 = f32[1024,256]{1,0:T(8,128)} custom-call(f32[256,256]{1,0:T(8,128)S(1)} %shard_map.47.mine_ref, f32[256,256]{1,0:T(8,128)S(1)} %collective-permute-done.6.other_ref, f32[528,256]{1,0:T(8,128)S(1)} %maximum_select_fusion.pay_ref, f32[1024,256]{1,0:T(8,128)S(1)} %shard_map.48.z_ref), custom_call_target="tpu_custom_call" | custom-call | tf_op jit(solution)/shard_map/pallas_call | solution.py:259
  (15 shorter events, 0.3 us)
Async XLA Ops:
  0.0 1.2 %copy-start = (f32[1024,256]{1,0:T(8,128)S(1)}, f32[1024,256]{1,0:T(8,128)}, u32[]{:S(2)}) copy-start(f32[1024,256]{1,0:T(8,128)} %b_ref.3) | copy-start | bytes 3145732
  1.2 1.2 %copy-start.2 = (f32[1024,256]{1,0:T(8,128)S(1)}, f32[1024,256]{1,0:T(8,128)}, u32[]{:S(2)}) copy-start(f32[1024,256]{1,0:T(8,128)} %t_ref.3) | copy-start | bytes 3145732
  5.5 1.7 %collective-permute-start = (f32[264,256]{1,0:T(8,128)S(1)}, f32[264,256]{1,0:T(8,128)S(1)}, u32[]{:S(2)}, u32[]{:S(2)}) collective-permute-start(f32[264,256]{1,0:T(8,128)S(1)} %constant_dynamic-slice_fusion), channel_id=1, source_target_pairs={{0,1},{1,0},{2,3},{3,2},{4,5},{5,4},{6,7},{7,6},{8,9},{9,8},{10,11... | collective-permute-start | bytes 811016 | tf_op jit(solution)/shard_map/ppermute | solution.py:209
  7.2 9.7 %collective-permute-start.1 = (f32[264,256]{1,0:T(8,128)S(1)}, f32[264,256]{1,0:T(8,128)S(1)}, u32[]{:S(2)}, u32[]{:S(2)}) collective-permute-start(f32[264,256]{1,0:T(8,128)S(1)} %dynamic-slice_add_fusion), channel_id=1, source_target_pairs={{0,2},{2,0},{1,3},{3,1},{4,6},{6,4},{5,7},{7,5},{8,10},{10,8},{9,1... | collective-permute-start | bytes 811016 | tf_op jit(solution)/shard_map/ppermute | solution.py:213
  17.0 8.1 %collective-permute-start.2 = (f32[264,256]{1,0:T(8,128)S(1)}, f32[264,256]{1,0:T(8,128)S(1)}, u32[]{:S(2)}, u32[]{:S(2)}) collective-permute-start(f32[264,256]{1,0:T(8,128)S(1)} %add.29), channel_id=1, source_target_pairs={{0,4},{4,0},{8,12},{12,8},{16,20},{20,16},{24,28},{28,24},{1,5},{5... | collective-permute-start | bytes 811016 | tf_op jit(solution)/shard_map/ppermute | solution.py:213
  25.1 7.2 %collective-permute-start.3 = (f32[264,256]{1,0:T(8,128)S(1)}, f32[264,256]{1,0:T(8,128)S(1)}, u32[]{:S(2)}, u32[]{:S(2)}) collective-permute-start(f32[264,256]{1,0:T(8,128)S(1)} %add.30), channel_id=1, source_target_pairs={{0,8},{4,12},{8,0},{12,4},{16,24},{20,28},{24,16},{28,20},{1,9},{5... | collective-permute-start | bytes 811016 | tf_op jit(solution)/shard_map/ppermute | solution.py:213
  32.3 12.9 %collective-permute-start.4 = (f32[264,256]{1,0:T(8,128)S(1)}, f32[264,256]{1,0:T(8,128)S(1)}, u32[]{:S(2)}, u32[]{:S(2)}) collective-permute-start(f32[264,256]{1,0:T(8,128)S(1)} %add.31), channel_id=1, source_target_pairs={{0,16},{4,20},{8,24},{12,28},{16,0},{20,4},{24,8},{28,12},{1,17},{... | collective-permute-start | bytes 811016 | tf_op jit(solution)/shard_map/ppermute | solution.py:213
  45.3 1.6 %collective-permute-start.5 = (f32[264,256]{1,0:T(8,128)S(1)}, f32[264,256]{1,0:T(8,128)S(1)}, u32[]{:S(2)}, u32[]{:S(2)}) collective-permute-start(f32[264,256]{1,0:T(8,128)S(1)} %add.32), channel_id=1, source_target_pairs={{0,1},{1,0},{2,3},{3,2},{4,5},{5,4},{6,7},{7,6},{8,9},{9,8},{10,11... | collective-permute-start | bytes 811016 | tf_op jit(solution)/shard_map/ppermute | solution.py:215
  45.4 0.7 copy-start.5
  46.0 0.7 copy-start.4
  46.9 16.7 %copy-start.1 = (f32[1024,256]{1,0:T(8,128)S(1)}, f32[1024,256]{1,0:T(8,128)}, u32[]{:S(2)}) copy-start(f32[1024,256]{1,0:T(8,128)} %b_ref.3) | copy-start | bytes 3145732
  46.9 16.7 %copy-start.3 = (f32[1024,256]{1,0:T(8,128)S(1)}, f32[1024,256]{1,0:T(8,128)}, u32[]{:S(2)}) copy-start(f32[1024,256]{1,0:T(8,128)} %t_ref.3) | copy-start | bytes 3145732
  63.2 1.6 %collective-permute-start.6 = (f32[256,256]{1,0:T(8,128)S(1)}, f32[256,256]{1,0:T(8,128)S(1)}, u32[]{:S(2)}, u32[]{:S(2)}) collective-permute-start(f32[256,256]{1,0:T(8,128)S(1)} %shard_map.47.mine_ref), channel_id=1, source_target_pairs={{0,1},{1,0},{2,3},{3,2},{4,5},{5,4},{6,7},{7,6},{8,9},{9,8},{10,11... | collective-permute-start | bytes 786440 | tf_op jit(solution)/shard_map/ppermute | solution.py:250
where the time goes:
time: 67.8 us; the launch traced here: 67.6 us
  waiting for transfers between devices  30.9 us (46%)
  Pallas kernels  23 us (34%)
  starting transfers between devices  9.49 us (14%)
  local copies, waits for them, and re-layouts  3.87 us (6%)
    ppermute x4, waiting for transfers between devices, reduced(): lax.ppermute(mine, axis, [(i, i ^ bit) for i in range(sizes[axis])])  29.4 us
    pallas_call x1, Pallas kernels, on_device(): pl.pallas_call(resolvent_kernel, out_shape=jax.ShapeDtypeStruct((n, n), F...  16.3 us
    ppermute x4, starting transfers between devices, reduced(): lax.ppermute(mine, axis, [(i, i ^ bit) for i in range(sizes[axis])])  8.49 us
    unnamed x12, local copies, waits for them, and re-layouts  3.69 us
    pallas_call x1, Pallas kernels, on_device(): pl.pallas_call(gram_kernel, out_shape=jax.ShapeDtypeStruct((2 * n + 16, n...  2.97 us
    pallas_call x1, Pallas kernels, on_device(): pl.pallas_call(functools.partial(lift_kernel, float(np.sqrt(total_rows)))...  2.74 us
  transfers between devices with their start and end apart: 7, of which 7 were waited for; matrix products, arithmetic and copies ran while one was open for 0% of the time, Pallas kernels for 1%

commit v1 on v0

--- a/solution.py
+++ b/solution.py
@@ -31,6 +31,11 @@
 points = (np.array([-v for v in half_points[::-1]] + half_points) + 1.0) / 2.0
 weights = np.array(half_weights[::-1] + half_weights) / 2.0
 NODES = 8
+CHUNKS = 4
+CUBE = 8
+PIECE = 72
+HALF = CUBE * PIECE
+PAY_ROWS = 2 * HALF
 STEP = 32
 F32 = jnp.float32
 BF16 = jnp.bfloat16
@@ -52,25 +57,73 @@
     return jnp.dot(a, b, precision=highest, preferred_element_type=F32)
 
 
-def tdot(a, b):
-    return lax.dot_general(
-        a, b, (((0,), (0,)), ((), ())), precision=highest, preferred_element_type=F32
-    )
-
-
-def gram_kernel(b_ref, t_ref, out_ref):
-    n = b_ref.shape[1]
-    b, t = b_ref[...], t_ref[...]
-    bt, tt = b.T, t.T
-    out_ref[0:n, :] = dot(bt, t)
-    tgram = dot(tt, t)
-    bgram = dot(bt, b)
+def halves(x):
+    high = x.astype(BF16)
+    return high, (x - high.astype(F32)).astype(BF16)
+
+
+def dot3(a, b):
+    (ah, al), (bh, bl) = a, b
+    total = jnp.dot(ah, bl, preferred_element_type=F32) + jnp.dot(al, bh, preferred_element_type=F32)
+    return total + jnp.dot(ah, bh, preferred_element_type=F32)
+
+
+def gram_kernel(where_ref, b_hbm, t_hbm, keep_ref, send_ref, b_ref, t_ref, pay, sems):
+    rows, n = b_ref.shape
+    chunk = rows // CHUNKS
+    copies = []
+    for c in range(CHUNKS):
+        part = pl.ds(c * chunk, chunk)
+        for k, (source, dest) in enumerate(((b_hbm, b_ref), (t_hbm, t_ref))):
+            copy = pltpu.make_async_copy(source.at[part], dest.at[part], sems.at[k, c])
+            copy.start()
+            copies.append(copy)
+    cross = tgram = bgram = jnp.zeros((n, n), F32)
+    for c in range(CHUNKS):
+        part = slice(c * chunk, (c + 1) * chunk)
+        copies[2 * c].wait()
+        copies[2 * c + 1].wait()
+        b, t = b_ref[part, :], t_ref[part, :]
+        b, bt, t, tt = halves(b), halves(b.T), halves(t), halves(t.T)
+        cross += dot3(bt, t)
+        tgram += dot3(tt, t)
+        bgram += dot3(bt, b)
     row, col = iota((n, n), 0), iota((n, n), 1)
-    out_ref[n : 2 * n, :] = jnp.where(row < col, tgram, bgram)
+    packed = jnp.where(row < col, tgram, bgram)
     diag = row == col
     tdiag = jnp.sum(jnp.where(diag, tgram, 0.0), axis=0, keepdims=True)
     bdiag = jnp.sum(jnp.where(diag, bgram, 0.0), axis=0, keepdims=True)
-    out_ref[2 * n :, :] = jnp.concatenate([tdiag, bdiag, jnp.zeros((14, n), F32)], 0)
+    for c in range(2):
+        half = slice(c * 128, (c + 1) * 128)
+        pay[c * n : (c + 1) * n, :] = cross[:, half]
+        pay[(2 + c) * n : (3 + c) * n, :] = packed[:, half]
+    pay[4 * n :, :] = jnp.zeros((PAY_ROWS - 4 * n, 128), F32)
+    for c in range(2):
+        half = slice(c * 128, (c + 1) * 128)
+        pay[4 * n + c : 4 * n + c + 1, :] = tdiag[:, half]
+        pay[4 * n + 2 + c : 4 * n + 3 + c, :] = bdiag[:, half]
+    core = where_ref[0]
+    keep_ref[...] = pay[pl.ds(pl.multiple_of(core * HALF, 8), HALF), :]
+    send_ref[...] = pay[pl.ds(pl.multiple_of((1 - core) * HALF, 8), HALF), :]
+
+
+def scatter_kernel(where_ref, keep_ref, got_ref, *out_refs):
+    for mask, out_ref in enumerate(out_refs):
+        rows = pl.ds(pl.multiple_of((where_ref[1] ^ mask) * PIECE, 8), PIECE)
+        out_ref[...] = keep_ref[rows, :] + got_ref[rows, :]
+
+
+def sum_kernel(*refs):
+    total = refs[0][...]
+    for ref in refs[1:-1]:
+        total = total + ref[...]
+    refs[-1][...] = total
+
+
+def gather_kernel(where_ref, *refs):
+    for mask, ref in enumerate(refs[:-1]):
+        rows = pl.ds(pl.multiple_of((where_ref[1] ^ mask) * PIECE, 8), PIECE)
+        refs[-1][rows, :] = ref[...]
 
 
 def invert_blocks(v):
@@ -108,13 +161,21 @@
     return v
 
 
-def resolvent_kernel(shift_ref, weight_ref, pay_ref, out_ref, mats, turned, inverses, news):
+def resolvent_kernel(
+    where_ref, shift_ref, weight_ref, mine_ref, other_ref, out_ref, cross_ref, mats, turned, inverses, news, pay
+):
     n = out_ref.shape[1]
+    core = where_ref[0]
+    pay[pl.ds(pl.multiple_of(core * HALF, 8), HALF), :] = mine_ref[...]
+    pay[pl.ds(pl.multiple_of((1 - core) * HALF, 8), HALF), :] = other_ref[...]
     row, col = iota((n, n), 0), iota((n, n), 1)
-    cross = pay_ref[0:n, :]
-    packed = pay_ref[n : 2 * n, :]
-    tdiag = pay_ref[2 * n : 2 * n + 1, :]
-    bdiag = pay_ref[2 * n + 1 : 2 * n + 2, :]
+
+    def wide(start, rows):
+        return jnp.concatenate([pay[start : start + rows, :], pay[start + rows : start + 2 * rows, :]], 1)
+
+    cross, packed = wide(0, n), wide(2 * n, n)
+    cross_ref[...] = cross
+    tdiag, bdiag = wide(4 * n, 1), wide(4 * n + 2, 1)
     upper = jnp.where(row < col, packed, 0.0)
     lower = jnp.where(row > col, packed, 0.0)
     tgram = upper + upper.T + jnp.where(row == col, tdiag, 0.0)
@@ -187,33 +248,26 @@
         out_ref[:, c * 128 : (c + 1) * 128] = half
 
 
-def residual_kernel(pay_ref, b_ref, t_ref, out_ref):
-    n = b_ref.shape[1]
-    out_ref[...] = t_ref[...] - dot(b_ref[...], pay_ref[0:n, :])
-
-
-def lift_kernel(scale, mine_ref, other_ref, pay_ref, z_ref, out_ref):
-    n = out_ref.shape[1]
+def residual_kernel(cross_ref, b_ref, t_ref, out_ref):
+    out_ref[...] = t_ref[...] - dot3(halves(b_ref[...]), halves(cross_ref[...]))
+
+
+def lift_kernel(scale, mine_ref, other_ref, cross_ref, z_ref, out_ref):
     total = (mine_ref[...] + other_ref[...]) * -scale
-    out_ref[...] = dot(z_ref[...], dot(total, pay_ref[0:n, :].T))
-
-
-def reduced(x, mesh):
-    sizes = dict(mesh.shape)
-    if any(s & (s - 1) for s in sizes.values()) or sizes["gz"] != 2:
-        return lax.psum(x, ("gx", "gy", "gz"))
-    me = lax.axis_index("gz")
-    half = x.shape[0] // 2
-    mine = lax.dynamic_slice_in_dim(x, me * half, half, 0)
-    other = lax.dynamic_slice_in_dim(x, (1 - me) * half, half, 0)
-    mine = mine + lax.ppermute(other, "gz", [(0, 1), (1, 0)])
-    for axis in ("gy", "gx"):
-        bit = 1
-        while bit < sizes[axis]:
-            mine = mine + lax.ppermute(mine, axis, [(i, i ^ bit) for i in range(sizes[axis])])
-            bit *= 2
-    other = lax.ppermute(mine, "gz", [(0, 1), (1, 0)])
-    return jnp.where(me == 0, jnp.concatenate([mine, other], 0), jnp.concatenate([other, mine], 0))
+    right = halves(dot(total, cross_ref[...].T))
+    out_ref[...] = dot3(halves(z_ref[...]), right)
+
+
+AXES = ("gx", "gy", "gz")
+
+
+def exchange(x, mesh, gx=0, gy=0, gz=0):
+    ny, nz = mesh.shape["gy"], mesh.shape["gz"]
+    perm = []
+    for i in range(mesh.size):
+        x0, y0, z0 = i // (ny * nz), i // nz % ny, i % nz
+        perm.append((i, ((x0 ^ gx) * ny + (y0 ^ gy)) * nz + (z0 ^ gz)))
+    return lax.ppermute(x, AXES, perm)
 
 
 def on_device(basis, target, mesh):
@@ -221,33 +275,64 @@
     total_rows = rows * mesh.size
     vmem = pl.BlockSpec(memory_space=pltpu.VMEM)
     smem = pl.BlockSpec(memory_space=pltpu.SMEM)
+    hbm = pl.BlockSpec(memory_space=pltpu.HBM)
     limit = pltpu.CompilerParams(vmem_limit_bytes=48 * 1024 * 1024)
-    pay = pl.pallas_call(
+    core, gx, gy = lax.axis_index("gz"), lax.axis_index("gx"), lax.axis_index("gy")
+    where = jnp.stack([core, (gx & 3) + 4 * (gy & 1)]).astype(jnp.int32)
+    half = jax.ShapeDtypeStruct((HALF, 128), F32)
+    piece = jax.ShapeDtypeStruct((PIECE, 128), F32)
+    keep, send = pl.pallas_call(
         gram_kernel,
-        out_shape=jax.ShapeDtypeStruct((2 * n + 16, n), F32),
-        in_specs=[vmem, vmem],
-        out_specs=vmem,
-        compiler_params=limit,
-    )(basis, target)
-    pay = reduced(pay, mesh)
-    first = lax.axis_index("gz") * NODES
+        out_shape=(half, half),
+        in_specs=[smem, hbm, hbm],
+        out_specs=(vmem, vmem),
+        scratch_shapes=[
+            pltpu.VMEM((rows, n), F32),
+            pltpu.VMEM((rows, n), F32),
+            pltpu.VMEM((PAY_ROWS, 128), F32),
+            pltpu.SemaphoreType.DMA((2, CHUNKS)),
+        ],
+    )(where, basis, target)
+    pieces = pl.pallas_call(
+        scatter_kernel,
+        out_shape=(piece,) * CUBE,
+        in_specs=[smem, vmem, vmem],
+        out_specs=(vmem,) * CUBE,
+    )(where, keep, exchange(send, mesh, gz=1))
+    masks = [(mask & 3, mask >> 2) for mask in range(CUBE)]
+    got = [exchange(pieces[m], mesh, gx=masks[m][0], gy=masks[m][1]) for m in range(1, CUBE)]
+    mine = pl.pallas_call(
+        sum_kernel, out_shape=piece, in_specs=[vmem] * CUBE, out_specs=vmem
+    )(pieces[0], *got)
+    for bit in range(2, (mesh.shape["gx"] - 1).bit_length()):
+        mine = mine + exchange(mine, mesh, gx=1 << bit)
+    for bit in range(1, (mesh.shape["gy"] - 1).bit_length()):
+        mine = mine + exchange(mine, mesh, gy=1 << bit)
+    got = [exchange(mine, mesh, gx=masks[m][0], gy=masks[m][1]) for m in range(1, CUBE)]
+    mine = pl.pallas_call(
+        gather_kernel, out_shape=half, in_specs=[smem] + [vmem] * CUBE, out_specs=vmem
+    )(where, mine, *got)
+    other = exchange(mine, mesh, gz=1)
+    first = core * NODES
     shifts = lax.dynamic_slice_in_dim(jnp.asarray(points**2, F32), first, NODES)
     node_wts = lax.dynamic_slice_in_dim(jnp.asarray(weights, F32), first, NODES)
-    mine = pl.pallas_call(
+    square = jax.ShapeDtypeStruct((n, n), F32)
+    part, cross = pl.pallas_call(
         resolvent_kernel,
-        out_shape=jax.ShapeDtypeStruct((n, n), F32),
-        in_specs=[smem, smem, vmem],
-        out_specs=vmem,
+        out_shape=(square, square),
+        in_specs=[smem, smem, smem, vmem, vmem],
+        out_specs=(vmem, vmem),
         scratch_shapes=[
             pltpu.VMEM((2, NODES * n, 128), F32),
             pltpu.VMEM((2, 128, 128), F32),
             pltpu.VMEM((2, 2 * 128, 128), F32),
             pltpu.VMEM((NODES, STEP, n), F32),
+            pltpu.VMEM((PAY_ROWS, 128), F32),
         ],
         compiler_params=limit,
         cost_estimate=pl.CostEstimate(flops=10**11, bytes_accessed=10**6, transcendentals=0),
-    )(shifts, node_wts, pay)
-    other = lax.ppermute(mine, "gz", [(0, 1), (1, 0)])
+    )(where, shifts, node_wts, mine, other)
+    other = exchange(part, mesh, gz=1)
     residual = pl.pallas_call(
         residual_kernel,
         out_shape=jax.ShapeDtypeStruct((rows, n), F32),
@@ -255,14 +340,14 @@
         out_specs=vmem,
         compiler_params=limit,
         cost_estimate=pl.CostEstimate(flops=10**9, bytes_accessed=3 * 10**6, transcendentals=0),
-    )(pay, basis, target)
+    )(cross, basis, target)
     return pl.pallas_call(
         functools.partial(lift_kernel, float(np.sqrt(total_rows))),
         out_shape=jax.ShapeDtypeStruct((rows, n), F32),
         in_specs=[vmem] * 4,
         out_specs=vmem,
         compiler_params=limit,
-    )(mine, other, pay, residual)
+    )(part, other, cross, residual)
 
 
 def solution(mesh):

time: 67.8 us -> 72.5 us (1.069)
  waiting for transfers between devices: 30.9 us -> 13.5 us
  starting transfers between devices: 9.49 us -> 23.4 us
  Pallas kernels: 23 us -> 29.2 us
  other arithmetic: 0.21 us -> 1.33 us
    ppermute x7 -> x18, waiting for transfers between devices: 30.9 us -> 13.5 us  [exchange(): return lax.ppermute(x, AXES, perm)]
    ppermute x7 -> x18, starting transfers between devices: 9.49 us -> 23.4 us  [exchange(): return lax.ppermute(x, AXES, perm)]
    pallas_call x2 -> x5, Pallas kernels: 19.2 us -> 26.3 us  [the longest x1 16.4 us: on_device(): pl.pallas_call(resolvent_kernel, out_shape=(square, square), in_specs=[sm...]
    unnamed x12 -> x44, local copies, waits for them, and re-layouts: 3.69 us -> 4.36 us
  transfers between devices with their start and end apart: 7 -> 18, of which waited for: 7 -> 9; matrix products, arithmetic and copies ran while one was open for 0% -> 0% of each run, Pallas kernels for 1% -> 1%
where the time goes in v1:
time: 72.5 us; the launch traced here: 72.1 us
  Pallas kernels  29.2 us (40%)
  starting transfers between devices  23.4 us (32%)
  waiting for transfers between devices  13.5 us (19%)
  local copies, waits for them, and re-layouts  4.51 us (6%)
  other arithmetic  1.33 us (2%)
    ppermute x18, starting transfers between devices, exchange(): return lax.ppermute(x, AXES, perm)  23.4 us
    pallas_call x1, Pallas kernels, on_device(): pl.pallas_call(resolvent_kernel, out_shape=(square, square), in_specs=[sm...  16.4 us
    ppermute x18, waiting for transfers between devices, exchange(): return lax.ppermute(x, AXES, perm)  13.5 us
    pallas_call x1, Pallas kernels, on_device(): pl.pallas_call(gram_kernel, out_shape=(half, half), in_specs=[smem, hbm,...  4.97 us
    unnamed x44, local copies, waits for them, and re-layouts  4.36 us
    pallas_call x1, Pallas kernels, on_device(): pl.pallas_call(functools.partial(lift_kernel, float(np.sqrt(total_rows)))...  2.31 us
    pallas_call x1, Pallas kernels, on_device(): pl.pallas_call(scatter_kernel, out_shape=(piece,) * CUBE, in_specs=[smem,...  1.81 us
    pallas_call x1, Pallas kernels, on_device(): pl.pallas_call(gather_kernel, out_shape=half, in_specs=[smem] + [vmem] *...  1.64 us
  transfers between devices with their start and end apart: 18, of which 9 were waited for; matrix products, arithmetic and copies ran while one was open for 0% of the time, Pallas kernels for 1%

profile of v1, /device:TPU:0, one launch (start us, length us, event | category | flops | bytes accessed | tf_op | source)
XLA Modules:
  0.0 72.1 jit_solution(17411574175176586808)
XLA Ops:
  0.6 5.0 %shard_map.46 = (f32[576,128]{1,0:T(8,128)}, f32[576,128]{1,0:T(8,128)}) custom-call(s32[2]{0:T(128)} %pad_add_fusion.where_ref, f32[1024,256]{1,0:T(8,128)} %b_ref.1, f32[1024,256]{1,0:T(8,128)} %t_ref.1), custom_call_target="tpu_custom_call" | custom-call | tf_op jit(solution)/shard_map/pallas_call | solution.py:284
  6.1 1.4 %collective-permute-done.got_ref = f32[576,128]{1,0:T(8,128)S(1)} collective-permute-done((f32[576,128]{1,0:T(8,128)}, f32[576,128]{1,0:T(8,128)S(1)}, u32[]{:S(2)}, u32[]{:S(2)}) %collective-permute-start) | collective-permute-done | bytes 294944 | tf_op jit(solution)/shard_map/ppermute | solution.py:270
  8.2 1.8 %shard_map.47 = (f32[72,128]{1,0:T(8,128)}, f32[72,128]{1,0:T(8,128)}, f32[72,128]{1,0:T(8,128)}, f32[72,128]{1,0:T(8,128)}, f32[72,128]{1,0:T(8,128)}, /*index=...) custom-call(s32[2]{0:T(128)} %pad_add_fusion.where_ref, f32[576,128]{1,0:T(8,128)} %get-tuple-element.17.keep_ref, ...), custom_call_target="tpu_custom_call" | custom-call | tf_op jit(solution)/shard_map/pallas_call | solution.py:296
  10.0 2.9 %collective-permute-start.1 = (f32[72,128]{1,0:T(8,128)}, f32[72,128]{1,0:T(8,128)S(1)}, u32[]{:S(2)}, u32[]{:S(2)}) collective-permute-start(f32[72,128]{1,0:T(8,128)} %get-tuple-element.20), channel_id=1, source_target_pairs={{0,4},{1,5},{2,6},{3,7},{4,0},{5,1},{6,2},{7,3},{8,12},{9,13},{10,... | collective-permute-start | bytes 110600 | tf_op jit(solution)/shard_map/ppermute | solution.py:270
  12.9 1.6 %collective-permute-start.2 = (f32[72,128]{1,0:T(8,128)}, f32[72,128]{1,0:T(8,128)S(1)}, u32[]{:S(2)}, u32[]{:S(2)}) collective-permute-start(f32[72,128]{1,0:T(8,128)} %get-tuple-element.21), channel_id=1, source_target_pairs={{0,8},{1,9},{2,10},{3,11},{4,12},{5,13},{6,14},{7,15},{8,0},{9,1},... | collective-permute-start | bytes 110600 | tf_op jit(solution)/shard_map/ppermute | solution.py:270
  14.5 1.9 %collective-permute-start.4 = (f32[72,128]{1,0:T(8,128)}, f32[72,128]{1,0:T(8,128)S(1)}, u32[]{:S(2)}, u32[]{:S(2)}) collective-permute-start(f32[72,128]{1,0:T(8,128)} %get-tuple-element.23), channel_id=1, source_target_pairs={{0,2},{1,3},{2,0},{3,1},{4,6},{5,7},{6,4},{7,5},{8,10},{9,11},{10,... | collective-permute-start | bytes 110600 | tf_op jit(solution)/shard_map/ppermute | solution.py:270
  16.4 1.4 %collective-permute-start.5 = (f32[72,128]{1,0:T(8,128)}, f32[72,128]{1,0:T(8,128)S(1)}, u32[]{:S(2)}, u32[]{:S(2)}) collective-permute-start(f32[72,128]{1,0:T(8,128)} %get-tuple-element.24), channel_id=1, source_target_pairs={{0,6},{1,7},{2,4},{3,5},{4,2},{5,3},{6,0},{7,1},{8,14},{9,15},{10,... | collective-permute-start | bytes 110600 | tf_op jit(solution)/shard_map/ppermute | solution.py:270
  17.8 2.5 %collective-permute-start.6 = (f32[72,128]{1,0:T(8,128)}, f32[72,128]{1,0:T(8,128)S(1)}, u32[]{:S(2)}, u32[]{:S(2)}) collective-permute-start(f32[72,128]{1,0:T(8,128)} %get-tuple-element.25), channel_id=1, source_target_pairs={{0,10},{1,11},{2,8},{3,9},{4,14},{5,15},{6,12},{7,13},{8,2},{9,3},... | collective-permute-start | bytes 110600 | tf_op jit(solution)/shard_map/ppermute | solution.py:270
  21.5 1.8 %collective-permute-done.6.refs_6_ = f32[72,128]{1,0:T(8,128)S(1)} collective-permute-done((f32[72,128]{1,0:T(8,128)}, f32[72,128]{1,0:T(8,128)S(1)}, u32[]{:S(2)}, u32[]{:S(2)}) %collective-permute-start.6) | collective-permute-done | bytes 36896 | tf_op jit(solution)/shard_map/ppermute | solution.py:270
  23.3 3.0 %collective-permute-done.7.refs_7_ = f32[72,128]{1,0:T(8,128)S(1)} collective-permute-done((f32[72,128]{1,0:T(8,128)}, f32[72,128]{1,0:T(8,128)S(1)}, u32[]{:S(2)}, u32[]{:S(2)}) %collective-permute-start.7) | collective-permute-done | bytes 36896 | tf_op jit(solution)/shard_map/ppermute | solution.py:270
  26.9 1.5 %shard_map.48 = f32[72,128]{1,0:T(8,128)} custom-call(f32[72,128]{1,0:T(8,128)} %get-tuple-element.19.refs_0_, f32[72,128]{1,0:T(8,128)} %copy-done.6, f32[72,128]{1,0:T(8,128)} %copy-done.7, f32[72,128]{1,0:T(8,128)} %copy-done.8, f32[72,128]{1,0:T(8,128)} %copy-done.9, f32[72,128]{1,0:T(8,128)} %copy-done.10, f32[72,128]{1,0:T(8,128)} %copy-done.11, ...), custom_call_target="tpu_custom_call" | custom-call | tf_op jit(solution)/shard_map/pallas_call | solution.py:304
  28.5 2.6 %collective-permute-start.8 = (f32[72,128]{1,0:T(8,128)}, f32[72,128]{1,0:T(8,128)S(1)}, u32[]{:S(2)}, u32[]{:S(2)}) collective-permute-start(f32[72,128]{1,0:T(8,128)} %shard_map.48), channel_id=1, source_target_pairs={{0,16},{1,17},{2,18},{3,19},{4,20},{5,21},{6,22},{7,23},{8,24},{9,... | collective-permute-start | bytes 110600 | tf_op jit(solution)/shard_map/ppermute | solution.py:270
  31.1 2.8 %collective-permute-done.8 = f32[72,128]{1,0:T(8,128)S(1)} collective-permute-done((f32[72,128]{1,0:T(8,128)}, f32[72,128]{1,0:T(8,128)S(1)}, u32[]{:S(2)}, u32[]{:S(2)}) %collective-permute-start.8) | collective-permute-done | bytes 36896 | tf_op jit(solution)/shard_map/ppermute | solution.py:270
  34.7 2.8 %collective-permute-start.14 = (f32[72,128]{1,0:T(8,128)S(1)}, f32[72,128]{1,0:T(8,128)S(1)}, u32[]{:S(2)}, u32[]{:S(2)}) collective-permute-start(f32[72,128]{1,0:T(8,128)S(1)} %add.12.refs_0_), channel_id=1, source_target_pairs={{0,10},{1,11},{2,8},{3,9},{4,14},{5,15},{6,12},{7,13},{8,2},{9,3},... | collective-permute-start | bytes 110600 | tf_op jit(solution)/shard_map/ppermute | solution.py:270
  37.5 1.4 %collective-permute-start.13 = (f32[72,128]{1,0:T(8,128)S(1)}, f32[72,128]{1,0:T(8,128)S(1)}, u32[]{:S(2)}, u32[]{:S(2)}) collective-permute-start(f32[72,128]{1,0:T(8,128)S(1)} %add.12.refs_0_), channel_id=1, source_target_pairs={{0,6},{1,7},{2,4},{3,5},{4,2},{5,3},{6,0},{7,1},{8,14},{9,15},{10,... | collective-permute-start | bytes 110600 | tf_op jit(solution)/shard_map/ppermute | solution.py:270
  38.9 1.5 %collective-permute-start.12 = (f32[72,128]{1,0:T(8,128)S(1)}, f32[72,128]{1,0:T(8,128)S(1)}, u32[]{:S(2)}, u32[]{:S(2)}) collective-permute-start(f32[72,128]{1,0:T(8,128)S(1)} %add.12.refs_0_), channel_id=1, source_target_pairs={{0,2},{1,3},{2,0},{3,1},{4,6},{5,7},{6,4},{7,5},{8,10},{9,11},{10,... | collective-permute-start | bytes 110600 | tf_op jit(solution)/shard_map/ppermute | solution.py:270
  40.6 1.8 %collective-permute-start.10 = (f32[72,128]{1,0:T(8,128)S(1)}, f32[72,128]{1,0:T(8,128)S(1)}, u32[]{:S(2)}, u32[]{:S(2)}) collective-permute-start(f32[72,128]{1,0:T(8,128)S(1)} %add.12.refs_0_), channel_id=1, source_target_pairs={{0,8},{1,9},{2,10},{3,11},{4,12},{5,13},{6,14},{7,15},{8,0},{9,1},... | collective-permute-start | bytes 110600 | tf_op jit(solution)/shard_map/ppermute | solution.py:270
  42.5 1.5 %collective-permute-start.9 = (f32[72,128]{1,0:T(8,128)S(1)}, f32[72,128]{1,0:T(8,128)S(1)}, u32[]{:S(2)}, u32[]{:S(2)}) collective-permute-start(f32[72,128]{1,0:T(8,128)S(1)} %add.12.refs_0_), channel_id=1, source_target_pairs={{0,4},{1,5},{2,6},{3,7},{4,0},{5,1},{6,2},{7,3},{8,12},{9,13},{10,... | collective-permute-start | bytes 110600 | tf_op jit(solution)/shard_map/ppermute | solution.py:270
  44.0 1.3 %collective-permute-done.11.refs_3_ = f32[72,128]{1,0:T(8,128)S(1)} collective-permute-done((f32[72,128]{1,0:T(8,128)S(1)}, f32[72,128]{1,0:T(8,128)S(1)}, u32[]{:S(2)}, u32[]{:S(2)}) %collective-permute-start.11) | collective-permute-done | bytes 36896 | tf_op jit(solution)/shard_map/ppermute | solution.py:270
  45.3 1.1 %collective-permute-done.9.refs_1_ = f32[72,128]{1,0:T(8,128)S(1)} collective-permute-done((f32[72,128]{1,0:T(8,128)S(1)}, f32[72,128]{1,0:T(8,128)S(1)}, u32[]{:S(2)}, u32[]{:S(2)}) %collective-permute-start.9) | collective-permute-done | bytes 36896 | tf_op jit(solution)/shard_map/ppermute | solution.py:270
  47.1 1.6 %shard_map.49.mine_ref = f32[576,128]{1,0:T(8,128)} custom-call(s32[2]{0:T(128)} %pad_add_fusion.where_ref, f32[72,128]{1,0:T(8,128)} %copy-done.5, f32[72,128]{1,0:T(8,128)} %copy-done.19, f32[72,128]{1,0:T(8,128)} %copy-done.18, f32[72,128]{1,0:T(8,128)} %copy-done.17, f32[72,128]{1,0:T(8,128)} %copy-done.16, f32[72,128]{1,0:T(8,128)} %copy-done.15, ...), custom_call_target="tpu_custom_call" | custom-call | tf_op jit(solution)/shard_map/pallas_call | solution.py:312
  50.6 1.1 %copy-done.2 = f32[576,128]{1,0:T(8,128)S(1)} copy-done((f32[576,128]{1,0:T(8,128)S(1)}, f32[576,128]{1,0:T(8,128)}, u32[]{:S(2)}) %copy-start.2) | copy-done | bytes 294936
  51.7 16.4 %shard_map.50 = (f32[256,256]{1,0:T(8,128)S(1)}, f32[256,256]{1,0:T(8,128)S(1)}) custom-call(s32[2]{0:T(128)S(1)} %copy-done.3, f32[8]{0:T(128)S(1)} %dynamic_slice.6.shift_ref, f32[8]{0:T(128)S(1)} %dynamic_slice.7.weight_ref, f32[576,128]{1,0:T(8,128)S(1)} %copy-done.2, f32[576,128]{1,0:T(8,128)S(1)} %collective-permute-done.16.other_ref), custom_call_target="tpu_custom_call" | custom-call | flops 99999997952 | bytes 1000000 | tf_op jit(solution)/shard_map/pallas_call | solution.py:320
  69.8 2.3 %shard_map.52 = f32[1024,256]{1,0:T(8,128)} custom-call(f32[256,256]{1,0:T(8,128)S(1)} %get-tuple-element.27.mine_ref, f32[256,256]{1,0:T(8,128)S(1)} %collective-permute-done.17.other_ref, f32[256,256]{1,0:T(8,128)S(1)} %get-tuple-element.28.cross_ref, f32[1024,256]{1,0:T(8,128)S(1)} %shard_map.51.z_ref), custom_call_target="tpu_custom_call" | custom-call | tf_op jit(solution)/shard_map/pallas_call | solution.py:344
  (67 shorter events, 8.7 us)
Async XLA Ops:
  5.5 1.9 %collective-permute-start = (f32[576,128]{1,0:T(8,128)}, f32[576,128]{1,0:T(8,128)S(1)}, u32[]{:S(2)}, u32[]{:S(2)}) collective-permute-start(f32[576,128]{1,0:T(8,128)} %get-tuple-element.18), channel_id=1, source_target_pairs={{0,1},{1,0},{2,3},{3,2},{4,5},{5,4},{6,7},{7,6},{8,9},{9,8},{10,11... | collective-permute-start | bytes 884744 | tf_op jit(solution)/shard_map/ppermute | solution.py:270
  10.0 7.8 %collective-permute-start.1 = (f32[72,128]{1,0:T(8,128)}, f32[72,128]{1,0:T(8,128)S(1)}, u32[]{:S(2)}, u32[]{:S(2)}) collective-permute-start(f32[72,128]{1,0:T(8,128)} %get-tuple-element.20), channel_id=1, source_target_pairs={{0,4},{1,5},{2,6},{3,7},{4,0},{5,1},{6,2},{7,3},{8,12},{9,13},{10,... | collective-permute-start | bytes 110600 | tf_op jit(solution)/shard_map/ppermute | solution.py:270
  12.9 7.5 %collective-permute-start.2 = (f32[72,128]{1,0:T(8,128)}, f32[72,128]{1,0:T(8,128)S(1)}, u32[]{:S(2)}, u32[]{:S(2)}) collective-permute-start(f32[72,128]{1,0:T(8,128)} %get-tuple-element.21), channel_id=1, source_target_pairs={{0,8},{1,9},{2,10},{3,11},{4,12},{5,13},{6,14},{7,15},{8,0},{9,1},... | collective-permute-start | bytes 110600 | tf_op jit(solution)/shard_map/ppermute | solution.py:270
  14.4 6.0 %collective-permute-start.3 = (f32[72,128]{1,0:T(8,128)}, f32[72,128]{1,0:T(8,128)S(1)}, u32[]{:S(2)}, u32[]{:S(2)}) collective-permute-start(f32[72,128]{1,0:T(8,128)} %get-tuple-element.22), channel_id=1, source_target_pairs={{0,12},{1,13},{2,14},{3,15},{4,8},{5,9},{6,10},{7,11},{8,4},{9,5},... | collective-permute-start | bytes 110600 | tf_op jit(solution)/shard_map/ppermute | solution.py:270
  14.5 6.0 %collective-permute-start.4 = (f32[72,128]{1,0:T(8,128)}, f32[72,128]{1,0:T(8,128)S(1)}, u32[]{:S(2)}, u32[]{:S(2)}) collective-permute-start(f32[72,128]{1,0:T(8,128)} %get-tuple-element.23), channel_id=1, source_target_pairs={{0,2},{1,3},{2,0},{3,1},{4,6},{5,7},{6,4},{7,5},{8,10},{9,11},{10,... | collective-permute-start | bytes 110600 | tf_op jit(solution)/shard_map/ppermute | solution.py:270
  16.4 5.1 %collective-permute-start.5 = (f32[72,128]{1,0:T(8,128)}, f32[72,128]{1,0:T(8,128)S(1)}, u32[]{:S(2)}, u32[]{:S(2)}) collective-permute-start(f32[72,128]{1,0:T(8,128)} %get-tuple-element.24), channel_id=1, source_target_pairs={{0,6},{1,7},{2,4},{3,5},{4,2},{5,3},{6,0},{7,1},{8,14},{9,15},{10,... | collective-permute-start | bytes 110600 | tf_op jit(solution)/shard_map/ppermute | solution.py:270
  17.8 8.5 %copy-start.6 = (f32[72,128]{1,0:T(8,128)}, f32[72,128]{1,0:T(8,128)S(1)}, u32[]{:S(2)}) copy-start(f32[72,128]{1,0:T(8,128)S(1)} %collective-permute-done.1.refs_1_) | copy-start | bytes 110596
  17.8 5.5 %collective-permute-start.6 = (f32[72,128]{1,0:T(8,128)}, f32[72,128]{1,0:T(8,128)S(1)}, u32[]{:S(2)}, u32[]{:S(2)}) collective-permute-start(f32[72,128]{1,0:T(8,128)} %get-tuple-element.25), channel_id=1, source_target_pairs={{0,10},{1,11},{2,8},{3,9},{4,14},{5,15},{6,12},{7,13},{8,2},{9,3},... | collective-permute-start | bytes 110600 | tf_op jit(solution)/shard_map/ppermute | solution.py:270
  20.4 6.0 %copy-start.7 = (f32[72,128]{1,0:T(8,128)}, f32[72,128]{1,0:T(8,128)S(1)}, u32[]{:S(2)}) copy-start(f32[72,128]{1,0:T(8,128)S(1)} %collective-permute-done.2.refs_2_) | copy-start | bytes 110596
  20.4 6.0 %collective-permute-start.7 = (f32[72,128]{1,0:T(8,128)}, f32[72,128]{1,0:T(8,128)S(1)}, u32[]{:S(2)}, u32[]{:S(2)}) collective-permute-start(f32[72,128]{1,0:T(8,128)} %get-tuple-element.26), channel_id=1, source_target_pairs={{0,14},{1,15},{2,12},{3,13},{4,10},{5,11},{6,8},{7,9},{8,6},{9,7},... | collective-permute-start | bytes 110600 | tf_op jit(solution)/shard_map/ppermute | solution.py:270
  20.4 5.9 %copy-start.8 = (f32[72,128]{1,0:T(8,128)}, f32[72,128]{1,0:T(8,128)S(1)}, u32[]{:S(2)}) copy-start(f32[72,128]{1,0:T(8,128)S(1)} %collective-permute-done.3.refs_3_) | copy-start | bytes 110596
  28.5 5.4 %collective-permute-start.8 = (f32[72,128]{1,0:T(8,128)}, f32[72,128]{1,0:T(8,128)S(1)}, u32[]{:S(2)}, u32[]{:S(2)}) collective-permute-start(f32[72,128]{1,0:T(8,128)} %shard_map.48), channel_id=1, source_target_pairs={{0,16},{1,17},{2,18},{3,19},{4,20},{5,21},{6,22},{7,23},{8,24},{9,... | collective-permute-start | bytes 110600 | tf_op jit(solution)/shard_map/ppermute | solution.py:270
  34.6 11.8 %copy-start.5 = (f32[72,128]{1,0:T(8,128)}, f32[72,128]{1,0:T(8,128)S(1)}, u32[]{:S(2)}) copy-start(f32[72,128]{1,0:T(8,128)S(1)} %add.12.refs_0_) | copy-start | bytes 110596
  34.6 6.0 %collective-permute-start.15 = (f32[72,128]{1,0:T(8,128)S(1)}, f32[72,128]{1,0:T(8,128)S(1)}, u32[]{:S(2)}, u32[]{:S(2)}) collective-permute-start(f32[72,128]{1,0:T(8,128)S(1)} %add.12.refs_0_), channel_id=1, source_target_pairs={{0,14},{1,15},{2,12},{3,13},{4,10},{5,11},{6,8},{7,9},{8,6},{9,7},... | collective-permute-start | bytes 110600 | tf_op jit(solution)/shard_map/ppermute | solution.py:270
  34.7 7.7 %collective-permute-start.14 = (f32[72,128]{1,0:T(8,128)S(1)}, f32[72,128]{1,0:T(8,128)S(1)}, u32[]{:S(2)}, u32[]{:S(2)}) collective-permute-start(f32[72,128]{1,0:T(8,128)S(1)} %add.12.refs_0_), channel_id=1, source_target_pairs={{0,10},{1,11},{2,8},{3,9},{4,14},{5,15},{6,12},{7,13},{8,2},{9,3},... | collective-permute-start | bytes 110600 | tf_op jit(solution)/shard_map/ppermute | solution.py:270
  37.5 6.5 %collective-permute-start.13 = (f32[72,128]{1,0:T(8,128)S(1)}, f32[72,128]{1,0:T(8,128)S(1)}, u32[]{:S(2)}, u32[]{:S(2)}) collective-permute-start(f32[72,128]{1,0:T(8,128)S(1)} %add.12.refs_0_), channel_id=1, source_target_pairs={{0,6},{1,7},{2,4},{3,5},{4,2},{5,3},{6,0},{7,1},{8,14},{9,15},{10,... | collective-permute-start | bytes 110600 | tf_op jit(solution)/shard_map/ppermute | solution.py:270
  38.9 5.1 %collective-permute-start.12 = (f32[72,128]{1,0:T(8,128)S(1)}, f32[72,128]{1,0:T(8,128)S(1)}, u32[]{:S(2)}, u32[]{:S(2)}) collective-permute-start(f32[72,128]{1,0:T(8,128)S(1)} %add.12.refs_0_), channel_id=1, source_target_pairs={{0,2},{1,3},{2,0},{3,1},{4,6},{5,7},{6,4},{7,5},{8,10},{9,11},{10,... | collective-permute-start | bytes 110600 | tf_op jit(solution)/shard_map/ppermute | solution.py:270
  40.5 4.9 %collective-permute-start.11 = (f32[72,128]{1,0:T(8,128)S(1)}, f32[72,128]{1,0:T(8,128)S(1)}, u32[]{:S(2)}, u32[]{:S(2)}) collective-permute-start(f32[72,128]{1,0:T(8,128)S(1)} %add.12.refs_0_), channel_id=1, source_target_pairs={{0,12},{1,13},{2,14},{3,15},{4,8},{5,9},{6,10},{7,11},{8,4},{9,5},... | collective-permute-start | bytes 110600 | tf_op jit(solution)/shard_map/ppermute | solution.py:270
  40.6 4.7 %collective-permute-start.10 = (f32[72,128]{1,0:T(8,128)S(1)}, f32[72,128]{1,0:T(8,128)S(1)}, u32[]{:S(2)}, u32[]{:S(2)}) collective-permute-start(f32[72,128]{1,0:T(8,128)S(1)} %add.12.refs_0_), channel_id=1, source_target_pairs={{0,8},{1,9},{2,10},{3,11},{4,12},{5,13},{6,14},{7,15},{8,0},{9,1},... | collective-permute-start | bytes 110600 | tf_op jit(solution)/shard_map/ppermute | solution.py:270
  42.5 4.0 %collective-permute-start.9 = (f32[72,128]{1,0:T(8,128)S(1)}, f32[72,128]{1,0:T(8,128)S(1)}, u32[]{:S(2)}, u32[]{:S(2)}) collective-permute-start(f32[72,128]{1,0:T(8,128)S(1)} %add.12.refs_0_), channel_id=1, source_target_pairs={{0,4},{1,5},{2,6},{3,7},{4,0},{5,1},{6,2},{7,3},{8,12},{9,13},{10,... | collective-permute-start | bytes 110600 | tf_op jit(solution)/shard_map/ppermute | solution.py:270
  48.7 1.8 %collective-permute-start.16 = (f32[576,128]{1,0:T(8,128)}, f32[576,128]{1,0:T(8,128)S(1)}, u32[]{:S(2)}, u32[]{:S(2)}) collective-permute-start(f32[576,128]{1,0:T(8,128)} %shard_map.49.mine_ref), channel_id=1, source_target_pairs={{0,1},{1,0},{2,3},{3,2},{4,5},{5,4},{6,7},{7,6},{8,9},{9,8},{10,11... | collective-permute-start | bytes 884744 | tf_op jit(solution)/shard_map/ppermute | solution.py:270
  50.1 18.5 %copy-start = (f32[1024,256]{1,0:T(8,128)S(1)}, f32[1024,256]{1,0:T(8,128)}, u32[]{:S(2)}) copy-start(f32[1024,256]{1,0:T(8,128)} %b_ref.1) | copy-start | bytes 3145732
  50.1 18.5 %copy-start.1 = (f32[1024,256]{1,0:T(8,128)S(1)}, f32[1024,256]{1,0:T(8,128)}, u32[]{:S(2)}) copy-start(f32[1024,256]{1,0:T(8,128)} %t_ref.1) | copy-start | bytes 3145732
  68.1 1.7 %collective-permute-start.17 = (f32[256,256]{1,0:T(8,128)S(1)}, f32[256,256]{1,0:T(8,128)S(1)}, u32[]{:S(2)}, u32[]{:S(2)}) collective-permute-start(f32[256,256]{1,0:T(8,128)S(1)} %get-tuple-element.27.mine_ref), channel_id=1, source_target_pairs={{0,1},{1,0},{2,3},{3,2},{4,5},{5,4},{6,7},{7,6},{8,9},{9,8},{10,11... | collective-permute-start | bytes 786440 | tf_op jit(solution)/shard_map/ppermute | solution.py:270
  (16 other events, 35.7 us)

commit v2 on v1

--- a/solution.py
+++ b/solution.py
@@ -32,10 +32,7 @@
 weights = np.array(half_weights[::-1] + half_weights) / 2.0
 NODES = 8
 CHUNKS = 4
-CUBE = 8
-PIECE = 72
-HALF = CUBE * PIECE
-PAY_ROWS = 2 * HALF
+GRANT = 63 * 1024 * 1024
 STEP = 32
 F32 = jnp.float32
 BF16 = jnp.bfloat16
@@ -97,33 +94,14 @@
         half = slice(c * 128, (c + 1) * 128)
         pay[c * n : (c + 1) * n, :] = cross[:, half]
         pay[(2 + c) * n : (3 + c) * n, :] = packed[:, half]
-    pay[4 * n :, :] = jnp.zeros((PAY_ROWS - 4 * n, 128), F32)
+    pay[4 * n :, :] = jnp.zeros((pay.shape[0] - 4 * n, 128), F32)
     for c in range(2):
         half = slice(c * 128, (c + 1) * 128)
         pay[4 * n + c : 4 * n + c + 1, :] = tdiag[:, half]
         pay[4 * n + 2 + c : 4 * n + 3 + c, :] = bdiag[:, half]
-    core = where_ref[0]
-    keep_ref[...] = pay[pl.ds(pl.multiple_of(core * HALF, 8), HALF), :]
-    send_ref[...] = pay[pl.ds(pl.multiple_of((1 - core) * HALF, 8), HALF), :]
-
-
-def scatter_kernel(where_ref, keep_ref, got_ref, *out_refs):
-    for mask, out_ref in enumerate(out_refs):
-        rows = pl.ds(pl.multiple_of((where_ref[1] ^ mask) * PIECE, 8), PIECE)
-        out_ref[...] = keep_ref[rows, :] + got_ref[rows, :]
-
-
-def sum_kernel(*refs):
-    total = refs[0][...]
-    for ref in refs[1:-1]:
-        total = total + ref[...]
-    refs[-1][...] = total
-
-
-def gather_kernel(where_ref, *refs):
-    for mask, ref in enumerate(refs[:-1]):
-        rows = pl.ds(pl.multiple_of((where_ref[1] ^ mask) * PIECE, 8), PIECE)
-        refs[-1][rows, :] = ref[...]
+    half, core = keep_ref.shape[0], where_ref[0]
+    keep_ref[...] = pay[pl.ds(pl.multiple_of(core * half, 8), half), :]
+    send_ref[...] = pay[pl.ds(pl.multiple_of((1 - core) * half, 8), half), :]
 
 
 def invert_blocks(v):
@@ -165,9 +143,9 @@
     where_ref, shift_ref, weight_ref, mine_ref, other_ref, out_ref, cross_ref, mats, turned, inverses, news, pay
 ):
     n = out_ref.shape[1]
-    core = where_ref[0]
-    pay[pl.ds(pl.multiple_of(core * HALF, 8), HALF), :] = mine_ref[...]
-    pay[pl.ds(pl.multiple_of((1 - core) * HALF, 8), HALF), :] = other_ref[...]
+    half, core = mine_ref.shape[0], where_ref[0]
+    pay[pl.ds(pl.multiple_of(core * half, 8), half), :] = mine_ref[...]
+    pay[pl.ds(pl.multiple_of((1 - core) * half, 8), half), :] = other_ref[...]
     row, col = iota((n, n), 0), iota((n, n), 1)
 
     def wide(start, rows):
@@ -258,29 +236,28 @@
     out_ref[...] = dot3(halves(z_ref[...]), right)
 
 
-AXES = ("gx", "gy", "gz")
-
-
-def exchange(x, mesh, gx=0, gy=0, gz=0):
-    ny, nz = mesh.shape["gy"], mesh.shape["gz"]
-    perm = []
-    for i in range(mesh.size):
-        x0, y0, z0 = i // (ny * nz), i // nz % ny, i % nz
-        perm.append((i, ((x0 ^ gx) * ny + (y0 ^ gy)) * nz + (z0 ^ gz)))
-    return lax.ppermute(x, AXES, perm)
+def swap_cores(x):
+    return lax.ppermute(x, "gz", [(0, 1), (1, 0)])
+
+
+def summed(x, chips):
+    pieces = lax.all_to_all(x, ("gx", "gy"), 0, 0, tiled=True)
+    piece = jnp.sum(pieces.reshape(chips, -1, x.shape[1]), axis=0)
+    return lax.all_to_all(jnp.tile(piece, (chips, 1)), ("gx", "gy"), 0, 0, tiled=True)
 
 
 def on_device(basis, target, mesh):
     rows, n = basis.shape
     total_rows = rows * mesh.size
+    chips = mesh.shape["gx"] * mesh.shape["gy"]
+    pay_half = -(-(2 * n + 8) // (8 * chips)) * 8 * chips
     vmem = pl.BlockSpec(memory_space=pltpu.VMEM)
     smem = pl.BlockSpec(memory_space=pltpu.SMEM)
     hbm = pl.BlockSpec(memory_space=pltpu.HBM)
     limit = pltpu.CompilerParams(vmem_limit_bytes=48 * 1024 * 1024)
-    core, gx, gy = lax.axis_index("gz"), lax.axis_index("gx"), lax.axis_index("gy")
-    where = jnp.stack([core, (gx & 3) + 4 * (gy & 1)]).astype(jnp.int32)
-    half = jax.ShapeDtypeStruct((HALF, 128), F32)
-    piece = jax.ShapeDtypeStruct((PIECE, 128), F32)
+    core = lax.axis_index("gz")
+    where = jnp.reshape(core, (1,)).astype(jnp.int32)
+    half = jax.ShapeDtypeStruct((pay_half, 128), F32)
     keep, send = pl.pallas_call(
         gram_kernel,
         out_shape=(half, half),
@@ -289,30 +266,13 @@
         scratch_shapes=[
             pltpu.VMEM((rows, n), F32),
             pltpu.VMEM((rows, n), F32),
-            pltpu.VMEM((PAY_ROWS, 128), F32),
+            pltpu.VMEM((2 * pay_half, 128), F32),
             pltpu.SemaphoreType.DMA((2, CHUNKS)),
         ],
+        compiler_params=pltpu.CompilerParams(vmem_limit_bytes=GRANT),
     )(where, basis, target)
-    pieces = pl.pallas_call(
-        scatter_kernel,
-        out_shape=(piece,) * CUBE,
-        in_specs=[smem, vmem, vmem],
-        out_specs=(vmem,) * CUBE,
-    )(where, keep, exchange(send, mesh, gz=1))
-    masks = [(mask & 3, mask >> 2) for mask in range(CUBE)]
-    got = [exchange(pieces[m], mesh, gx=masks[m][0], gy=masks[m][1]) for m in range(1, CUBE)]
-    mine = pl.pallas_call(
-        sum_kernel, out_shape=piece, in_specs=[vmem] * CUBE, out_specs=vmem
-    )(pieces[0], *got)
-    for bit in range(2, (mesh.shape["gx"] - 1).bit_length()):
-        mine = mine + exchange(mine, mesh, gx=1 << bit)
-    for bit in range(1, (mesh.shape["gy"] - 1).bit_length()):
-        mine = mine + exchange(mine, mesh, gy=1 << bit)
-    got = [exchange(mine, mesh, gx=masks[m][0], gy=masks[m][1]) for m in range(1, CUBE)]
-    mine = pl.pallas_call(
-        gather_kernel, out_shape=half, in_specs=[smem] + [vmem] * CUBE, out_specs=vmem
-    )(where, mine, *got)
-    other = exchange(mine, mesh, gz=1)
+    mine = summed(keep + swap_cores(send), chips)
+    other = swap_cores(mine)
     first = core * NODES
     shifts = lax.dynamic_slice_in_dim(jnp.asarray(points**2, F32), first, NODES)
     node_wts = lax.dynamic_slice_in_dim(jnp.asarray(weights, F32), first, NODES)
@@ -327,12 +287,12 @@
             pltpu.VMEM((2, 128, 128), F32),
             pltpu.VMEM((2, 2 * 128, 128), F32),
             pltpu.VMEM((NODES, STEP, n), F32),
-            pltpu.VMEM((PAY_ROWS, 128), F32),
+            pltpu.VMEM((2 * pay_half, 128), F32),
         ],
         compiler_params=limit,
         cost_estimate=pl.CostEstimate(flops=10**11, bytes_accessed=10**6, transcendentals=0),
     )(where, shifts, node_wts, mine, other)
-    other = exchange(part, mesh, gz=1)
+    other = swap_cores(part)
     residual = pl.pallas_call(
         residual_kernel,
         out_shape=jax.ShapeDtypeStruct((rows, n), F32),

time: 72.5 us -> 63.4 us (0.87)
  blocking collectives: 0 us -> 33.8 us
  starting transfers between devices: 23.4 us -> 0.86 us
  waiting for transfers between devices: 13.5 us -> 2.36 us
  Pallas kernels: 29.2 us -> 23.6 us
  local copies, waits for them, and re-layouts: 4.51 us -> 1.41 us
    all_to_all x0 -> x2, blocking collectives: none -> 33.8 us  [the longest x1 19.7 us: summed(): pieces = lax.all_to_all(x, ('gx', 'gy'), 0, 0, tiled=True)]
    ppermute x18 -> x3, starting transfers between devices: 23.4 us -> 0.86 us  [swap_cores(): return lax.ppermute(x, 'gz', [(0, 1), (1, 0)])]
    ppermute x18 -> x3, waiting for transfers between devices: 13.5 us -> 2.36 us  [swap_cores(): return lax.ppermute(x, 'gz', [(0, 1), (1, 0)])]
    pallas_call x3 -> x0, Pallas kernels: 4.98 us -> none  [the longest x1 1.81 us: on_device(): pl.pallas_call(scatter_kernel, out_shape=(piece,) * CUBE, in_specs=[smem,...]
    unnamed x44 -> x8, local copies, waits for them, and re-layouts: 4.36 us -> 1.24 us
  transfers between devices with their start and end apart: 18 -> 3, of which waited for: 9 -> 3; matrix products, arithmetic and copies ran while one was open for 0% -> 0% of each run, Pallas kernels for 1% -> 1%
where the time goes in v2:
time: 63.4 us; the launch traced here: 63.1 us
  blocking collectives  33.8 us (53%)
  Pallas kernels  23.6 us (37%)
  waiting for transfers between devices  2.36 us (4%)
  local copies, waits for them, and re-layouts  1.41 us (2%)
  other arithmetic  1.05 us (2%)
  starting transfers between devices  0.86 us (1%)
    all_to_all x1, blocking collectives, summed(): pieces = lax.all_to_all(x, ('gx', 'gy'), 0, 0, tiled=True)  19.7 us
    pallas_call x1, Pallas kernels, on_device(): pl.pallas_call(resolvent_kernel, out_shape=(square, square), in_specs=[sm...  16.3 us
    all_to_all x1, blocking collectives, summed(): lax.all_to_all(jnp.tile(piece, (chips, 1)), ('gx', 'gy'), 0, 0, tiled=True)  14.1 us
    pallas_call x1, Pallas kernels, on_device(): pl.pallas_call(gram_kernel, out_shape=(half, half), in_specs=[smem, hbm,...  4.35 us
    ppermute x3, waiting for transfers between devices, swap_cores(): return lax.ppermute(x, 'gz', [(0, 1), (1, 0)])  2.36 us
    pallas_call x1, Pallas kernels, on_device(): pl.pallas_call(functools.partial(lift_kernel, float(np.sqrt(total_rows)))...  2.31 us
  transfers between devices with their start and end apart: 3, of which 3 were waited for; matrix products, arithmetic and copies ran while one was open for 0% of the time, Pallas kernels for 1%

profile of v2, /device:TPU:0, one launch (start us, length us, event | category | flops | bytes accessed | tf_op | source)
XLA Modules:
  0.0 63.1 jit_solution(4742013883173754727)
XLA Ops:
  0.0 4.4 %shard_map.46 = (f32[640,128]{1,0:T(8,128)}, f32[640,128]{1,0:T(8,128)}) custom-call(s32[1]{0:T(128)} %bitcast.where_ref, f32[1024,256]{1,0:T(8,128)} %b_ref.1, f32[1024,256]{1,0:T(8,128)} %t_ref.1), custom_call_target="tpu_custom_call" | custom-call | tf_op jit(solution)/shard_map/pallas_call | solution.py:261
  4.4 0.5 collective-permute-start
  4.9 1.5 %collective-permute-done = f32[640,128]{1,0:T(8,128)S(1)} collective-permute-done((f32[640,128]{1,0:T(8,128)}, f32[640,128]{1,0:T(8,128)S(1)}, u32[]{:S(2)}, u32[]{:S(2)}) %collective-permute-start) | collective-permute-done | bytes 327712 | tf_op jit(solution)/shard_map/ppermute | solution.py:240
  6.3 1.0 %add.8 = f32[640,128]{1,0:T(8,128)S(1)} add(f32[640,128]{1,0:T(8,128)} %get-tuple-element.9, f32[640,128]{1,0:T(8,128)S(1)} %collective-permute-done) | non-fusion elementwise | flops 81920 | bytes 983040 | tf_op jit(solution)/shard_map/add | solution.py:274
  7.4 19.7 %all_to_all.17 = f32[16,40,128]{2,1,0:T(8,128)S(1)} all-to-all(f32[16,40,128]{2,1,0:T(8,128)S(1)} %bitcast.5), channel_id=1, replica_groups=mesh['gx'=8,'gy'=2,'gz'=2] {'gx','gy'}, dimensions={0} | all-to-all | bytes 655360 | tf_op jit(solution)/shard_map/all_to_all | solution.py:244
  27.1 14.1 %all_to_all.18 = f32[16,40,128]{2,1,0:T(8,128)S(1)} all-to-all(f32[16,40,128]{2,1,0:T(8,128)S(1)} %tile.2), channel_id=1, replica_groups=mesh['gx'=8,'gy'=2,'gz'=2] {'gx','gy'}, dimensions={0} | all-to-all | bytes 655360 | tf_op jit(solution)/shard_map/all_to_all | solution.py:246
  41.2 0.0 collective-permute-start.1
  41.2 0.0 copy-start.3
  41.2 0.7 %copy-done.3 = f32[16]{0:T(128)S(1)} copy-done((f32[16]{0:T(128)S(1)}, f32[16]{0:T(128)}, u32[]{:S(2)}) %copy-start.3) | copy-done | bytes 88
  41.9 0.0 copy-start.2
  41.9 0.1 dynamic_slice.6.shift_ref
  41.9 0.6 copy-done.2
  42.5 0.1 dynamic_slice.7.weight_ref
  42.6 0.0 copy-start
  42.6 0.0 copy-start.1
  42.6 0.2 collective-permute-done.1.other_ref
  42.8 16.3 %shard_map.47 = (f32[256,256]{1,0:T(8,128)S(1)}, f32[256,256]{1,0:T(8,128)S(1)}) custom-call(s32[1]{0:T(128)} %bitcast.where_ref, f32[8]{0:T(128)S(1)} %dynamic_slice.6.shift_ref, f32[8]{0:T(128)S(1)} %dynamic_slice.7.weight_ref, f32[640,128]{1,0:T(8,128)S(1)} %bitcast.4, f32[640,128]{1,0:T(8,128)S(1)} %collective-permute-done.1.other_ref), custom_call_target="tpu_custom_call" | custom-call | flops 99999997952 | bytes 1000000 | tf_op jit(solution)/shard_map/pallas_call | solution.py:280
  59.2 0.3 collective-permute-start.2
  59.5 0.0 copy-done
  59.5 0.0 copy-done.1
  59.5 0.6 shard_map.48.z_ref
  60.1 0.7 %collective-permute-done.2.other_ref = f32[256,256]{1,0:T(8,128)S(1)} collective-permute-done((f32[256,256]{1,0:T(8,128)S(1)}, f32[256,256]{1,0:T(8,128)S(1)}, u32[]{:S(2)}, u32[]{:S(2)}) %collective-permute-start.2) | collective-permute-done | bytes 262176 | tf_op jit(solution)/shard_map/ppermute | solution.py:240
  60.8 2.3 %shard_map.49 = f32[1024,256]{1,0:T(8,128)} custom-call(f32[256,256]{1,0:T(8,128)S(1)} %get-tuple-element.11.mine_ref, f32[256,256]{1,0:T(8,128)S(1)} %collective-permute-done.2.other_ref, f32[256,256]{1,0:T(8,128)S(1)} %get-tuple-element.12.cross_ref, f32[1024,256]{1,0:T(8,128)S(1)} %shard_map.48.z_ref), custom_call_target="tpu_custom_call" | custom-call | tf_op jit(solution)/shard_map/pallas_call | solution.py:304
  (2 shorter events, 0.0 us)
Async XLA Ops:
  4.4 2.0 %collective-permute-start = (f32[640,128]{1,0:T(8,128)}, f32[640,128]{1,0:T(8,128)S(1)}, u32[]{:S(2)}, u32[]{:S(2)}) collective-permute-start(f32[640,128]{1,0:T(8,128)} %get-tuple-element.10), channel_id=1, source_target_pairs={{0,1},{1,0},{2,3},{3,2},{4,5},{5,4},{6,7},{7,6},{8,9},{9,8},{10,11... | collective-permute-start | bytes 983048 | tf_op jit(solution)/shard_map/ppermute | solution.py:240
  41.2 1.6 %collective-permute-start.1 = (f32[640,128]{1,0:T(8,128)S(1)}, f32[640,128]{1,0:T(8,128)S(1)}, u32[]{:S(2)}, u32[]{:S(2)}) collective-permute-start(f32[640,128]{1,0:T(8,128)S(1)} %bitcast.3), channel_id=1, source_target_pairs={{0,1},{1,0},{2,3},{3,2},{4,5},{5,4},{6,7},{7,6},{8,9},{9,8},{10,11... | collective-permute-start | bytes 983048 | tf_op jit(solution)/shard_map/ppermute | solution.py:240
  41.2 0.7 %copy-start.3 = (f32[16]{0:T(128)S(1)}, f32[16]{0:T(128)}, u32[]{:S(2)}) copy-start(f32[16]{0:T(128)} %constant.16.clone) | copy-start | bytes 196
  41.9 0.7 %copy-start.2 = (f32[16]{0:T(128)S(1)}, f32[16]{0:T(128)}, u32[]{:S(2)}) copy-start(f32[16]{0:T(128)} %constant.17.clone) | copy-start | bytes 196
  42.6 16.9 %copy-start = (f32[1024,256]{1,0:T(8,128)S(1)}, f32[1024,256]{1,0:T(8,128)}, u32[]{:S(2)}) copy-start(f32[1024,256]{1,0:T(8,128)} %b_ref.1) | copy-start | bytes 3145732
  42.6 16.9 %copy-start.1 = (f32[1024,256]{1,0:T(8,128)S(1)}, f32[1024,256]{1,0:T(8,128)}, u32[]{:S(2)}) copy-start(f32[1024,256]{1,0:T(8,128)} %t_ref.1) | copy-start | bytes 3145732
  59.2 1.6 %collective-permute-start.2 = (f32[256,256]{1,0:T(8,128)S(1)}, f32[256,256]{1,0:T(8,128)S(1)}, u32[]{:S(2)}, u32[]{:S(2)}) collective-permute-start(f32[256,256]{1,0:T(8,128)S(1)} %get-tuple-element.11.mine_ref), channel_id=1, source_target_pairs={{0,1},{1,0},{2,3},{3,2},{4,5},{5,4},{6,7},{7,6},{8,9},{9,8},{10,11... | collective-permute-start | bytes 786440 | tf_op jit(solution)/shard_map/ppermute | solution.py:240

commit v3 on v2

--- a/solution.py
+++ b/solution.py
@@ -162,7 +162,7 @@
     square = dot(crosst, cross)
     normal = tgram - 2.0 * square + dot(crosst, dot(bgram, cross))
     for m in range(NODES):
-        shifted = square + shift_ref[m] * normal
+        shifted = square + shift_ref[core * NODES + m] * normal
         mats[0, m * n : (m + 1) * n, :] = shifted[:, 0:128]
         mats[1, m * n : (m + 1) * n, :] = shifted[:, 128:256]
 
@@ -220,9 +220,9 @@
     for tile in range(2):
         lax.fori_loop(0, 4, functools.partial(step, tile), 0)
     for c in range(2):
-        half = weight_ref[0] * mats[c, 0:n, :]
+        half = weight_ref[core * NODES] * mats[c, 0:n, :]
         for m in range(1, NODES):
-            half = half + weight_ref[m] * mats[c, m * n : (m + 1) * n, :]
+            half = half + weight_ref[core * NODES + m] * mats[c, m * n : (m + 1) * n, :]
         out_ref[:, c * 128 : (c + 1) * 128] = half
 
 
@@ -230,27 +230,60 @@
     out_ref[...] = t_ref[...] - dot3(halves(b_ref[...]), halves(cross_ref[...]))
 
 
-def lift_kernel(scale, mine_ref, other_ref, cross_ref, z_ref, out_ref):
+def lift_kernel(scale, mine_ref, other_ref, cross_ref, z_ref, out_hbm, out_ref, sems):
+    rows = z_ref.shape[0] // CHUNKS
     total = (mine_ref[...] + other_ref[...]) * -scale
     right = halves(dot(total, cross_ref[...].T))
-    out_ref[...] = dot3(halves(z_ref[...]), right)
+    copies = []
+    for c in range(CHUNKS):
+        part = pl.ds(c * rows, rows)
+        out_ref[part, :] = dot3(halves(z_ref[part, :]), right)
+        copies.append(pltpu.make_async_copy(out_ref.at[part], out_hbm.at[part], sems.at[c]))
+        copies[-1].start()
+    for copy in copies:
+        copy.wait()
 
 
 def swap_cores(x):
     return lax.ppermute(x, "gz", [(0, 1), (1, 0)])
 
 
-def summed(x, chips):
-    pieces = lax.all_to_all(x, ("gx", "gy"), 0, 0, tiled=True)
-    piece = jnp.sum(pieces.reshape(chips, -1, x.shape[1]), axis=0)
-    return lax.all_to_all(jnp.tile(piece, (chips, 1)), ("gx", "gy"), 0, 0, tiled=True)
+def swap_bits(x, mesh, flips):
+    ny, nz = mesh.shape["gy"], mesh.shape["gz"]
+    perm = []
+    for i in range(mesh.size):
+        gx, gy, gz = i // (ny * nz), i // nz % ny, i % nz
+        perm.append((i, ((gx ^ flips[gz][0]) * ny + (gy ^ flips[gz][1])) * nz + gz))
+    return lax.ppermute(x, ("gx", "gy", "gz"), perm)
+
+
+def joined(side, mine, other):
+    return jnp.where(side == 0, jnp.concatenate([mine, other], 0), jnp.concatenate([other, mine], 0))
+
+
+def summed(x, mesh):
+    core = lax.axis_index("gz")
+    bit_x, bit_y = lax.axis_index("gx") & 1, lax.axis_index("gy") & 1
+    sides = [jnp.where(core == 0, bit_x, bit_y), jnp.where(core == 0, bit_y, bit_x)]
+    flips = [((1, 0), (0, 1)), ((0, 1), (1, 0))]
+    for side, flip in zip(sides, flips):
+        half = x.shape[0] // 2
+        keep = lax.dynamic_slice_in_dim(x, side * half, half, 0)
+        send = lax.dynamic_slice_in_dim(x, (1 - side) * half, half, 0)
+        x = keep + swap_bits(send, mesh, flip)
+    gx = [(1 << bit, 0) for bit in range(1, (mesh.shape["gx"] - 1).bit_length())]
+    gy = [(0, 1 << bit) for bit in range(1, (mesh.shape["gy"] - 1).bit_length())]
+    for flip in zip(gx + gy, (gx + gy)[::-1]):
+        x = x + swap_bits(x, mesh, flip)
+    for side, flip in zip(sides[::-1], flips[::-1]):
+        x = joined(side, x, swap_bits(x, mesh, flip))
+    return x
 
 
 def on_device(basis, target, mesh):
     rows, n = basis.shape
     total_rows = rows * mesh.size
-    chips = mesh.shape["gx"] * mesh.shape["gy"]
-    pay_half = -(-(2 * n + 8) // (8 * chips)) * 8 * chips
+    pay_half = -(-(2 * n + 8) // 32) * 32
     vmem = pl.BlockSpec(memory_space=pltpu.VMEM)
     smem = pl.BlockSpec(memory_space=pltpu.SMEM)
     hbm = pl.BlockSpec(memory_space=pltpu.HBM)
@@ -271,11 +304,8 @@
         ],
         compiler_params=pltpu.CompilerParams(vmem_limit_bytes=GRANT),
     )(where, basis, target)
-    mine = summed(keep + swap_cores(send), chips)
+    mine = summed(keep + swap_cores(send), mesh)
     other = swap_cores(mine)
-    first = core * NODES
-    shifts = lax.dynamic_slice_in_dim(jnp.asarray(points**2, F32), first, NODES)
-    node_wts = lax.dynamic_slice_in_dim(jnp.asarray(weights, F32), first, NODES)
     square = jax.ShapeDtypeStruct((n, n), F32)
     part, cross = pl.pallas_call(
         resolvent_kernel,
@@ -291,7 +321,7 @@
         ],
         compiler_params=limit,
         cost_estimate=pl.CostEstimate(flops=10**11, bytes_accessed=10**6, transcendentals=0),
-    )(where, shifts, node_wts, mine, other)
+    )(where, jnp.asarray(points**2, F32), jnp.asarray(weights, F32), mine, other)
     other = swap_cores(part)
     residual = pl.pallas_call(
         residual_kernel,
@@ -305,7 +335,8 @@
         functools.partial(lift_kernel, float(np.sqrt(total_rows))),
         out_shape=jax.ShapeDtypeStruct((rows, n), F32),
         in_specs=[vmem] * 4,
-        out_specs=vmem,
+        out_specs=hbm,
+        scratch_shapes=[pltpu.VMEM((rows, n), F32), pltpu.SemaphoreType.DMA((CHUNKS,))],
         compiler_params=limit,
     )(part, other, cross, residual)
 

time: 63.4 us -> 59.2 us (0.934)
  blocking collectives: 33.8 us -> 0 us
  waiting for transfers between devices: 2.36 us -> 19.7 us
  starting transfers between devices: 0.86 us -> 14.7 us
  local copies, waits for them, and re-layouts: 1.41 us -> 0.05 us
    all_to_all x2 -> x0, blocking collectives: 33.8 us -> none  [the longest x1 19.7 us: summed(): pieces = lax.all_to_all(x, ('gx', 'gy'), 0, 0, tiled=True)]
    ppermute x0 -> x6, waiting for transfers between devices: none -> 16 us  [swap_bits(): return lax.ppermute(x, ('gx', 'gy', 'gz'), perm)]
    ppermute x0 -> x6, starting transfers between devices: none -> 13.9 us  [swap_bits(): return lax.ppermute(x, ('gx', 'gy', 'gz'), perm)]
    ppermute x3, waiting for transfers between devices: 2.36 us -> 3.74 us  [swap_cores(): return lax.ppermute(x, 'gz', [(0, 1), (1, 0)])]
    unnamed x8, local copies, waits for them, and re-layouts: 1.24 us -> 0.02 us
  transfers between devices with their start and end apart: 3 -> 9, of which waited for: 3 -> 9; matrix products, arithmetic and copies ran while one was open for 0% -> 0% of each run, Pallas kernels for 1% -> 1%
where the time goes in v3:
time: 59.2 us; the launch traced here: 59 us
  Pallas kernels  23.4 us (40%)
  waiting for transfers between devices  19.7 us (33%)
  starting transfers between devices  14.7 us (25%)
  other arithmetic  1.07 us (2%)
    pallas_call x1, Pallas kernels, on_device(): pl.pallas_call(resolvent_kernel, out_shape=(square, square), in_specs=[sm...  16.3 us
    ppermute x6, waiting for transfers between devices, swap_bits(): return lax.ppermute(x, ('gx', 'gy', 'gz'), perm)  16 us
    ppermute x6, starting transfers between devices, swap_bits(): return lax.ppermute(x, ('gx', 'gy', 'gz'), perm)  13.9 us
    pallas_call x1, Pallas kernels, on_device(): pl.pallas_call(gram_kernel, out_shape=(half, half), in_specs=[smem, hbm,...  4.3 us
    ppermute x3, waiting for transfers between devices, swap_cores(): return lax.ppermute(x, 'gz', [(0, 1), (1, 0)])  3.74 us
    pallas_call x1, Pallas kernels, on_device(): pl.pallas_call(functools.partial(lift_kernel, float(np.sqrt(total_rows)))...  2.17 us
  transfers between devices with their start and end apart: 9, of which 9 were waited for; matrix products, arithmetic and copies ran while one was open for 0% of the time, Pallas kernels for 1%

profile of v3, /device:TPU:0, one launch (start us, length us, event | category | flops | bytes accessed | tf_op | source)
XLA Modules:
  0.0 59.0 jit_solution(7157122486153025978)
XLA Ops:
  0.0 4.3 %shard_map.46 = (f32[544,128]{1,0:T(8,128)}, f32[544,128]{1,0:T(8,128)}) custom-call(s32[1]{0:T(128)} %bitcast.where_ref, f32[1024,256]{1,0:T(8,128)} %b_ref.1, f32[1024,256]{1,0:T(8,128)} %t_ref.1), custom_call_target="tpu_custom_call" | custom-call | tf_op jit(solution)/shard_map/pallas_call | solution.py:294
  4.3 0.5 collective-permute-start
  4.8 1.4 %collective-permute-done = f32[544,128]{1,0:T(8,128)S(1)} collective-permute-done((f32[544,128]{1,0:T(8,128)}, f32[544,128]{1,0:T(8,128)S(1)}, u32[]{:S(2)}, u32[]{:S(2)}) %collective-permute-start) | collective-permute-done | bytes 278560 | tf_op jit(solution)/shard_map/ppermute | solution.py:248
  6.2 1.0 %add.27 = f32[544,128]{1,0:T(8,128)S(1)} add(f32[544,128]{1,0:T(8,128)} %get-tuple-element.9, f32[544,128]{1,0:T(8,128)S(1)} %collective-permute-done) | non-fusion elementwise | flops 69632 | bytes 835584 | tf_op jit(solution)/shard_map/add | solution.py:307
  7.2 2.9 %collective-permute-start.1 = (f32[272,128]{1,0:T(8,128)S(1)}, f32[272,128]{1,0:T(8,128)S(1)}, u32[]{:S(2)}, u32[]{:S(2)}) collective-permute-start(f32[272,128]{1,0:T(8,128)S(1)} %constant_dynamic-slice_fusion.1), channel_id=1, source_target_pairs={{0,4},{1,3},{2,6},{3,1},{4,0},{5,7},{6,2},{7,5},{8,12},{9,11},{10,... | collective-permute-start | bytes 417800 | tf_op jit(solution)/shard_map/ppermute | solution.py:257
  10.2 3.0 %collective-permute-done.1 = f32[272,128]{1,0:T(8,128)S(1)} collective-permute-done((f32[272,128]{1,0:T(8,128)S(1)}, f32[272,128]{1,0:T(8,128)S(1)}, u32[]{:S(2)}, u32[]{:S(2)}) %collective-permute-start.1) | collective-permute-done | bytes 139296 | tf_op jit(solution)/shard_map/ppermute | solution.py:257
  13.2 2.1 %collective-permute-start.2 = (f32[136,128]{1,0:T(8,128)S(1)}, f32[136,128]{1,0:T(8,128)S(1)}, u32[]{:S(2)}, u32[]{:S(2)}) collective-permute-start(f32[136,128]{1,0:T(8,128)S(1)} %constant_dynamic-slice_fusion), channel_id=1, source_target_pairs={{0,2},{1,5},{2,0},{3,7},{4,6},{5,1},{6,4},{7,3},{8,10},{9,13},{10,... | collective-permute-start | bytes 208904 | tf_op jit(solution)/shard_map/ppermute | solution.py:257
  15.4 2.3 %collective-permute-done.2 = f32[136,128]{1,0:T(8,128)S(1)} collective-permute-done((f32[136,128]{1,0:T(8,128)S(1)}, f32[136,128]{1,0:T(8,128)S(1)}, u32[]{:S(2)}, u32[]{:S(2)}) %collective-permute-start.2) | collective-permute-done | bytes 69664 | tf_op jit(solution)/shard_map/ppermute | solution.py:257
  17.7 2.1 %collective-permute-start.3 = (f32[136,128]{1,0:T(8,128)S(1)}, f32[136,128]{1,0:T(8,128)S(1)}, u32[]{:S(2)}, u32[]{:S(2)}) collective-permute-start(f32[136,128]{1,0:T(8,128)S(1)} %dynamic-slice_add_fusion.1), channel_id=1, source_target_pairs={{0,8},{1,17},{2,10},{3,19},{4,12},{5,21},{6,14},{7,23},{8,0},{9,25... | collective-permute-start | bytes 208904 | tf_op jit(solution)/shard_map/ppermute | solution.py:257
  19.8 2.3 %collective-permute-done.3 = f32[136,128]{1,0:T(8,128)S(1)} collective-permute-done((f32[136,128]{1,0:T(8,128)S(1)}, f32[136,128]{1,0:T(8,128)S(1)}, u32[]{:S(2)}, u32[]{:S(2)}) %collective-permute-start.3) | collective-permute-done | bytes 69664 | tf_op jit(solution)/shard_map/ppermute | solution.py:257
  22.1 3.1 %collective-permute-start.4 = (f32[136,128]{1,0:T(8,128)S(1)}, f32[136,128]{1,0:T(8,128)S(1)}, u32[]{:S(2)}, u32[]{:S(2)}) collective-permute-start(f32[136,128]{1,0:T(8,128)S(1)} %add.34), channel_id=1, source_target_pairs={{0,16},{1,9},{2,18},{3,11},{4,20},{5,13},{6,22},{7,15},{8,24},{9,1... | collective-permute-start | bytes 208904 | tf_op jit(solution)/shard_map/ppermute | solution.py:257
  25.2 2.3 %collective-permute-done.4 = f32[136,128]{1,0:T(8,128)S(1)} collective-permute-done((f32[136,128]{1,0:T(8,128)S(1)}, f32[136,128]{1,0:T(8,128)S(1)}, u32[]{:S(2)}, u32[]{:S(2)}) %collective-permute-start.4) | collective-permute-done | bytes 69664 | tf_op jit(solution)/shard_map/ppermute | solution.py:257
  27.5 1.9 %collective-permute-start.5 = (f32[136,128]{1,0:T(8,128)S(1)}, f32[136,128]{1,0:T(8,128)S(1)}, u32[]{:S(2)}, u32[]{:S(2)}) collective-permute-start(f32[136,128]{1,0:T(8,128)S(1)} %add.35), channel_id=1, source_target_pairs={{0,2},{1,5},{2,0},{3,7},{4,6},{5,1},{6,4},{7,3},{8,10},{9,13},{10,... | collective-permute-start | bytes 208904 | tf_op jit(solution)/shard_map/ppermute | solution.py:257
  29.4 2.7 %collective-permute-done.5 = f32[136,128]{1,0:T(8,128)S(1)} collective-permute-done((f32[136,128]{1,0:T(8,128)S(1)}, f32[136,128]{1,0:T(8,128)S(1)}, u32[]{:S(2)}, u32[]{:S(2)}) %collective-permute-start.5) | collective-permute-done | bytes 69664 | tf_op jit(solution)/shard_map/ppermute | solution.py:257
  32.1 1.7 %collective-permute-start.6 = (f32[272,128]{1,0:T(8,128)S(1)}, f32[272,128]{1,0:T(8,128)S(1)}, u32[]{:S(2)}, u32[]{:S(2)}) collective-permute-start(f32[272,128]{1,0:T(8,128)S(1)} %maximum_select_fusion.1), channel_id=1, source_target_pairs={{0,4},{1,3},{2,6},{3,1},{4,0},{5,7},{6,2},{7,5},{8,12},{9,11},{10,... | collective-permute-start | bytes 417800 | tf_op jit(solution)/shard_map/ppermute | solution.py:257
  33.8 3.4 %collective-permute-done.6 = f32[272,128]{1,0:T(8,128)S(1)} collective-permute-done((f32[272,128]{1,0:T(8,128)S(1)}, f32[272,128]{1,0:T(8,128)S(1)}, u32[]{:S(2)}, u32[]{:S(2)}) %collective-permute-start.6) | collective-permute-done | bytes 139296 | tf_op jit(solution)/shard_map/ppermute | solution.py:257
  37.2 0.0 copy-start
  37.3 0.1 collective-permute-start.7
  37.3 1.5 %collective-permute-done.7.other_ref = f32[544,128]{1,0:T(8,128)S(1)} collective-permute-done((f32[544,128]{1,0:T(8,128)S(1)}, f32[544,128]{1,0:T(8,128)S(1)}, u32[]{:S(2)}, u32[]{:S(2)}) %collective-permute-start.7) | collective-permute-done | bytes 278560 | tf_op jit(solution)/shard_map/ppermute | solution.py:248
  38.9 16.3 %shard_map.47 = (f32[256,256]{1,0:T(8,128)S(1)}, f32[256,256]{1,0:T(8,128)S(1)}) custom-call(s32[1]{0:T(128)} %bitcast.where_ref, f32[16]{0:T(128)S(1)} %copy-done.3, f32[16]{0:T(128)S(1)} %copy-done.2, f32[544,128]{1,0:T(8,128)S(1)} %maximum_select_fusion.mine_ref, f32[544,128]{1,0:T(8,128)S(1)} %collective-permute-done.7.other_ref), custom_call_target="tpu_custom_call" | custom-call | flops 99999997952 | bytes 1000000 | tf_op jit(solution)/shard_map/pallas_call | solution.py:310
  55.2 0.2 collective-permute-start.8
  55.5 0.6 shard_map.48.z_ref
  56.0 0.8 %collective-permute-done.8.other_ref = f32[256,256]{1,0:T(8,128)S(1)} collective-permute-done((f32[256,256]{1,0:T(8,128)S(1)}, f32[256,256]{1,0:T(8,128)S(1)}, u32[]{:S(2)}, u32[]{:S(2)}) %collective-permute-start.8) | collective-permute-done | bytes 262176 | tf_op jit(solution)/shard_map/ppermute | solution.py:248
  56.8 2.2 %shard_map.49 = f32[1024,256]{1,0:T(8,128)} custom-call(f32[256,256]{1,0:T(8,128)S(1)} %get-tuple-element.11.mine_ref, f32[256,256]{1,0:T(8,128)S(1)} %collective-permute-done.8.other_ref, f32[256,256]{1,0:T(8,128)S(1)} %get-tuple-element.12.cross_ref, f32[1024,256]{1,0:T(8,128)S(1)} %shard_map.48.z_ref), custom_call_target="tpu_custom_call" | custom-call | tf_op jit(solution)/shard_map/pallas_call | solution.py:334
  (15 shorter events, 0.1 us)
Async XLA Ops:
  4.3 1.9 %collective-permute-start = (f32[544,128]{1,0:T(8,128)}, f32[544,128]{1,0:T(8,128)S(1)}, u32[]{:S(2)}, u32[]{:S(2)}) collective-permute-start(f32[544,128]{1,0:T(8,128)} %get-tuple-element.10), channel_id=1, source_target_pairs={{0,1},{1,0},{2,3},{3,2},{4,5},{5,4},{6,7},{7,6},{8,9},{9,8},{10,11... | collective-permute-start | bytes 835592 | tf_op jit(solution)/shard_map/ppermute | solution.py:248
  7.2 6.0 %collective-permute-start.1 = (f32[272,128]{1,0:T(8,128)S(1)}, f32[272,128]{1,0:T(8,128)S(1)}, u32[]{:S(2)}, u32[]{:S(2)}) collective-permute-start(f32[272,128]{1,0:T(8,128)S(1)} %constant_dynamic-slice_fusion.1), channel_id=1, source_target_pairs={{0,4},{1,3},{2,6},{3,1},{4,0},{5,7},{6,2},{7,5},{8,12},{9,11},{10,... | collective-permute-start | bytes 417800 | tf_op jit(solution)/shard_map/ppermute | solution.py:257
  13.2 4.4 %collective-permute-start.2 = (f32[136,128]{1,0:T(8,128)S(1)}, f32[136,128]{1,0:T(8,128)S(1)}, u32[]{:S(2)}, u32[]{:S(2)}) collective-permute-start(f32[136,128]{1,0:T(8,128)S(1)} %constant_dynamic-slice_fusion), channel_id=1, source_target_pairs={{0,2},{1,5},{2,0},{3,7},{4,6},{5,1},{6,4},{7,3},{8,10},{9,13},{10,... | collective-permute-start | bytes 208904 | tf_op jit(solution)/shard_map/ppermute | solution.py:257
  17.7 4.4 %collective-permute-start.3 = (f32[136,128]{1,0:T(8,128)S(1)}, f32[136,128]{1,0:T(8,128)S(1)}, u32[]{:S(2)}, u32[]{:S(2)}) collective-permute-start(f32[136,128]{1,0:T(8,128)S(1)} %dynamic-slice_add_fusion.1), channel_id=1, source_target_pairs={{0,8},{1,17},{2,10},{3,19},{4,12},{5,21},{6,14},{7,23},{8,0},{9,25... | collective-permute-start | bytes 208904 | tf_op jit(solution)/shard_map/ppermute | solution.py:257
  22.1 5.4 %collective-permute-start.4 = (f32[136,128]{1,0:T(8,128)S(1)}, f32[136,128]{1,0:T(8,128)S(1)}, u32[]{:S(2)}, u32[]{:S(2)}) collective-permute-start(f32[136,128]{1,0:T(8,128)S(1)} %add.34), channel_id=1, source_target_pairs={{0,16},{1,9},{2,18},{3,11},{4,20},{5,13},{6,22},{7,15},{8,24},{9,1... | collective-permute-start | bytes 208904 | tf_op jit(solution)/shard_map/ppermute | solution.py:257
  27.5 4.6 %collective-permute-start.5 = (f32[136,128]{1,0:T(8,128)S(1)}, f32[136,128]{1,0:T(8,128)S(1)}, u32[]{:S(2)}, u32[]{:S(2)}) collective-permute-start(f32[136,128]{1,0:T(8,128)S(1)} %add.35), channel_id=1, source_target_pairs={{0,2},{1,5},{2,0},{3,7},{4,6},{5,1},{6,4},{7,3},{8,10},{9,13},{10,... | collective-permute-start | bytes 208904 | tf_op jit(solution)/shard_map/ppermute | solution.py:257
  32.1 5.1 %collective-permute-start.6 = (f32[272,128]{1,0:T(8,128)S(1)}, f32[272,128]{1,0:T(8,128)S(1)}, u32[]{:S(2)}, u32[]{:S(2)}) collective-permute-start(f32[272,128]{1,0:T(8,128)S(1)} %maximum_select_fusion.1), channel_id=1, source_target_pairs={{0,4},{1,3},{2,6},{3,1},{4,0},{5,7},{6,2},{7,5},{8,12},{9,11},{10,... | collective-permute-start | bytes 417800 | tf_op jit(solution)/shard_map/ppermute | solution.py:257
  33.8 5.1 %copy-start.2 = (f32[16]{0:T(128)S(1)}, f32[16]{0:T(128)}, u32[]{:S(2)}) copy-start(f32[16]{0:T(128)} %constant.27.clone.weight_ref) | copy-start | bytes 196
  33.8 5.1 %copy-start.3 = (f32[16]{0:T(128)S(1)}, f32[16]{0:T(128)}, u32[]{:S(2)}) copy-start(f32[16]{0:T(128)} %constant.26.clone.shift_ref) | copy-start | bytes 196
  37.2 18.2 %copy-start = (f32[1024,256]{1,0:T(8,128)S(1)}, f32[1024,256]{1,0:T(8,128)}, u32[]{:S(2)}) copy-start(f32[1024,256]{1,0:T(8,128)} %b_ref.1) | copy-start | bytes 3145732
  37.2 18.2 %copy-start.1 = (f32[1024,256]{1,0:T(8,128)S(1)}, f32[1024,256]{1,0:T(8,128)}, u32[]{:S(2)}) copy-start(f32[1024,256]{1,0:T(8,128)} %t_ref.1) | copy-start | bytes 3145732
  37.3 1.6 %collective-permute-start.7 = (f32[544,128]{1,0:T(8,128)S(1)}, f32[544,128]{1,0:T(8,128)S(1)}, u32[]{:S(2)}, u32[]{:S(2)}) collective-permute-start(f32[544,128]{1,0:T(8,128)S(1)} %maximum_select_fusion.mine_ref), channel_id=1, source_target_pairs={{0,1},{1,0},{2,3},{3,2},{4,5},{5,4},{6,7},{7,6},{8,9},{9,8},{10,11... | collective-permute-start | bytes 835592 | tf_op jit(solution)/shard_map/ppermute | solution.py:248
  55.2 1.6 %collective-permute-start.8 = (f32[256,256]{1,0:T(8,128)S(1)}, f32[256,256]{1,0:T(8,128)S(1)}, u32[]{:S(2)}, u32[]{:S(2)}) collective-permute-start(f32[256,256]{1,0:T(8,128)S(1)} %get-tuple-element.11.mine_ref), channel_id=1, source_target_pairs={{0,1},{1,0},{2,3},{3,2},{4,5},{5,4},{6,7},{7,6},{8,9},{9,8},{10,11... | collective-permute-start | bytes 786440 | tf_op jit(solution)/shard_map/ppermute | solution.py:248

commit v4 on v3

--- a/solution.py
+++ b/solution.py
@@ -32,6 +32,7 @@
 weights = np.array(half_weights[::-1] + half_weights) / 2.0
 NODES = 8
 CHUNKS = 4
+CUBE = 8
 GRANT = 63 * 1024 * 1024
 STEP = 32
 F32 = jnp.float32
@@ -248,42 +249,39 @@
     return lax.ppermute(x, "gz", [(0, 1), (1, 0)])
 
 
-def swap_bits(x, mesh, flips):
+def swap_bits(x, mesh, gx, gy):
     ny, nz = mesh.shape["gy"], mesh.shape["gz"]
     perm = []
     for i in range(mesh.size):
-        gx, gy, gz = i // (ny * nz), i // nz % ny, i % nz
-        perm.append((i, ((gx ^ flips[gz][0]) * ny + (gy ^ flips[gz][1])) * nz + gz))
+        x0, y0, z0 = i // (ny * nz), i // nz % ny, i % nz
+        perm.append((i, ((x0 ^ gx) * ny + (y0 ^ gy)) * nz + z0))
     return lax.ppermute(x, ("gx", "gy", "gz"), perm)
 
 
-def joined(side, mine, other):
-    return jnp.where(side == 0, jnp.concatenate([mine, other], 0), jnp.concatenate([other, mine], 0))
-
-
 def summed(x, mesh):
-    core = lax.axis_index("gz")
-    bit_x, bit_y = lax.axis_index("gx") & 1, lax.axis_index("gy") & 1
-    sides = [jnp.where(core == 0, bit_x, bit_y), jnp.where(core == 0, bit_y, bit_x)]
-    flips = [((1, 0), (0, 1)), ((0, 1), (1, 0))]
-    for side, flip in zip(sides, flips):
-        half = x.shape[0] // 2
-        keep = lax.dynamic_slice_in_dim(x, side * half, half, 0)
-        send = lax.dynamic_slice_in_dim(x, (1 - side) * half, half, 0)
-        x = keep + swap_bits(send, mesh, flip)
-    gx = [(1 << bit, 0) for bit in range(1, (mesh.shape["gx"] - 1).bit_length())]
-    gy = [(0, 1 << bit) for bit in range(1, (mesh.shape["gy"] - 1).bit_length())]
-    for flip in zip(gx + gy, (gx + gy)[::-1]):
-        x = x + swap_bits(x, mesh, flip)
-    for side, flip in zip(sides[::-1], flips[::-1]):
-        x = joined(side, x, swap_bits(x, mesh, flip))
-    return x
+    nx, ny = mesh.shape["gx"], mesh.shape["gy"]
+    low = [(a, b) for a in range(4) for b in range(2)]
+    groups = [
+        [(gx + a) * ny + gy + b for a, b in low] for gx in range(0, nx, 4) for gy in range(0, ny, 2)
+    ]
+
+    def cube(pieces):
+        return lax.all_to_all(
+            pieces, ("gx", "gy"), 0, 0, axis_index_groups=groups, tiled=True
+        )
+
+    x = jnp.sum(cube(x).reshape(CUBE, -1, x.shape[1]), axis=0)
+    for bit in range(2, (nx - 1).bit_length()):
+        x = x + swap_bits(x, mesh, 1 << bit, 0)
+    for bit in range(1, (ny - 1).bit_length()):
+        x = x + swap_bits(x, mesh, 0, 1 << bit)
+    return cube(jnp.tile(x, (CUBE, 1)))
 
 
 def on_device(basis, target, mesh):
     rows, n = basis.shape
     total_rows = rows * mesh.size
-    pay_half = -(-(2 * n + 8) // 32) * 32
+    pay_half = -(-(2 * n + 8) // (8 * CUBE)) * 8 * CUBE
     vmem = pl.BlockSpec(memory_space=pltpu.VMEM)
     smem = pl.BlockSpec(memory_space=pltpu.SMEM)
     hbm = pl.BlockSpec(memory_space=pltpu.HBM)

time: 59.2 us -> 57.6 us (0.973)
  blocking collectives: 0 us -> 23 us
  waiting for transfers between devices: 19.7 us -> 6.45 us
  starting transfers between devices: 14.7 us -> 3.44 us
    all_to_all x0 -> x2, blocking collectives: none -> 23 us  [cube(): lax.all_to_all(pieces, ('gx', 'gy'), 0, 0, axis_index_groups=groups, tile...]
    ppermute x6 -> x1, waiting for transfers between devices: 16 us -> 2.66 us  [swap_bits(): return lax.ppermute(x, ('gx', 'gy', 'gz'), perm)]
    ppermute x6 -> x1, starting transfers between devices: 13.9 us -> 2.65 us  [swap_bits(): return lax.ppermute(x, ('gx', 'gy', 'gz'), perm)]
  transfers between devices with their start and end apart: 9 -> 4, of which waited for: 9 -> 4; matrix products, arithmetic and copies ran while one was open for 0% -> 0% of each run, Pallas kernels for 1% -> 1%
where the time goes in v4:
time: 57.6 us; the launch traced here: 57.4 us
  Pallas kernels  23.4 us (41%)
  blocking collectives  23 us (40%)
  waiting for transfers between devices  6.45 us (11%)
  starting transfers between devices  3.44 us (6%)
  other arithmetic  1.03 us (2%)
    all_to_all x2, blocking collectives, cube(): lax.all_to_all(pieces, ('gx', 'gy'), 0, 0, axis_index_groups=groups, tile...  23 us
    pallas_call x1, Pallas kernels, on_device(): pl.pallas_call(resolvent_kernel, out_shape=(square, square), in_specs=[sm...  16.4 us
    pallas_call x1, Pallas kernels, on_device(): pl.pallas_call(gram_kernel, out_shape=(half, half), in_specs=[smem, hbm,...  4.31 us
    ppermute x3, waiting for transfers between devices, swap_cores(): return lax.ppermute(x, 'gz', [(0, 1), (1, 0)])  3.79 us
    ppermute x1, waiting for transfers between devices, swap_bits(): return lax.ppermute(x, ('gx', 'gy', 'gz'), perm)  2.66 us
    ppermute x1, starting transfers between devices, swap_bits(): return lax.ppermute(x, ('gx', 'gy', 'gz'), perm)  2.65 us
    pallas_call x1, Pallas kernels, on_device(): pl.pallas_call(functools.partial(lift_kernel, float(np.sqrt(total_rows)))...  2.17 us
  transfers between devices with their start and end apart: 4, of which 4 were waited for; matrix products, arithmetic and copies ran while one was open for 0% of the time, Pallas kernels for 1%

profile of v4, /device:TPU:0, one launch (start us, length us, event | category | flops | bytes accessed | tf_op | source)
XLA Modules:
  0.0 57.4 jit_solution(1304455739480142925)
XLA Ops:
  0.0 4.3 %shard_map.46 = (f32[576,128]{1,0:T(8,128)}, f32[576,128]{1,0:T(8,128)}) custom-call(s32[1]{0:T(128)} %bitcast.where_ref, f32[1024,256]{1,0:T(8,128)} %b_ref.1, f32[1024,256]{1,0:T(8,128)} %t_ref.1), custom_call_target="tpu_custom_call" | custom-call | tf_op jit(solution)/shard_map/pallas_call | solution.py:292
  4.3 0.5 collective-permute-start
  4.8 1.4 %collective-permute-done = f32[576,128]{1,0:T(8,128)S(1)} collective-permute-done((f32[576,128]{1,0:T(8,128)}, f32[576,128]{1,0:T(8,128)S(1)}, u32[]{:S(2)}, u32[]{:S(2)}) %collective-permute-start) | collective-permute-done | bytes 294944 | tf_op jit(solution)/shard_map/ppermute | solution.py:249
  6.3 1.0 %add.6 = f32[576,128]{1,0:T(8,128)S(1)} add(f32[576,128]{1,0:T(8,128)} %get-tuple-element.9, f32[576,128]{1,0:T(8,128)S(1)} %collective-permute-done) | non-fusion elementwise | flops 73728 | bytes 884736 | tf_op jit(solution)/shard_map/add | solution.py:305
  7.3 13.5 %all_to_all.17 = f32[8,72,128]{2,1,0:T(8,128)S(1)} all-to-all(f32[8,72,128]{2,1,0:T(8,128)S(1)} %bitcast.5), channel_id=1, replica_groups={{0,2,4,6,8,10,12,14},{16,18,20,22,24,26,28,30},{1,3,5,7,9,11,13,15},{17..., dimensions={0} | all-to-all | bytes 589824 | tf_op jit(solution)/shard_map/all_to_all | solution.py:269
  20.8 2.7 %collective-permute-start.1 = (f32[72,128]{1,0:T(8,128)S(1)}, f32[72,128]{1,0:T(8,128)S(1)}, u32[]{:S(2)}, u32[]{:S(2)}) collective-permute-start(f32[72,128]{1,0:T(8,128)S(1)} %reduce_sum.9), channel_id=1, source_target_pairs={{0,16},{1,17},{2,18},{3,19},{4,20},{5,21},{6,22},{7,23},{8,24},{9,... | collective-permute-start | bytes 110600 | tf_op jit(solution)/shard_map/ppermute | solution.py:258
  23.4 2.7 %collective-permute-done.1 = f32[72,128]{1,0:T(8,128)S(1)} collective-permute-done((f32[72,128]{1,0:T(8,128)S(1)}, f32[72,128]{1,0:T(8,128)S(1)}, u32[]{:S(2)}, u32[]{:S(2)}) %collective-permute-start.1) | collective-permute-done | bytes 36896 | tf_op jit(solution)/shard_map/ppermute | solution.py:258
  26.1 9.5 %all_to_all.18 = f32[8,72,128]{2,1,0:T(8,128)S(1)} all-to-all(f32[8,72,128]{2,1,0:T(8,128)S(1)} %tile.2), channel_id=1, replica_groups={{0,2,4,6,8,10,12,14},{16,18,20,22,24,26,28,30},{1,3,5,7,9,11,13,15},{17..., dimensions={0} | all-to-all | bytes 589824 | tf_op jit(solution)/shard_map/all_to_all | solution.py:269
  35.6 0.0 copy-start.2
  35.6 0.0 copy-start.3
  35.6 0.0 copy-start
  35.6 0.0 copy-start.1
  35.6 0.1 collective-permute-start.2
  35.7 1.6 %collective-permute-done.2.other_ref = f32[576,128]{1,0:T(8,128)S(1)} collective-permute-done((f32[576,128]{1,0:T(8,128)S(1)}, f32[576,128]{1,0:T(8,128)S(1)}, u32[]{:S(2)}, u32[]{:S(2)}) %collective-permute-start.2) | collective-permute-done | bytes 294944 | tf_op jit(solution)/shard_map/ppermute | solution.py:249
  37.3 0.0 copy-done.2
  37.3 0.0 copy-done.3
  37.3 16.4 %shard_map.47 = (f32[256,256]{1,0:T(8,128)S(1)}, f32[256,256]{1,0:T(8,128)S(1)}) custom-call(s32[1]{0:T(128)} %bitcast.where_ref, f32[16]{0:T(128)S(1)} %copy-done.3, f32[16]{0:T(128)S(1)} %copy-done.2, f32[576,128]{1,0:T(8,128)S(1)} %bitcast.4, f32[576,128]{1,0:T(8,128)S(1)} %collective-permute-done.2.other_ref), custom_call_target="tpu_custom_call" | custom-call | flops 99999997952 | bytes 1000000 | tf_op jit(solution)/shard_map/pallas_call | solution.py:308
  53.6 0.2 collective-permute-start.3
  53.8 0.0 copy-done
  53.8 0.0 copy-done.1
  53.8 0.6 %shard_map.48.z_ref = f32[1024,256]{1,0:T(8,128)S(1)} custom-call(f32[256,256]{1,0:T(8,128)S(1)} %get-tuple-element.12.cross_ref, f32[1024,256]{1,0:T(8,128)S(1)} %copy-done, f32[1024,256]{1,0:T(8,128)S(1)} %copy-done.1), custom_call_target="tpu_custom_call" | custom-call | flops 1000000000 | bytes 3000000 | tf_op jit(solution)/shard_map/pallas_call | solution.py:324
  54.4 0.8 %collective-permute-done.3.other_ref = f32[256,256]{1,0:T(8,128)S(1)} collective-permute-done((f32[256,256]{1,0:T(8,128)S(1)}, f32[256,256]{1,0:T(8,128)S(1)}, u32[]{:S(2)}, u32[]{:S(2)}) %collective-permute-start.3) | collective-permute-done | bytes 262176 | tf_op jit(solution)/shard_map/ppermute | solution.py:249
  55.2 2.2 %shard_map.49 = f32[1024,256]{1,0:T(8,128)} custom-call(f32[256,256]{1,0:T(8,128)S(1)} %get-tuple-element.11.mine_ref, f32[256,256]{1,0:T(8,128)S(1)} %collective-permute-done.3.other_ref, f32[256,256]{1,0:T(8,128)S(1)} %get-tuple-element.12.cross_ref, f32[1024,256]{1,0:T(8,128)S(1)} %shard_map.48.z_ref), custom_call_target="tpu_custom_call" | custom-call | tf_op jit(solution)/shard_map/pallas_call | solution.py:332
  (3 shorter events, 0.0 us)
Async XLA Ops:
  4.3 1.9 %collective-permute-start = (f32[576,128]{1,0:T(8,128)}, f32[576,128]{1,0:T(8,128)S(1)}, u32[]{:S(2)}, u32[]{:S(2)}) collective-permute-start(f32[576,128]{1,0:T(8,128)} %get-tuple-element.10), channel_id=1, source_target_pairs={{0,1},{1,0},{2,3},{3,2},{4,5},{5,4},{6,7},{7,6},{8,9},{9,8},{10,11... | collective-permute-start | bytes 884744 | tf_op jit(solution)/shard_map/ppermute | solution.py:249
  20.8 5.3 %collective-permute-start.1 = (f32[72,128]{1,0:T(8,128)S(1)}, f32[72,128]{1,0:T(8,128)S(1)}, u32[]{:S(2)}, u32[]{:S(2)}) collective-permute-start(f32[72,128]{1,0:T(8,128)S(1)} %reduce_sum.9), channel_id=1, source_target_pairs={{0,16},{1,17},{2,18},{3,19},{4,20},{5,21},{6,22},{7,23},{8,24},{9,... | collective-permute-start | bytes 110600 | tf_op jit(solution)/shard_map/ppermute | solution.py:258
  35.6 1.7 %copy-start.2 = (f32[16]{0:T(128)S(1)}, f32[16]{0:T(128)}, u32[]{:S(2)}) copy-start(f32[16]{0:T(128)} %constant.11.clone.weight_ref) | copy-start | bytes 196
  35.6 1.7 %copy-start.3 = (f32[16]{0:T(128)S(1)}, f32[16]{0:T(128)}, u32[]{:S(2)}) copy-start(f32[16]{0:T(128)} %constant.10.clone.shift_ref) | copy-start | bytes 196
  35.6 18.2 %copy-start = (f32[1024,256]{1,0:T(8,128)S(1)}, f32[1024,256]{1,0:T(8,128)}, u32[]{:S(2)}) copy-start(f32[1024,256]{1,0:T(8,128)} %b_ref.1) | copy-start | bytes 3145732
  35.6 18.2 %copy-start.1 = (f32[1024,256]{1,0:T(8,128)S(1)}, f32[1024,256]{1,0:T(8,128)}, u32[]{:S(2)}) copy-start(f32[1024,256]{1,0:T(8,128)} %t_ref.1) | copy-start | bytes 3145732
  35.6 1.6 %collective-permute-start.2 = (f32[576,128]{1,0:T(8,128)S(1)}, f32[576,128]{1,0:T(8,128)S(1)}, u32[]{:S(2)}, u32[]{:S(2)}) collective-permute-start(f32[576,128]{1,0:T(8,128)S(1)} %bitcast.3), channel_id=1, source_target_pairs={{0,1},{1,0},{2,3},{3,2},{4,5},{5,4},{6,7},{7,6},{8,9},{9,8},{10,11... | collective-permute-start | bytes 884744 | tf_op jit(solution)/shard_map/ppermute | solution.py:249
  53.6 1.6 %collective-permute-start.3 = (f32[256,256]{1,0:T(8,128)S(1)}, f32[256,256]{1,0:T(8,128)S(1)}, u32[]{:S(2)}, u32[]{:S(2)}) collective-permute-start(f32[256,256]{1,0:T(8,128)S(1)} %get-tuple-element.11.mine_ref), channel_id=1, source_target_pairs={{0,1},{1,0},{2,3},{3,2},{4,5},{5,4},{6,7},{7,6},{8,9},{9,8},{10,11... | collective-permute-start | bytes 786440 | tf_op jit(solution)/shard_map/ppermute | solution.py:249

commit v5 on v4

--- a/solution.py
+++ b/solution.py
@@ -33,7 +33,7 @@
 NODES = 8
 CHUNKS = 4
 CUBE = 8
-GRANT = 63 * 1024 * 1024
+GRANT = 53 * 1024 * 1024
 STEP = 32
 F32 = jnp.float32
 BF16 = jnp.bfloat16
@@ -116,7 +116,9 @@
             index = node + (first + p) * NODES
             pan.append([jnp.take_along_axis(x, index, axis=1) for x in v[q]])
         for p in range(8):
-            recip = 1.0 / pan[p][g][p : p + 1, :]
+            pivot = pan[p][g][p : p + 1, :]
+            recip = pl.reciprocal(pivot, approx=True)
+            recip = recip * (2.0 - pivot * recip)
             new = [x for x in pan[p]]
             new[g] = jnp.where(row == p, 1.0, new[g])
             new = [x * recip for x in new]
@@ -186,8 +188,6 @@
             inverses[0, q * 128 : (q + 1) * 128, :] = jnp.concatenate([h, h, m, h], 0).T
             inverses[1, q * 128 : (q + 1) * 128, :] = jnp.concatenate([l, m, m, l], 0).T
 
-        group = iota((n, 128), 1) // STEP
-        index = iota((n, 128), 1) % STEP + inner
         local = iota((STEP, n), 1) - start
         inblock = (local >= 0) & (local < STEP)
         minus = jnp.where(local == iota((STEP, n), 0), -1.0, 0.0)
@@ -200,12 +200,12 @@
             news[m] = jnp.dot(left, stack(panel), preferred_element_type=F32)
         for m in range(NODES):
             rows = slice(m * n, (m + 1) * n)
-            columns = jnp.take_along_axis(mats[tile, rows, :], index, axis=1)
-            h, d, l = split(columns)
-            one = jnp.where(group == 2, d, h)
-            two = jnp.where((group == 0) | (group == 3), l, d)
-            lhs = jnp.concatenate([one, two], 1).astype(BF16)
-            change = jnp.dot(lhs, stack(news[m]), preferred_element_type=F32)
+            here = pl.ds(pl.multiple_of(m * n + start, STEP), STEP)
+            h, d, l = split(jnp.concatenate([mats[0, here, :], mats[1, here, :]], 1))
+            lhs = jnp.concatenate([h, h, d, h, l, d, d, l], 0).astype(BF16)
+            change = lax.dot_general(
+                lhs, stack(news[m]), (((0,), (0,)), ((), ())), preferred_element_type=F32
+            )
             for c in range(2):
                 half = slice(c * 128, (c + 1) * 128)
                 old = mats[c, rows, :]
@@ -227,18 +227,19 @@
         out_ref[:, c * 128 : (c + 1) * 128] = half
 
 
-def residual_kernel(cross_ref, b_ref, t_ref, out_ref):
-    out_ref[...] = t_ref[...] - dot3(halves(b_ref[...]), halves(cross_ref[...]))
-
-
-def lift_kernel(scale, mine_ref, other_ref, cross_ref, z_ref, out_hbm, out_ref, sems):
-    rows = z_ref.shape[0] // CHUNKS
+def residual_kernel(cross_ref, b_ref, t_ref, high_ref, low_ref):
+    z = t_ref[...] - dot3(halves(b_ref[...]), halves(cross_ref[...]))
+    high_ref[...], low_ref[...] = halves(z)
+
+
+def lift_kernel(scale, mine_ref, other_ref, cross_ref, high_ref, low_ref, out_hbm, out_ref, sems):
+    rows = high_ref.shape[0] // CHUNKS
     total = (mine_ref[...] + other_ref[...]) * -scale
-    right = halves(dot(total, cross_ref[...].T))
+    right = halves(dot3(halves(total), halves(cross_ref[...].T)))
     copies = []
     for c in range(CHUNKS):
         part = pl.ds(c * rows, rows)
-        out_ref[part, :] = dot3(halves(z_ref[part, :]), right)
+        out_ref[part, :] = dot3((high_ref[part, :], low_ref[part, :]), right)
         copies.append(pltpu.make_async_copy(out_ref.at[part], out_hbm.at[part], sems.at[c]))
         copies[-1].start()
     for copy in copies:
@@ -321,22 +322,22 @@
         cost_estimate=pl.CostEstimate(flops=10**11, bytes_accessed=10**6, transcendentals=0),
     )(where, jnp.asarray(points**2, F32), jnp.asarray(weights, F32), mine, other)
     other = swap_cores(part)
-    residual = pl.pallas_call(
+    high, low = pl.pallas_call(
         residual_kernel,
-        out_shape=jax.ShapeDtypeStruct((rows, n), F32),
+        out_shape=(jax.ShapeDtypeStruct((rows, n), BF16),) * 2,
         in_specs=[vmem, vmem, vmem],
-        out_specs=vmem,
+        out_specs=(vmem, vmem),
         compiler_params=limit,
         cost_estimate=pl.CostEstimate(flops=10**9, bytes_accessed=3 * 10**6, transcendentals=0),
     )(cross, basis, target)
     return pl.pallas_call(
         functools.partial(lift_kernel, float(np.sqrt(total_rows))),
         out_shape=jax.ShapeDtypeStruct((rows, n), F32),
-        in_specs=[vmem] * 4,
+        in_specs=[vmem] * 5,
         out_specs=hbm,
         scratch_shapes=[pltpu.VMEM((rows, n), F32), pltpu.SemaphoreType.DMA((CHUNKS,))],
         compiler_params=limit,
-    )(part, other, cross, residual)
+    )(part, other, cross, high, low)
 
 
 def solution(mesh):

time: 57.6 us -> 67.7 us (1.18)
  Pallas kernels: 23.4 us -> 34.7 us
  other arithmetic: 1.03 us -> 0.06 us
    pallas_call x1, Pallas kernels: 16.4 us -> 28.9 us  [on_device(): pl.pallas_call(resolvent_kernel, out_shape=(square, square), in_specs=[sm...]
    add x1, other arithmetic: 1.01 us -> 0.03 us  [on_device(): mine = summed(keep + swap_cores(send), mesh)]
    pallas_call x1, Pallas kernels: 4.31 us -> 3.52 us  [on_device(): pl.pallas_call(gram_kernel, out_shape=(half, half), in_specs=[smem, hbm,...]
where the time goes in v5:
time: 67.7 us; the launch traced here: 67.5 us
  Pallas kernels  34.7 us (51%)
  blocking collectives  23 us (34%)
  waiting for transfers between devices  6.23 us (9%)
  starting transfers between devices  3.45 us (5%)
    pallas_call x1, Pallas kernels, on_device(): pl.pallas_call(resolvent_kernel, out_shape=(square, square), in_specs=[sm...  28.9 us
    all_to_all x2, blocking collectives, cube(): lax.all_to_all(pieces, ('gx', 'gy'), 0, 0, axis_index_groups=groups, tile...  23 us
    ppermute x3, waiting for transfers between devices, swap_cores(): return lax.ppermute(x, 'gz', [(0, 1), (1, 0)])  3.57 us
    pallas_call x1, Pallas kernels, on_device(): pl.pallas_call(gram_kernel, out_shape=(half, half), in_specs=[smem, hbm,...  3.52 us
    ppermute x1, waiting for transfers between devices, swap_bits(): return lax.ppermute(x, ('gx', 'gy', 'gz'), perm)  2.66 us
    ppermute x1, starting transfers between devices, swap_bits(): return lax.ppermute(x, ('gx', 'gy', 'gz'), perm)  2.65 us
    pallas_call x1, Pallas kernels, on_device(): pl.pallas_call(functools.partial(lift_kernel, float(np.sqrt(total_rows)))...  1.74 us
  transfers between devices with their start and end apart: 4, of which 4 were waited for; matrix products, arithmetic and copies ran while one was open for 0% of the time, Pallas kernels for 1%

profile of v5, /device:TPU:0, one launch (start us, length us, event | category | flops | bytes accessed | tf_op | source)
XLA Modules:
  0.0 67.5 jit_solution(6933349920546123433)
XLA Ops:
  0.0 3.5 %shard_map.46 = (f32[576,128]{1,0:T(8,128)S(1)}, f32[576,128]{1,0:T(8,128)S(1)}) custom-call(s32[1]{0:T(128)} %bitcast.where_ref, f32[1024,256]{1,0:T(8,128)} %b_ref.1, f32[1024,256]{1,0:T(8,128)} %t_ref.1), custom_call_target="tpu_custom_call" | custom-call | tf_op jit(solution)/shard_map/pallas_call | solution.py:293
  3.5 0.5 collective-permute-start
  4.1 1.2 %collective-permute-done = f32[576,128]{1,0:T(8,128)S(1)} collective-permute-done((f32[576,128]{1,0:T(8,128)S(1)}, f32[576,128]{1,0:T(8,128)S(1)}, u32[]{:S(2)}, u32[]{:S(2)}) %collective-permute-start) | collective-permute-done | bytes 294944 | tf_op jit(solution)/shard_map/ppermute | solution.py:250
  5.3 13.5 %all_to_all.17 = f32[8,72,128]{2,1,0:T(8,128)S(1)} all-to-all(f32[8,72,128]{2,1,0:T(8,128)S(1)} %bitcast.5), channel_id=1, replica_groups={{0,2,4,6,8,10,12,14},{16,18,20,22,24,26,28,30},{1,3,5,7,9,11,13,15},{17..., dimensions={0} | all-to-all | bytes 589824 | tf_op jit(solution)/shard_map/all_to_all | solution.py:270
  18.8 2.7 %collective-permute-start.1 = (f32[72,128]{1,0:T(8,128)S(1)}, f32[72,128]{1,0:T(8,128)S(1)}, u32[]{:S(2)}, u32[]{:S(2)}) collective-permute-start(f32[72,128]{1,0:T(8,128)S(1)} %reduce_sum.9), channel_id=1, source_target_pairs={{0,16},{1,17},{2,18},{3,19},{4,20},{5,21},{6,22},{7,23},{8,24},{9,... | collective-permute-start | bytes 110600 | tf_op jit(solution)/shard_map/ppermute | solution.py:259
  21.4 2.7 %collective-permute-done.1 = f32[72,128]{1,0:T(8,128)S(1)} collective-permute-done((f32[72,128]{1,0:T(8,128)S(1)}, f32[72,128]{1,0:T(8,128)S(1)}, u32[]{:S(2)}, u32[]{:S(2)}) %collective-permute-start.1) | collective-permute-done | bytes 36896 | tf_op jit(solution)/shard_map/ppermute | solution.py:259
  24.1 9.5 %all_to_all.18 = f32[8,72,128]{2,1,0:T(8,128)S(1)} all-to-all(f32[8,72,128]{2,1,0:T(8,128)S(1)} %tile.2), channel_id=1, replica_groups={{0,2,4,6,8,10,12,14},{16,18,20,22,24,26,28,30},{1,3,5,7,9,11,13,15},{17..., dimensions={0} | all-to-all | bytes 589824 | tf_op jit(solution)/shard_map/all_to_all | solution.py:270
  33.6 0.0 copy-start.2
  33.6 0.0 copy-start.3
  33.6 0.0 copy-start
  33.6 0.0 copy-start.1
  33.6 0.1 collective-permute-start.2
  33.7 1.6 %collective-permute-done.2.other_ref = f32[576,128]{1,0:T(8,128)S(1)} collective-permute-done((f32[576,128]{1,0:T(8,128)S(1)}, f32[576,128]{1,0:T(8,128)S(1)}, u32[]{:S(2)}, u32[]{:S(2)}) %collective-permute-start.2) | collective-permute-done | bytes 294944 | tf_op jit(solution)/shard_map/ppermute | solution.py:250
  35.3 0.0 copy-done.2
  35.3 0.0 copy-done.3
  35.3 28.9 %shard_map.47 = (f32[256,256]{1,0:T(8,128)S(1)}, f32[256,256]{1,0:T(8,128)S(1)}) custom-call(s32[1]{0:T(128)} %bitcast.where_ref, f32[16]{0:T(128)S(1)} %copy-done.3, f32[16]{0:T(128)S(1)} %copy-done.2, f32[576,128]{1,0:T(8,128)S(1)} %bitcast.4, f32[576,128]{1,0:T(8,128)S(1)} %collective-permute-done.2.other_ref), custom_call_target="tpu_custom_call" | custom-call | flops 99999997952 | bytes 1000000 | tf_op jit(solution)/shard_map/pallas_call | solution.py:309
  64.1 0.2 collective-permute-start.3
  64.4 0.0 copy-done
  64.4 0.0 copy-done.1
  64.4 0.6 shard_map.48
  65.0 0.8 %collective-permute-done.3.other_ref = f32[256,256]{1,0:T(8,128)S(1)} collective-permute-done((f32[256,256]{1,0:T(8,128)S(1)}, f32[256,256]{1,0:T(8,128)S(1)}, u32[]{:S(2)}, u32[]{:S(2)}) %collective-permute-start.3) | collective-permute-done | bytes 262176 | tf_op jit(solution)/shard_map/ppermute | solution.py:250
  65.7 1.7 %shard_map.49 = f32[1024,256]{1,0:T(8,128)} custom-call(f32[256,256]{1,0:T(8,128)S(1)} %get-tuple-element.13.mine_ref, f32[256,256]{1,0:T(8,128)S(1)} %collective-permute-done.3.other_ref, f32[256,256]{1,0:T(8,128)S(1)} %get-tuple-element.14.cross_ref, bf16[1024,256]{1,0:T(8,128)(2,1)S(1)} %get-tuple-element.15.high_ref, ...), custom_call_target="tpu_custom_call" | custom-call | tf_op jit(solution)/shard_map/pallas_call | solution.py:333
  (4 shorter events, 0.1 us)
Async XLA Ops:
  3.5 1.7 %collective-permute-start = (f32[576,128]{1,0:T(8,128)S(1)}, f32[576,128]{1,0:T(8,128)S(1)}, u32[]{:S(2)}, u32[]{:S(2)}) collective-permute-start(f32[576,128]{1,0:T(8,128)S(1)} %get-tuple-element.12), channel_id=1, source_target_pairs={{0,1},{1,0},{2,3},{3,2},{4,5},{5,4},{6,7},{7,6},{8,9},{9,8},{10,11... | collective-permute-start | bytes 884744 | tf_op jit(solution)/shard_map/ppermute | solution.py:250
  18.8 5.3 %collective-permute-start.1 = (f32[72,128]{1,0:T(8,128)S(1)}, f32[72,128]{1,0:T(8,128)S(1)}, u32[]{:S(2)}, u32[]{:S(2)}) collective-permute-start(f32[72,128]{1,0:T(8,128)S(1)} %reduce_sum.9), channel_id=1, source_target_pairs={{0,16},{1,17},{2,18},{3,19},{4,20},{5,21},{6,22},{7,23},{8,24},{9,... | collective-permute-start | bytes 110600 | tf_op jit(solution)/shard_map/ppermute | solution.py:259
  33.6 1.7 %copy-start.2 = (f32[16]{0:T(128)S(1)}, f32[16]{0:T(128)}, u32[]{:S(2)}) copy-start(f32[16]{0:T(128)} %constant.11.clone.weight_ref) | copy-start | bytes 196
  33.6 1.7 %copy-start.3 = (f32[16]{0:T(128)S(1)}, f32[16]{0:T(128)}, u32[]{:S(2)}) copy-start(f32[16]{0:T(128)} %constant.10.clone.shift_ref) | copy-start | bytes 196
  33.6 30.7 %copy-start = (f32[1024,256]{1,0:T(8,128)S(1)}, f32[1024,256]{1,0:T(8,128)}, u32[]{:S(2)}) copy-start(f32[1024,256]{1,0:T(8,128)} %b_ref.1) | copy-start | bytes 3145732
  33.6 30.7 %copy-start.1 = (f32[1024,256]{1,0:T(8,128)S(1)}, f32[1024,256]{1,0:T(8,128)}, u32[]{:S(2)}) copy-start(f32[1024,256]{1,0:T(8,128)} %t_ref.1) | copy-start | bytes 3145732
  33.6 1.6 %collective-permute-start.2 = (f32[576,128]{1,0:T(8,128)S(1)}, f32[576,128]{1,0:T(8,128)S(1)}, u32[]{:S(2)}, u32[]{:S(2)}) collective-permute-start(f32[576,128]{1,0:T(8,128)S(1)} %bitcast.3), channel_id=1, source_target_pairs={{0,1},{1,0},{2,3},{3,2},{4,5},{5,4},{6,7},{7,6},{8,9},{9,8},{10,11... | collective-permute-start | bytes 884744 | tf_op jit(solution)/shard_map/ppermute | solution.py:250
  64.1 1.6 %collective-permute-start.3 = (f32[256,256]{1,0:T(8,128)S(1)}, f32[256,256]{1,0:T(8,128)S(1)}, u32[]{:S(2)}, u32[]{:S(2)}) collective-permute-start(f32[256,256]{1,0:T(8,128)S(1)} %get-tuple-element.13.mine_ref), channel_id=1, source_target_pairs={{0,1},{1,0},{2,3},{3,2},{4,5},{5,4},{6,7},{7,6},{8,9},{9,8},{10,11... | collective-permute-start | bytes 786440 | tf_op jit(solution)/shard_map/ppermute | solution.py:250

commit v6 on v5

--- a/solution.py
+++ b/solution.py
@@ -105,7 +105,7 @@
     send_ref[...] = pay[pl.ds(pl.multiple_of((1 - core) * half, 8), half), :]
 
 
-def invert_blocks(v):
+def invert_blocks(v, between):
     group = iota((8, 128), 1) // NODES
     node = iota((8, 128), 1) % NODES
     row = iota((8, 128), 0)
@@ -139,13 +139,15 @@
                 for p in range(8):
                     acc = [jnp.where(group == first + p, y, x) for x, y in zip(acc, pan[p])]
             v[o] = acc
+        between[g]()
     return v
 
 
 def resolvent_kernel(
-    where_ref, shift_ref, weight_ref, mine_ref, other_ref, out_ref, cross_ref, mats, turned, inverses, news, pay
+    where_ref, shift_ref, weight_ref, mine_ref, other_ref, out_ref, cross_ref, pay, blocks, turned, inverses, news, *mats
 ):
     n = out_ref.shape[1]
+    last = n // STEP - 1
     half, core = mine_ref.shape[0], where_ref[0]
     pay[pl.ds(pl.multiple_of(core * half, 8), half), :] = mine_ref[...]
     pay[pl.ds(pl.multiple_of((1 - core) * half, 8), half), :] = other_ref[...]
@@ -166,65 +168,83 @@
     normal = tgram - 2.0 * square + dot(crosst, dot(bgram, cross))
     for m in range(NODES):
         shifted = square + shift_ref[core * NODES + m] * normal
-        mats[0, m * n : (m + 1) * n, :] = shifted[:, 0:128]
-        mats[1, m * n : (m + 1) * n, :] = shifted[:, 128:256]
+        mats[m][0] = shifted[:, 0:128]
+        mats[m][1] = shifted[:, 128:256]
+        blocks[m * STEP : (m + 1) * STEP, :] = shifted[0:STEP, 0:128]
 
     def stack(x):
         h, m, l = split(x)
         return jnp.concatenate([h, m, h, l, h, m, l, m], 0).astype(BF16)
 
-    def step(tile, part, carry):
-        inner = pl.multiple_of(part * STEP, STEP)
-        start = pl.multiple_of(tile * 128 + inner, STEP)
+    def spread(x, first):
+        lane = iota(x.shape, 1)
+        group = lane // STEP
+        h, d, l = split(jnp.take_along_axis(x, lane % STEP + first, axis=1))
+        one = jnp.where(group == 2, d, h)
+        two = jnp.where((group == 0) | (group == 3), l, d)
+        return jnp.concatenate([one, two], 1).astype(BF16)
+
+    def place(kb):
+        return kb // 4, pl.multiple_of(kb % 4 * STEP, STEP), pl.ds(pl.multiple_of(kb * STEP, STEP), STEP)
+
+    def columns_of(kb):
+        local = iota((STEP, n), 1) - kb * STEP
+        return local, (local >= 0) & (local < STEP)
+
+    def update(kb, m):
+        tile, first, here = place(kb)
+        local, inblock = columns_of(kb)
+        new = jnp.concatenate([news[m, 0], news[m, 1]], 1)
+        change = jnp.dot(spread(mats[m][tile], first), stack(new), preferred_element_type=F32)
+        for c in range(2):
+            part = slice(c * 128, (c + 1) * 128)
+            mats[m][c] = jnp.where(inblock[0:1, part], 0.0, mats[m][c]) - change[:, part]
+        for c in range(2):
+            mats[m][c, here, :] = news[m, c]
+
+    def pivots(kb, work):
+        tile, first, here = place(kb)
         v = []
         for q in range(2):
-            rows = [mats[tile, pl.ds(start + 16 * q + i, NODES, stride=n), :] for i in range(16)]
+            rows = [blocks[pl.ds(16 * q + i, NODES, stride=STEP), :] for i in range(16)]
             turned[q] = jnp.concatenate(rows, 0).T
-            block = turned[q, pl.ds(inner, STEP), :]
+            block = turned[q, pl.ds(first, STEP), :]
             v.append([block[8 * g : 8 * g + 8] for g in range(4)])
-        v = invert_blocks(v)
+        v = invert_blocks(v, work)
         for q in range(2):
-            h, m, l = split(jnp.concatenate(v[q], 0))
-            inverses[0, q * 128 : (q + 1) * 128, :] = jnp.concatenate([h, h, m, h], 0).T
-            inverses[1, q * 128 : (q + 1) * 128, :] = jnp.concatenate([l, m, m, l], 0).T
-
-        local = iota((STEP, n), 1) - start
-        inblock = (local >= 0) & (local < STEP)
+            inverses[q * 128 : (q + 1) * 128, 0:STEP] = jnp.concatenate(v[q], 0).T
+        local, inblock = columns_of(kb)
         minus = jnp.where(local == iota((STEP, n), 0), -1.0, 0.0)
         for m in range(NODES):
-            left = [inverses[c, pl.ds(m, STEP, stride=NODES), :] for c in range(2)]
-            left = jnp.concatenate(left, 1).astype(BF16)
-            here = pl.ds(pl.multiple_of(m * n + start, STEP), STEP)
-            panel = jnp.concatenate([mats[0, here, :], mats[1, here, :]], 1)
+            left = spread(inverses[pl.ds(m, STEP, stride=NODES), :], 0)
+            panel = jnp.concatenate([mats[m][0, here, :], mats[m][1, here, :]], 1)
             panel = jnp.where(inblock, minus, panel)
-            news[m] = jnp.dot(left, stack(panel), preferred_element_type=F32)
+            new = jnp.dot(left, stack(panel), preferred_element_type=F32)
+            news[m, 0] = new[:, 0:128]
+            news[m, 1] = new[:, 128:256]
+        tile1, _, here1 = place(jnp.minimum(kb + 1, last))
         for m in range(NODES):
-            rows = slice(m * n, (m + 1) * n)
-            here = pl.ds(pl.multiple_of(m * n + start, STEP), STEP)
-            h, d, l = split(jnp.concatenate([mats[0, here, :], mats[1, here, :]], 1))
-            lhs = jnp.concatenate([h, h, d, h, l, d, d, l], 0).astype(BF16)
-            change = lax.dot_general(
-                lhs, stack(news[m]), (((0,), (0,)), ((), ())), preferred_element_type=F32
-            )
-            for c in range(2):
-                half = slice(c * 128, (c + 1) * 128)
-                old = mats[c, rows, :]
-                if c == tile:
-                    old = jnp.where(inblock[0:1, half], 0.0, old)
-                mats[c, rows, :] = old - change[:, half]
-        for m in range(NODES):
-            here = pl.ds(pl.multiple_of(m * n + start, STEP), STEP)
-            mats[0, here, :] = news[m, :, 0:128]
-            mats[1, here, :] = news[m, :, 128:256]
+            left = spread(mats[m][tile, here1, :], first)
+            change = jnp.dot(left, stack(news[m, tile1]), preferred_element_type=F32)
+            blocks[m * STEP : (m + 1) * STEP, :] = mats[m][tile1, here1, :] - change
+
+    def step(kb, carry):
+        def updates(g):
+            for m in range(2 * g, 2 * g + 2):
+                update(kb - 1, m)
+
+        pivots(kb, [functools.partial(updates, g) for g in range(4)])
         return carry
 
-    for tile in range(2):
-        lax.fori_loop(0, 4, functools.partial(step, tile), 0)
+    pivots(jnp.int32(0), [lambda: None] * 4)
+    lax.fori_loop(1, last + 1, step, 0)
+    for m in range(NODES):
+        update(jnp.int32(last), m)
     for c in range(2):
-        half = weight_ref[core * NODES] * mats[c, 0:n, :]
+        total = weight_ref[core * NODES] * mats[0][c]
         for m in range(1, NODES):
-            half = half + weight_ref[core * NODES + m] * mats[c, m * n : (m + 1) * n, :]
-        out_ref[:, c * 128 : (c + 1) * 128] = half
+            total = total + weight_ref[core * NODES + m] * mats[m][c]
+        out_ref[:, c * 128 : (c + 1) * 128] = total
 
 
 def residual_kernel(cross_ref, b_ref, t_ref, high_ref, low_ref):
@@ -312,12 +332,13 @@
         in_specs=[smem, smem, smem, vmem, vmem],
         out_specs=(vmem, vmem),
         scratch_shapes=[
-            pltpu.VMEM((2, NODES * n, 128), F32),
+            pltpu.VMEM((2 * pay_half, 128), F32),
+            pltpu.VMEM((NODES * STEP, 128), F32),
             pltpu.VMEM((2, 128, 128), F32),
-            pltpu.VMEM((2, 2 * 128, 128), F32),
-            pltpu.VMEM((NODES, STEP, n), F32),
-            pltpu.VMEM((2 * pay_half, 128), F32),
-        ],
+            pltpu.VMEM((2 * 128, 128), F32),
+            pltpu.VMEM((NODES, 2, STEP, 128), F32),
+        ]
+        + [pltpu.VMEM((2, n, 128), F32)] * NODES,
         compiler_params=limit,
         cost_estimate=pl.CostEstimate(flops=10**11, bytes_accessed=10**6, transcendentals=0),
     )(where, jnp.asarray(points**2, F32), jnp.asarray(weights, F32), mine, other)

time: 67.7 us -> 56.2 us (0.83)
  Pallas kernels: 34.7 us -> 23.2 us
    pallas_call x1, Pallas kernels: 28.9 us -> 17.3 us  [on_device(): pl.pallas_call(resolvent_kernel, out_shape=(square, square), in_specs=[sm...]
where the time goes in v6:
time: 56.2 us; the launch traced here: 56 us
  Pallas kernels  23.2 us (41%)
  blocking collectives  23 us (41%)
  waiting for transfers between devices  6.23 us (11%)
  starting transfers between devices  3.45 us (6%)
    all_to_all x2, blocking collectives, cube(): lax.all_to_all(pieces, ('gx', 'gy'), 0, 0, axis_index_groups=groups, tile...  23 us
    pallas_call x1, Pallas kernels, on_device(): pl.pallas_call(resolvent_kernel, out_shape=(square, square), in_specs=[sm...  17.3 us
    ppermute x3, waiting for transfers between devices, swap_cores(): return lax.ppermute(x, 'gz', [(0, 1), (1, 0)])  3.57 us
    pallas_call x1, Pallas kernels, on_device(): pl.pallas_call(gram_kernel, out_shape=(half, half), in_specs=[smem, hbm,...  3.52 us
    ppermute x1, waiting for transfers between devices, swap_bits(): return lax.ppermute(x, ('gx', 'gy', 'gz'), perm)  2.66 us
    ppermute x1, starting transfers between devices, swap_bits(): return lax.ppermute(x, ('gx', 'gy', 'gz'), perm)  2.65 us
    pallas_call x1, Pallas kernels, on_device(): pl.pallas_call(functools.partial(lift_kernel, float(np.sqrt(total_rows)))...  1.74 us
  transfers between devices with their start and end apart: 4, of which 4 were waited for; matrix products, arithmetic and copies ran while one was open for 0% of the time, Pallas kernels for 1%

profile of v6, /device:TPU:0, one launch (start us, length us, event | category | flops | bytes accessed | tf_op | source)
XLA Modules:
  0.0 56.0 jit_solution(4017393945494747297)
XLA Ops:
  0.0 3.5 %shard_map.46 = (f32[576,128]{1,0:T(8,128)S(1)}, f32[576,128]{1,0:T(8,128)S(1)}) custom-call(s32[1]{0:T(128)} %bitcast.where_ref, f32[1024,256]{1,0:T(8,128)} %b_ref.1, f32[1024,256]{1,0:T(8,128)} %t_ref.1), custom_call_target="tpu_custom_call" | custom-call | tf_op jit(solution)/shard_map/pallas_call | solution.py:313
  3.5 0.5 collective-permute-start
  4.1 1.2 %collective-permute-done = f32[576,128]{1,0:T(8,128)S(1)} collective-permute-done((f32[576,128]{1,0:T(8,128)S(1)}, f32[576,128]{1,0:T(8,128)S(1)}, u32[]{:S(2)}, u32[]{:S(2)}) %collective-permute-start) | collective-permute-done | bytes 294944 | tf_op jit(solution)/shard_map/ppermute | solution.py:270
  5.3 13.5 %all_to_all.17 = f32[8,72,128]{2,1,0:T(8,128)S(1)} all-to-all(f32[8,72,128]{2,1,0:T(8,128)S(1)} %bitcast.5), channel_id=1, replica_groups={{0,2,4,6,8,10,12,14},{16,18,20,22,24,26,28,30},{1,3,5,7,9,11,13,15},{17..., dimensions={0} | all-to-all | bytes 589824 | tf_op jit(solution)/shard_map/all_to_all | solution.py:290
  18.8 2.7 %collective-permute-start.1 = (f32[72,128]{1,0:T(8,128)S(1)}, f32[72,128]{1,0:T(8,128)S(1)}, u32[]{:S(2)}, u32[]{:S(2)}) collective-permute-start(f32[72,128]{1,0:T(8,128)S(1)} %reduce_sum.9), channel_id=1, source_target_pairs={{0,16},{1,17},{2,18},{3,19},{4,20},{5,21},{6,22},{7,23},{8,24},{9,... | collective-permute-start | bytes 110600 | tf_op jit(solution)/shard_map/ppermute | solution.py:279
  21.4 2.7 %collective-permute-done.1 = f32[72,128]{1,0:T(8,128)S(1)} collective-permute-done((f32[72,128]{1,0:T(8,128)S(1)}, f32[72,128]{1,0:T(8,128)S(1)}, u32[]{:S(2)}, u32[]{:S(2)}) %collective-permute-start.1) | collective-permute-done | bytes 36896 | tf_op jit(solution)/shard_map/ppermute | solution.py:279
  24.1 9.5 %all_to_all.18 = f32[8,72,128]{2,1,0:T(8,128)S(1)} all-to-all(f32[8,72,128]{2,1,0:T(8,128)S(1)} %tile.2), channel_id=1, replica_groups={{0,2,4,6,8,10,12,14},{16,18,20,22,24,26,28,30},{1,3,5,7,9,11,13,15},{17..., dimensions={0} | all-to-all | bytes 589824 | tf_op jit(solution)/shard_map/all_to_all | solution.py:290
  33.6 0.0 copy-start.2
  33.6 0.0 copy-start.3
  33.6 0.0 copy-start
  33.6 0.0 copy-start.1
  33.6 0.1 collective-permute-start.2
  33.7 1.6 %collective-permute-done.2.other_ref = f32[576,128]{1,0:T(8,128)S(1)} collective-permute-done((f32[576,128]{1,0:T(8,128)S(1)}, f32[576,128]{1,0:T(8,128)S(1)}, u32[]{:S(2)}, u32[]{:S(2)}) %collective-permute-start.2) | collective-permute-done | bytes 294944 | tf_op jit(solution)/shard_map/ppermute | solution.py:270
  35.3 0.0 copy-done.2
  35.3 0.0 copy-done.3
  35.3 17.3 %shard_map.47 = (f32[256,256]{1,0:T(8,128)S(1)}, f32[256,256]{1,0:T(8,128)S(1)}) custom-call(s32[1]{0:T(128)} %bitcast.where_ref, f32[16]{0:T(128)S(1)} %copy-done.3, f32[16]{0:T(128)S(1)} %copy-done.2, f32[576,128]{1,0:T(8,128)S(1)} %bitcast.4, f32[576,128]{1,0:T(8,128)S(1)} %collective-permute-done.2.other_ref), custom_call_target="tpu_custom_call" | custom-call | flops 99999997952 | bytes 1000000 | tf_op jit(solution)/shard_map/pallas_call | solution.py:329
  52.6 0.2 collective-permute-start.3
  52.8 0.0 copy-done
  52.8 0.0 copy-done.1
  52.8 0.6 %shard_map.48 = (bf16[1024,256]{1,0:T(8,128)(2,1)S(1)}, bf16[1024,256]{1,0:T(8,128)(2,1)S(1)}) custom-call(f32[256,256]{1,0:T(8,128)S(1)} %get-tuple-element.14.cross_ref, f32[1024,256]{1,0:T(8,128)S(1)} %copy-done, f32[1024,256]{1,0:T(8,128)S(1)} %copy-done.1), custom_call_target="tpu_custom_call" | custom-call | flops 1000000000 | bytes 3000000 | tf_op jit(solution)/shard_map/pallas_call | solution.py:346
  53.4 0.8 %collective-permute-done.3.other_ref = f32[256,256]{1,0:T(8,128)S(1)} collective-permute-done((f32[256,256]{1,0:T(8,128)S(1)}, f32[256,256]{1,0:T(8,128)S(1)}, u32[]{:S(2)}, u32[]{:S(2)}) %collective-permute-start.3) | collective-permute-done | bytes 262176 | tf_op jit(solution)/shard_map/ppermute | solution.py:270
  54.2 1.7 %shard_map.49 = f32[1024,256]{1,0:T(8,128)} custom-call(f32[256,256]{1,0:T(8,128)S(1)} %get-tuple-element.13.mine_ref, f32[256,256]{1,0:T(8,128)S(1)} %collective-permute-done.3.other_ref, f32[256,256]{1,0:T(8,128)S(1)} %get-tuple-element.14.cross_ref, bf16[1024,256]{1,0:T(8,128)(2,1)S(1)} %get-tuple-element.15.high_ref, ...), custom_call_target="tpu_custom_call" | custom-call | tf_op jit(solution)/shard_map/pallas_call | solution.py:354
  (4 shorter events, 0.1 us)
Async XLA Ops:
  3.5 1.7 %collective-permute-start = (f32[576,128]{1,0:T(8,128)S(1)}, f32[576,128]{1,0:T(8,128)S(1)}, u32[]{:S(2)}, u32[]{:S(2)}) collective-permute-start(f32[576,128]{1,0:T(8,128)S(1)} %get-tuple-element.12), channel_id=1, source_target_pairs={{0,1},{1,0},{2,3},{3,2},{4,5},{5,4},{6,7},{7,6},{8,9},{9,8},{10,11... | collective-permute-start | bytes 884744 | tf_op jit(solution)/shard_map/ppermute | solution.py:270
  18.8 5.3 %collective-permute-start.1 = (f32[72,128]{1,0:T(8,128)S(1)}, f32[72,128]{1,0:T(8,128)S(1)}, u32[]{:S(2)}, u32[]{:S(2)}) collective-permute-start(f32[72,128]{1,0:T(8,128)S(1)} %reduce_sum.9), channel_id=1, source_target_pairs={{0,16},{1,17},{2,18},{3,19},{4,20},{5,21},{6,22},{7,23},{8,24},{9,... | collective-permute-start | bytes 110600 | tf_op jit(solution)/shard_map/ppermute | solution.py:279
  33.6 1.7 %copy-start.2 = (f32[16]{0:T(128)S(1)}, f32[16]{0:T(128)}, u32[]{:S(2)}) copy-start(f32[16]{0:T(128)} %constant.11.clone.weight_ref) | copy-start | bytes 196
  33.6 1.7 %copy-start.3 = (f32[16]{0:T(128)S(1)}, f32[16]{0:T(128)}, u32[]{:S(2)}) copy-start(f32[16]{0:T(128)} %constant.10.clone.shift_ref) | copy-start | bytes 196
  33.6 19.2 %copy-start = (f32[1024,256]{1,0:T(8,128)S(1)}, f32[1024,256]{1,0:T(8,128)}, u32[]{:S(2)}) copy-start(f32[1024,256]{1,0:T(8,128)} %b_ref.1) | copy-start | bytes 3145732
  33.6 19.2 %copy-start.1 = (f32[1024,256]{1,0:T(8,128)S(1)}, f32[1024,256]{1,0:T(8,128)}, u32[]{:S(2)}) copy-start(f32[1024,256]{1,0:T(8,128)} %t_ref.1) | copy-start | bytes 3145732
  33.6 1.6 %collective-permute-start.2 = (f32[576,128]{1,0:T(8,128)S(1)}, f32[576,128]{1,0:T(8,128)S(1)}, u32[]{:S(2)}, u32[]{:S(2)}) collective-permute-start(f32[576,128]{1,0:T(8,128)S(1)} %bitcast.3), channel_id=1, source_target_pairs={{0,1},{1,0},{2,3},{3,2},{4,5},{5,4},{6,7},{7,6},{8,9},{9,8},{10,11... | collective-permute-start | bytes 884744 | tf_op jit(solution)/shard_map/ppermute | solution.py:270
  52.6 1.6 %collective-permute-start.3 = (f32[256,256]{1,0:T(8,128)S(1)}, f32[256,256]{1,0:T(8,128)S(1)}, u32[]{:S(2)}, u32[]{:S(2)}) collective-permute-start(f32[256,256]{1,0:T(8,128)S(1)} %get-tuple-element.13.mine_ref), channel_id=1, source_target_pairs={{0,1},{1,0},{2,3},{3,2},{4,5},{5,4},{6,7},{7,6},{8,9},{9,8},{10,11... | collective-permute-start | bytes 786440 | tf_op jit(solution)/shard_map/ppermute | solution.py:270

commit v7 on v6

--- a/solution.py
+++ b/solution.py
@@ -129,6 +129,8 @@
                     old = [x for x in pan[o]]
                     old[g] = jnp.where(row == p, 0.0, old[g])
                     pan[o] = [x - factor * y for x, y in zip(old, new)]
+            if p % 2:
+                between[(8 * g + p) // 2]()
         for o in range(2):
             acc = [x for x in v[o]]
             acc[g] = jnp.zeros((8, 128), F32)
@@ -139,12 +141,11 @@
                 for p in range(8):
                     acc = [jnp.where(group == first + p, y, x) for x, y in zip(acc, pan[p])]
             v[o] = acc
-        between[g]()
     return v
 
 
 def resolvent_kernel(
-    where_ref, shift_ref, weight_ref, mine_ref, other_ref, out_ref, cross_ref, pay, blocks, turned, inverses, news, *mats
+    where_ref, shift_ref, weight_ref, mine_ref, other_ref, out_ref, cross_ref, pay, blocks, turned, inverses, news, stacks, *mats
 ):
     n = out_ref.shape[1]
     last = n // STEP - 1
@@ -191,16 +192,19 @@
         local = iota((STEP, n), 1) - kb * STEP
         return local, (local >= 0) & (local < STEP)
 
-    def update(kb, m):
+    def update(kb, m, side):
         tile, first, here = place(kb)
         local, inblock = columns_of(kb)
-        new = jnp.concatenate([news[m, 0], news[m, 1]], 1)
-        change = jnp.dot(spread(mats[m][tile], first), stack(new), preferred_element_type=F32)
+        rows = slice(side * 128, (side + 1) * 128)
+        right = jnp.concatenate([stacks[m, 0], stacks[m, 1]], 1)
+        change = jnp.dot(spread(mats[m][tile, rows, :], first), right, preferred_element_type=F32)
         for c in range(2):
             part = slice(c * 128, (c + 1) * 128)
-            mats[m][c] = jnp.where(inblock[0:1, part], 0.0, mats[m][c]) - change[:, part]
-        for c in range(2):
-            mats[m][c, here, :] = news[m, c]
+            old = jnp.where(inblock[0:1, part], 0.0, mats[m][c, rows, :])
+            mats[m][c, rows, :] = old - change[:, part]
+        if side == 1:
+            for c in range(2):
+                mats[m][c, here, :] = news[m, c]
 
     def pivots(kb, work):
         tile, first, here = place(kb)
@@ -220,26 +224,26 @@
             panel = jnp.concatenate([mats[m][0, here, :], mats[m][1, here, :]], 1)
             panel = jnp.where(inblock, minus, panel)
             new = jnp.dot(left, stack(panel), preferred_element_type=F32)
-            news[m, 0] = new[:, 0:128]
-            news[m, 1] = new[:, 128:256]
+            for c in range(2):
+                part = new[:, c * 128 : (c + 1) * 128]
+                news[m, c] = part
+                stacks[m, c] = stack(part)
         tile1, _, here1 = place(jnp.minimum(kb + 1, last))
         for m in range(NODES):
             left = spread(mats[m][tile, here1, :], first)
-            change = jnp.dot(left, stack(news[m, tile1]), preferred_element_type=F32)
+            change = jnp.dot(left, stacks[m, tile1], preferred_element_type=F32)
             blocks[m * STEP : (m + 1) * STEP, :] = mats[m][tile1, here1, :] - change
 
     def step(kb, carry):
-        def updates(g):
-            for m in range(2 * g, 2 * g + 2):
-                update(kb - 1, m)
-
-        pivots(kb, [functools.partial(updates, g) for g in range(4)])
+        work = [functools.partial(update, kb - 1, m, side) for m in range(NODES) for side in range(2)]
+        pivots(kb, work)
         return carry
 
-    pivots(jnp.int32(0), [lambda: None] * 4)
+    pivots(jnp.int32(0), [lambda: None] * 16)
     lax.fori_loop(1, last + 1, step, 0)
     for m in range(NODES):
-        update(jnp.int32(last), m)
+        for side in range(2):
+            update(jnp.int32(last), m, side)
     for c in range(2):
         total = weight_ref[core * NODES] * mats[0][c]
         for m in range(1, NODES):
@@ -337,6 +341,7 @@
             pltpu.VMEM((2, 128, 128), F32),
             pltpu.VMEM((2 * 128, 128), F32),
             pltpu.VMEM((NODES, 2, STEP, 128), F32),
+            pltpu.VMEM((NODES, 2, 8 * STEP, 128), BF16),
         ]
         + [pltpu.VMEM((2, n, 128), F32)] * NODES,
         compiler_params=limit,

time: 56.2 us -> 56.2 us (level)
  no operation moved by 1% of the time
where the time goes in v7:
time: 56.2 us; the launch traced here: 56 us
  Pallas kernels  23.2 us (41%)
  blocking collectives  23 us (41%)
  waiting for transfers between devices  6.24 us (11%)
  starting transfers between devices  3.45 us (6%)
    all_to_all x2, blocking collectives, cube(): lax.all_to_all(pieces, ('gx', 'gy'), 0, 0, axis_index_groups=groups, tile...  23 us
    pallas_call x1, Pallas kernels, on_device(): pl.pallas_call(resolvent_kernel, out_shape=(square, square), in_specs=[sm...  17.3 us
    ppermute x3, waiting for transfers between devices, swap_cores(): return lax.ppermute(x, 'gz', [(0, 1), (1, 0)])  3.57 us
    pallas_call x1, Pallas kernels, on_device(): pl.pallas_call(gram_kernel, out_shape=(half, half), in_specs=[smem, hbm,...  3.52 us
    ppermute x1, waiting for transfers between devices, swap_bits(): return lax.ppermute(x, ('gx', 'gy', 'gz'), perm)  2.66 us
    ppermute x1, starting transfers between devices, swap_bits(): return lax.ppermute(x, ('gx', 'gy', 'gz'), perm)  2.65 us
    pallas_call x1, Pallas kernels, on_device(): pl.pallas_call(functools.partial(lift_kernel, float(np.sqrt(total_rows)))...  1.74 us
  transfers between devices with their start and end apart: 4, of which 4 were waited for; matrix products, arithmetic and copies ran while one was open for 0% of the time, Pallas kernels for 1%

profile of v7, /device:TPU:0, one launch (start us, length us, event | category | flops | bytes accessed | tf_op | source)
XLA Modules:
  0.0 56.0 jit_solution(17503833359381538603)
XLA Ops:
  0.0 3.5 %shard_map.46 = (f32[576,128]{1,0:T(8,128)S(1)}, f32[576,128]{1,0:T(8,128)S(1)}) custom-call(s32[1]{0:T(128)} %bitcast.where_ref, f32[1024,256]{1,0:T(8,128)} %b_ref.1, f32[1024,256]{1,0:T(8,128)} %t_ref.1), custom_call_target="tpu_custom_call" | custom-call | tf_op jit(solution)/shard_map/pallas_call | solution.py:317
  3.5 0.5 collective-permute-start
  4.1 1.2 %collective-permute-done = f32[576,128]{1,0:T(8,128)S(1)} collective-permute-done((f32[576,128]{1,0:T(8,128)S(1)}, f32[576,128]{1,0:T(8,128)S(1)}, u32[]{:S(2)}, u32[]{:S(2)}) %collective-permute-start) | collective-permute-done | bytes 294944 | tf_op jit(solution)/shard_map/ppermute | solution.py:274
  5.3 13.5 %all_to_all.17 = f32[8,72,128]{2,1,0:T(8,128)S(1)} all-to-all(f32[8,72,128]{2,1,0:T(8,128)S(1)} %bitcast.5), channel_id=1, replica_groups={{0,2,4,6,8,10,12,14},{16,18,20,22,24,26,28,30},{1,3,5,7,9,11,13,15},{17..., dimensions={0} | all-to-all | bytes 589824 | tf_op jit(solution)/shard_map/all_to_all | solution.py:294
  18.8 2.7 %collective-permute-start.1 = (f32[72,128]{1,0:T(8,128)S(1)}, f32[72,128]{1,0:T(8,128)S(1)}, u32[]{:S(2)}, u32[]{:S(2)}) collective-permute-start(f32[72,128]{1,0:T(8,128)S(1)} %reduce_sum.9), channel_id=1, source_target_pairs={{0,16},{1,17},{2,18},{3,19},{4,20},{5,21},{6,22},{7,23},{8,24},{9,... | collective-permute-start | bytes 110600 | tf_op jit(solution)/shard_map/ppermute | solution.py:283
  21.4 2.7 %collective-permute-done.1 = f32[72,128]{1,0:T(8,128)S(1)} collective-permute-done((f32[72,128]{1,0:T(8,128)S(1)}, f32[72,128]{1,0:T(8,128)S(1)}, u32[]{:S(2)}, u32[]{:S(2)}) %collective-permute-start.1) | collective-permute-done | bytes 36896 | tf_op jit(solution)/shard_map/ppermute | solution.py:283
  24.1 9.5 %all_to_all.18 = f32[8,72,128]{2,1,0:T(8,128)S(1)} all-to-all(f32[8,72,128]{2,1,0:T(8,128)S(1)} %tile.2), channel_id=1, replica_groups={{0,2,4,6,8,10,12,14},{16,18,20,22,24,26,28,30},{1,3,5,7,9,11,13,15},{17..., dimensions={0} | all-to-all | bytes 589824 | tf_op jit(solution)/shard_map/all_to_all | solution.py:294
  33.6 0.0 copy-start.2
  33.6 0.0 copy-start.3
  33.6 0.0 copy-start
  33.6 0.0 copy-start.1
  33.6 0.1 collective-permute-start.2
  33.7 1.6 %collective-permute-done.2.other_ref = f32[576,128]{1,0:T(8,128)S(1)} collective-permute-done((f32[576,128]{1,0:T(8,128)S(1)}, f32[576,128]{1,0:T(8,128)S(1)}, u32[]{:S(2)}, u32[]{:S(2)}) %collective-permute-start.2) | collective-permute-done | bytes 294944 | tf_op jit(solution)/shard_map/ppermute | solution.py:274
  35.3 0.0 copy-done.2
  35.3 0.0 copy-done.3
  35.3 17.3 %shard_map.47 = (f32[256,256]{1,0:T(8,128)S(1)}, f32[256,256]{1,0:T(8,128)S(1)}) custom-call(s32[1]{0:T(128)} %bitcast.where_ref, f32[16]{0:T(128)S(1)} %copy-done.3, f32[16]{0:T(128)S(1)} %copy-done.2, f32[576,128]{1,0:T(8,128)S(1)} %bitcast.4, f32[576,128]{1,0:T(8,128)S(1)} %collective-permute-done.2.other_ref), custom_call_target="tpu_custom_call" | custom-call | flops 99999997952 | bytes 1000000 | tf_op jit(solution)/shard_map/pallas_call | solution.py:333
  52.6 0.2 collective-permute-start.3
  52.8 0.0 copy-done
  52.8 0.0 copy-done.1
  52.8 0.6 %shard_map.48 = (bf16[1024,256]{1,0:T(8,128)(2,1)S(1)}, bf16[1024,256]{1,0:T(8,128)(2,1)S(1)}) custom-call(f32[256,256]{1,0:T(8,128)S(1)} %get-tuple-element.14.cross_ref, f32[1024,256]{1,0:T(8,128)S(1)} %copy-done, f32[1024,256]{1,0:T(8,128)S(1)} %copy-done.1), custom_call_target="tpu_custom_call" | custom-call | flops 1000000000 | bytes 3000000 | tf_op jit(solution)/shard_map/pallas_call | solution.py:351
  53.4 0.8 %collective-permute-done.3.other_ref = f32[256,256]{1,0:T(8,128)S(1)} collective-permute-done((f32[256,256]{1,0:T(8,128)S(1)}, f32[256,256]{1,0:T(8,128)S(1)}, u32[]{:S(2)}, u32[]{:S(2)}) %collective-permute-start.3) | collective-permute-done | bytes 262176 | tf_op jit(solution)/shard_map/ppermute | solution.py:274
  54.2 1.7 %shard_map.49 = f32[1024,256]{1,0:T(8,128)} custom-call(f32[256,256]{1,0:T(8,128)S(1)} %get-tuple-element.13.mine_ref, f32[256,256]{1,0:T(8,128)S(1)} %collective-permute-done.3.other_ref, f32[256,256]{1,0:T(8,128)S(1)} %get-tuple-element.14.cross_ref, bf16[1024,256]{1,0:T(8,128)(2,1)S(1)} %get-tuple-element.15.high_ref, ...), custom_call_target="tpu_custom_call" | custom-call | tf_op jit(solution)/shard_map/pallas_call | solution.py:359
  (4 shorter events, 0.1 us)
Async XLA Ops:
  3.5 1.7 %collective-permute-start = (f32[576,128]{1,0:T(8,128)S(1)}, f32[576,128]{1,0:T(8,128)S(1)}, u32[]{:S(2)}, u32[]{:S(2)}) collective-permute-start(f32[576,128]{1,0:T(8,128)S(1)} %get-tuple-element.12), channel_id=1, source_target_pairs={{0,1},{1,0},{2,3},{3,2},{4,5},{5,4},{6,7},{7,6},{8,9},{9,8},{10,11... | collective-permute-start | bytes 884744 | tf_op jit(solution)/shard_map/ppermute | solution.py:274
  18.8 5.3 %collective-permute-start.1 = (f32[72,128]{1,0:T(8,128)S(1)}, f32[72,128]{1,0:T(8,128)S(1)}, u32[]{:S(2)}, u32[]{:S(2)}) collective-permute-start(f32[72,128]{1,0:T(8,128)S(1)} %reduce_sum.9), channel_id=1, source_target_pairs={{0,16},{1,17},{2,18},{3,19},{4,20},{5,21},{6,22},{7,23},{8,24},{9,... | collective-permute-start | bytes 110600 | tf_op jit(solution)/shard_map/ppermute | solution.py:283
  33.6 1.7 %copy-start.2 = (f32[16]{0:T(128)S(1)}, f32[16]{0:T(128)}, u32[]{:S(2)}) copy-start(f32[16]{0:T(128)} %constant.11.clone.weight_ref) | copy-start | bytes 196
  33.6 1.7 %copy-start.3 = (f32[16]{0:T(128)S(1)}, f32[16]{0:T(128)}, u32[]{:S(2)}) copy-start(f32[16]{0:T(128)} %constant.10.clone.shift_ref) | copy-start | bytes 196
  33.6 19.2 %copy-start = (f32[1024,256]{1,0:T(8,128)S(1)}, f32[1024,256]{1,0:T(8,128)}, u32[]{:S(2)}) copy-start(f32[1024,256]{1,0:T(8,128)} %b_ref.1) | copy-start | bytes 3145732
  33.6 19.2 %copy-start.1 = (f32[1024,256]{1,0:T(8,128)S(1)}, f32[1024,256]{1,0:T(8,128)}, u32[]{:S(2)}) copy-start(f32[1024,256]{1,0:T(8,128)} %t_ref.1) | copy-start | bytes 3145732
  33.6 1.6 %collective-permute-start.2 = (f32[576,128]{1,0:T(8,128)S(1)}, f32[576,128]{1,0:T(8,128)S(1)}, u32[]{:S(2)}, u32[]{:S(2)}) collective-permute-start(f32[576,128]{1,0:T(8,128)S(1)} %bitcast.3), channel_id=1, source_target_pairs={{0,1},{1,0},{2,3},{3,2},{4,5},{5,4},{6,7},{7,6},{8,9},{9,8},{10,11... | collective-permute-start | bytes 884744 | tf_op jit(solution)/shard_map/ppermute | solution.py:274
  52.6 1.6 %collective-permute-start.3 = (f32[256,256]{1,0:T(8,128)S(1)}, f32[256,256]{1,0:T(8,128)S(1)}, u32[]{:S(2)}, u32[]{:S(2)}) collective-permute-start(f32[256,256]{1,0:T(8,128)S(1)} %get-tuple-element.13.mine_ref), channel_id=1, source_target_pairs={{0,1},{1,0},{2,3},{3,2},{4,5},{5,4},{6,7},{7,6},{8,9},{9,8},{10,11... | collective-permute-start | bytes 786440 | tf_op jit(solution)/shard_map/ppermute | solution.py:274

commit v8 on v5

--- a/solution.py
+++ b/solution.py
@@ -171,7 +171,15 @@
 
     def stack(x):
         h, m, l = split(x)
-        return jnp.concatenate([h, m, h, l, h, m, l, m], 0).astype(BF16)
+        return jnp.concatenate([h, m, h, l, h, m], 0).astype(BF16)
+
+    def spread(x, first):
+        lane = iota(x.shape, 1)
+        group = lane // STEP
+        h, d, l = split(jnp.take_along_axis(x, lane % STEP + first, axis=1))
+        one = jnp.where(group == 2, d, h).astype(BF16)
+        two = jnp.where(group == 0, l, d).astype(BF16)
+        return jnp.concatenate([one, two[:, : 2 * STEP]], 1)
 
     def step(tile, part, carry):
         inner = pl.multiple_of(part * STEP, STEP)
@@ -184,28 +192,21 @@
             v.append([block[8 * g : 8 * g + 8] for g in range(4)])
         v = invert_blocks(v)
         for q in range(2):
-            h, m, l = split(jnp.concatenate(v[q], 0))
-            inverses[0, q * 128 : (q + 1) * 128, :] = jnp.concatenate([h, h, m, h], 0).T
-            inverses[1, q * 128 : (q + 1) * 128, :] = jnp.concatenate([l, m, m, l], 0).T
+            inverses[q * 128 : (q + 1) * 128, 0:STEP] = jnp.concatenate(v[q], 0).T
 
         local = iota((STEP, n), 1) - start
         inblock = (local >= 0) & (local < STEP)
         minus = jnp.where(local == iota((STEP, n), 0), -1.0, 0.0)
         for m in range(NODES):
-            left = [inverses[c, pl.ds(m, STEP, stride=NODES), :] for c in range(2)]
-            left = jnp.concatenate(left, 1).astype(BF16)
+            left = spread(inverses[pl.ds(m, STEP, stride=NODES), :], 0)
             here = pl.ds(pl.multiple_of(m * n + start, STEP), STEP)
             panel = jnp.concatenate([mats[0, here, :], mats[1, here, :]], 1)
             panel = jnp.where(inblock, minus, panel)
             news[m] = jnp.dot(left, stack(panel), preferred_element_type=F32)
         for m in range(NODES):
             rows = slice(m * n, (m + 1) * n)
-            here = pl.ds(pl.multiple_of(m * n + start, STEP), STEP)
-            h, d, l = split(jnp.concatenate([mats[0, here, :], mats[1, here, :]], 1))
-            lhs = jnp.concatenate([h, h, d, h, l, d, d, l], 0).astype(BF16)
-            change = lax.dot_general(
-                lhs, stack(news[m]), (((0,), (0,)), ((), ())), preferred_element_type=F32
-            )
+            left = spread(mats[tile, rows, :], inner)
+            change = jnp.dot(left, stack(news[m]), preferred_element_type=F32)
             for c in range(2):
                 half = slice(c * 128, (c + 1) * 128)
                 old = mats[c, rows, :]
@@ -314,7 +315,7 @@
         scratch_shapes=[
             pltpu.VMEM((2, NODES * n, 128), F32),
             pltpu.VMEM((2, 128, 128), F32),
-            pltpu.VMEM((2, 2 * 128, 128), F32),
+            pltpu.VMEM((2 * 128, 128), F32),
             pltpu.VMEM((NODES, STEP, n), F32),
             pltpu.VMEM((2 * pay_half, 128), F32),
         ],

time: 67.7 us -> 57 us (0.84)
  Pallas kernels: 34.7 us -> 24 us
    pallas_call x1, Pallas kernels: 28.9 us -> 18.2 us  [on_device(): pl.pallas_call(resolvent_kernel, out_shape=(square, square), in_specs=[sm...]
where the time goes in v8:
time: 57 us; the launch traced here: 56.8 us
  Pallas kernels  24 us (42%)
  blocking collectives  23 us (40%)
  waiting for transfers between devices  6.24 us (11%)
  starting transfers between devices  3.44 us (6%)
    all_to_all x2, blocking collectives, cube(): lax.all_to_all(pieces, ('gx', 'gy'), 0, 0, axis_index_groups=groups, tile...  23 us
    pallas_call x1, Pallas kernels, on_device(): pl.pallas_call(resolvent_kernel, out_shape=(square, square), in_specs=[sm...  18.2 us
    ppermute x3, waiting for transfers between devices, swap_cores(): return lax.ppermute(x, 'gz', [(0, 1), (1, 0)])  3.58 us
    pallas_call x1, Pallas kernels, on_device(): pl.pallas_call(gram_kernel, out_shape=(half, half), in_specs=[smem, hbm,...  3.52 us
    ppermute x1, waiting for transfers between devices, swap_bits(): return lax.ppermute(x, ('gx', 'gy', 'gz'), perm)  2.66 us
    ppermute x1, starting transfers between devices, swap_bits(): return lax.ppermute(x, ('gx', 'gy', 'gz'), perm)  2.65 us
    pallas_call x1, Pallas kernels, on_device(): pl.pallas_call(functools.partial(lift_kernel, float(np.sqrt(total_rows)))...  1.74 us
  transfers between devices with their start and end apart: 4, of which 4 were waited for; matrix products, arithmetic and copies ran while one was open for 0% of the time, Pallas kernels for 1%

profile of v8, /device:TPU:0, one launch (start us, length us, event | category | flops | bytes accessed | tf_op | source)
XLA Modules:
  0.0 56.8 jit_solution(15083746210208484968)
XLA Ops:
  0.0 3.5 %shard_map.46 = (f32[576,128]{1,0:T(8,128)S(1)}, f32[576,128]{1,0:T(8,128)S(1)}) custom-call(s32[1]{0:T(128)} %bitcast.where_ref, f32[1024,256]{1,0:T(8,128)} %b_ref.1, f32[1024,256]{1,0:T(8,128)} %t_ref.1), custom_call_target="tpu_custom_call" | custom-call | tf_op jit(solution)/shard_map/pallas_call | solution.py:294
  3.5 0.5 collective-permute-start
  4.1 1.2 %collective-permute-done = f32[576,128]{1,0:T(8,128)S(1)} collective-permute-done((f32[576,128]{1,0:T(8,128)S(1)}, f32[576,128]{1,0:T(8,128)S(1)}, u32[]{:S(2)}, u32[]{:S(2)}) %collective-permute-start) | collective-permute-done | bytes 294944 | tf_op jit(solution)/shard_map/ppermute | solution.py:251
  5.3 13.5 %all_to_all.17 = f32[8,72,128]{2,1,0:T(8,128)S(1)} all-to-all(f32[8,72,128]{2,1,0:T(8,128)S(1)} %bitcast.5), channel_id=1, replica_groups={{0,2,4,6,8,10,12,14},{16,18,20,22,24,26,28,30},{1,3,5,7,9,11,13,15},{17..., dimensions={0} | all-to-all | bytes 589824 | tf_op jit(solution)/shard_map/all_to_all | solution.py:271
  18.8 2.7 %collective-permute-start.1 = (f32[72,128]{1,0:T(8,128)S(1)}, f32[72,128]{1,0:T(8,128)S(1)}, u32[]{:S(2)}, u32[]{:S(2)}) collective-permute-start(f32[72,128]{1,0:T(8,128)S(1)} %reduce_sum.9), channel_id=1, source_target_pairs={{0,16},{1,17},{2,18},{3,19},{4,20},{5,21},{6,22},{7,23},{8,24},{9,... | collective-permute-start | bytes 110600 | tf_op jit(solution)/shard_map/ppermute | solution.py:260
  21.4 2.7 %collective-permute-done.1 = f32[72,128]{1,0:T(8,128)S(1)} collective-permute-done((f32[72,128]{1,0:T(8,128)S(1)}, f32[72,128]{1,0:T(8,128)S(1)}, u32[]{:S(2)}, u32[]{:S(2)}) %collective-permute-start.1) | collective-permute-done | bytes 36896 | tf_op jit(solution)/shard_map/ppermute | solution.py:260
  24.1 9.5 %all_to_all.18 = f32[8,72,128]{2,1,0:T(8,128)S(1)} all-to-all(f32[8,72,128]{2,1,0:T(8,128)S(1)} %tile.2), channel_id=1, replica_groups={{0,2,4,6,8,10,12,14},{16,18,20,22,24,26,28,30},{1,3,5,7,9,11,13,15},{17..., dimensions={0} | all-to-all | bytes 589824 | tf_op jit(solution)/shard_map/all_to_all | solution.py:271
  33.6 0.0 copy-start.2
  33.6 0.0 copy-start.3
  33.6 0.0 copy-start
  33.6 0.0 copy-start.1
  33.6 0.1 collective-permute-start.2
  33.7 1.6 %collective-permute-done.2.other_ref = f32[576,128]{1,0:T(8,128)S(1)} collective-permute-done((f32[576,128]{1,0:T(8,128)S(1)}, f32[576,128]{1,0:T(8,128)S(1)}, u32[]{:S(2)}, u32[]{:S(2)}) %collective-permute-start.2) | collective-permute-done | bytes 294944 | tf_op jit(solution)/shard_map/ppermute | solution.py:251
  35.3 0.0 copy-done.2
  35.3 0.0 copy-done.3
  35.3 18.2 %shard_map.47 = (f32[256,256]{1,0:T(8,128)S(1)}, f32[256,256]{1,0:T(8,128)S(1)}) custom-call(s32[1]{0:T(128)} %bitcast.where_ref, f32[16]{0:T(128)S(1)} %copy-done.3, f32[16]{0:T(128)S(1)} %copy-done.2, f32[576,128]{1,0:T(8,128)S(1)} %bitcast.4, f32[576,128]{1,0:T(8,128)S(1)} %collective-permute-done.2.other_ref), custom_call_target="tpu_custom_call" | custom-call | flops 99999997952 | bytes 1000000 | tf_op jit(solution)/shard_map/pallas_call | solution.py:310
  53.5 0.2 collective-permute-start.3
  53.7 0.0 copy-done
  53.7 0.0 copy-done.1
  53.7 0.6 %shard_map.48 = (bf16[1024,256]{1,0:T(8,128)(2,1)S(1)}, bf16[1024,256]{1,0:T(8,128)(2,1)S(1)}) custom-call(f32[256,256]{1,0:T(8,128)S(1)} %get-tuple-element.14.cross_ref, f32[1024,256]{1,0:T(8,128)S(1)} %copy-done, f32[1024,256]{1,0:T(8,128)S(1)} %copy-done.1), custom_call_target="tpu_custom_call" | custom-call | flops 1000000000 | bytes 3000000 | tf_op jit(solution)/shard_map/pallas_call | solution.py:326
  54.3 0.8 %collective-permute-done.3.other_ref = f32[256,256]{1,0:T(8,128)S(1)} collective-permute-done((f32[256,256]{1,0:T(8,128)S(1)}, f32[256,256]{1,0:T(8,128)S(1)}, u32[]{:S(2)}, u32[]{:S(2)}) %collective-permute-start.3) | collective-permute-done | bytes 262176 | tf_op jit(solution)/shard_map/ppermute | solution.py:251
  55.1 1.7 %shard_map.49 = f32[1024,256]{1,0:T(8,128)} custom-call(f32[256,256]{1,0:T(8,128)S(1)} %get-tuple-element.13.mine_ref, f32[256,256]{1,0:T(8,128)S(1)} %collective-permute-done.3.other_ref, f32[256,256]{1,0:T(8,128)S(1)} %get-tuple-element.14.cross_ref, bf16[1024,256]{1,0:T(8,128)(2,1)S(1)} %get-tuple-element.15.high_ref, ...), custom_call_target="tpu_custom_call" | custom-call | tf_op jit(solution)/shard_map/pallas_call | solution.py:334
  (4 shorter events, 0.1 us)
Async XLA Ops:
  3.5 1.7 %collective-permute-start = (f32[576,128]{1,0:T(8,128)S(1)}, f32[576,128]{1,0:T(8,128)S(1)}, u32[]{:S(2)}, u32[]{:S(2)}) collective-permute-start(f32[576,128]{1,0:T(8,128)S(1)} %get-tuple-element.12), channel_id=1, source_target_pairs={{0,1},{1,0},{2,3},{3,2},{4,5},{5,4},{6,7},{7,6},{8,9},{9,8},{10,11... | collective-permute-start | bytes 884744 | tf_op jit(solution)/shard_map/ppermute | solution.py:251
  18.8 5.3 %collective-permute-start.1 = (f32[72,128]{1,0:T(8,128)S(1)}, f32[72,128]{1,0:T(8,128)S(1)}, u32[]{:S(2)}, u32[]{:S(2)}) collective-permute-start(f32[72,128]{1,0:T(8,128)S(1)} %reduce_sum.9), channel_id=1, source_target_pairs={{0,16},{1,17},{2,18},{3,19},{4,20},{5,21},{6,22},{7,23},{8,24},{9,... | collective-permute-start | bytes 110600 | tf_op jit(solution)/shard_map/ppermute | solution.py:260
  33.6 1.7 %copy-start.2 = (f32[16]{0:T(128)S(1)}, f32[16]{0:T(128)}, u32[]{:S(2)}) copy-start(f32[16]{0:T(128)} %constant.11.clone.weight_ref) | copy-start | bytes 196
  33.6 1.7 %copy-start.3 = (f32[16]{0:T(128)S(1)}, f32[16]{0:T(128)}, u32[]{:S(2)}) copy-start(f32[16]{0:T(128)} %constant.10.clone.shift_ref) | copy-start | bytes 196
  33.6 20.0 %copy-start = (f32[1024,256]{1,0:T(8,128)S(1)}, f32[1024,256]{1,0:T(8,128)}, u32[]{:S(2)}) copy-start(f32[1024,256]{1,0:T(8,128)} %b_ref.1) | copy-start | bytes 3145732
  33.6 20.0 %copy-start.1 = (f32[1024,256]{1,0:T(8,128)S(1)}, f32[1024,256]{1,0:T(8,128)}, u32[]{:S(2)}) copy-start(f32[1024,256]{1,0:T(8,128)} %t_ref.1) | copy-start | bytes 3145732
  33.6 1.6 %collective-permute-start.2 = (f32[576,128]{1,0:T(8,128)S(1)}, f32[576,128]{1,0:T(8,128)S(1)}, u32[]{:S(2)}, u32[]{:S(2)}) collective-permute-start(f32[576,128]{1,0:T(8,128)S(1)} %bitcast.3), channel_id=1, source_target_pairs={{0,1},{1,0},{2,3},{3,2},{4,5},{5,4},{6,7},{7,6},{8,9},{9,8},{10,11... | collective-permute-start | bytes 884744 | tf_op jit(solution)/shard_map/ppermute | solution.py:251
  53.5 1.6 %collective-permute-start.3 = (f32[256,256]{1,0:T(8,128)S(1)}, f32[256,256]{1,0:T(8,128)S(1)}, u32[]{:S(2)}, u32[]{:S(2)}) collective-permute-start(f32[256,256]{1,0:T(8,128)S(1)} %get-tuple-element.13.mine_ref), channel_id=1, source_target_pairs={{0,1},{1,0},{2,3},{3,2},{4,5},{5,4},{6,7},{7,6},{8,9},{9,8},{10,11... | collective-permute-start | bytes 786440 | tf_op jit(solution)/shard_map/ppermute | solution.py:251

commit v9 on v5

--- a/solution.py
+++ b/solution.py
@@ -116,9 +116,7 @@
             index = node + (first + p) * NODES
             pan.append([jnp.take_along_axis(x, index, axis=1) for x in v[q]])
         for p in range(8):
-            pivot = pan[p][g][p : p + 1, :]
-            recip = pl.reciprocal(pivot, approx=True)
-            recip = recip * (2.0 - pivot * recip)
+            recip = 1.0 / pan[p][g][p : p + 1, :]
             new = [x for x in pan[p]]
             new[g] = jnp.where(row == p, 1.0, new[g])
             new = [x * recip for x in new]
@@ -188,6 +186,8 @@
             inverses[0, q * 128 : (q + 1) * 128, :] = jnp.concatenate([h, h, m, h], 0).T
             inverses[1, q * 128 : (q + 1) * 128, :] = jnp.concatenate([l, m, m, l], 0).T
 
+        group = iota((n, 128), 1) // STEP
+        index = iota((n, 128), 1) % STEP + inner
         local = iota((STEP, n), 1) - start
         inblock = (local >= 0) & (local < STEP)
         minus = jnp.where(local == iota((STEP, n), 0), -1.0, 0.0)
@@ -200,12 +200,12 @@
             news[m] = jnp.dot(left, stack(panel), preferred_element_type=F32)
         for m in range(NODES):
             rows = slice(m * n, (m + 1) * n)
-            here = pl.ds(pl.multiple_of(m * n + start, STEP), STEP)
-            h, d, l = split(jnp.concatenate([mats[0, here, :], mats[1, here, :]], 1))
-            lhs = jnp.concatenate([h, h, d, h, l, d, d, l], 0).astype(BF16)
-            change = lax.dot_general(
-                lhs, stack(news[m]), (((0,), (0,)), ((), ())), preferred_element_type=F32
-            )
+            columns = jnp.take_along_axis(mats[tile, rows, :], index, axis=1)
+            h, d, l = split(columns)
+            one = jnp.where(group == 2, d, h)
+            two = jnp.where((group == 0) | (group == 3), l, d)
+            lhs = jnp.concatenate([one, two], 1).astype(BF16)
+            change = jnp.dot(lhs, stack(news[m]), preferred_element_type=F32)
             for c in range(2):
                 half = slice(c * 128, (c + 1) * 128)
                 old = mats[c, rows, :]

time: 67.7 us -> 55.2 us (0.82)
  Pallas kernels: 34.7 us -> 22.2 us
    pallas_call x1, Pallas kernels: 28.9 us -> 16.3 us  [on_device(): pl.pallas_call(resolvent_kernel, out_shape=(square, square), in_specs=[sm...]
where the time goes in v9:
time: 55.2 us; the launch traced here: 55 us
  blocking collectives  23 us (42%)
  Pallas kernels  22.2 us (40%)
  waiting for transfers between devices  6.23 us (11%)
  starting transfers between devices  3.45 us (6%)
    all_to_all x2, blocking collectives, cube(): lax.all_to_all(pieces, ('gx', 'gy'), 0, 0, axis_index_groups=groups, tile...  23 us
    pallas_call x1, Pallas kernels, on_device(): pl.pallas_call(resolvent_kernel, out_shape=(square, square), in_specs=[sm...  16.3 us
    ppermute x3, waiting for transfers between devices, swap_cores(): return lax.ppermute(x, 'gz', [(0, 1), (1, 0)])  3.57 us
    pallas_call x1, Pallas kernels, on_device(): pl.pallas_call(gram_kernel, out_shape=(half, half), in_specs=[smem, hbm,...  3.52 us
    ppermute x1, waiting for transfers between devices, swap_bits(): return lax.ppermute(x, ('gx', 'gy', 'gz'), perm)  2.66 us
    ppermute x1, starting transfers between devices, swap_bits(): return lax.ppermute(x, ('gx', 'gy', 'gz'), perm)  2.65 us
    pallas_call x1, Pallas kernels, on_device(): pl.pallas_call(functools.partial(lift_kernel, float(np.sqrt(total_rows)))...  1.74 us
  transfers between devices with their start and end apart: 4, of which 4 were waited for; matrix products, arithmetic and copies ran while one was open for 0% of the time, Pallas kernels for 1%

profile of v9, /device:TPU:0, one launch (start us, length us, event | category | flops | bytes accessed | tf_op | source)
XLA Modules:
  0.0 55.0 jit_solution(7144684493395186827)
XLA Ops:
  0.0 3.5 %shard_map.46 = (f32[576,128]{1,0:T(8,128)S(1)}, f32[576,128]{1,0:T(8,128)S(1)}) custom-call(s32[1]{0:T(128)} %bitcast.where_ref, f32[1024,256]{1,0:T(8,128)} %b_ref.1, f32[1024,256]{1,0:T(8,128)} %t_ref.1), custom_call_target="tpu_custom_call" | custom-call | tf_op jit(solution)/shard_map/pallas_call | solution.py:293
  3.5 0.5 collective-permute-start
  4.1 1.2 %collective-permute-done = f32[576,128]{1,0:T(8,128)S(1)} collective-permute-done((f32[576,128]{1,0:T(8,128)S(1)}, f32[576,128]{1,0:T(8,128)S(1)}, u32[]{:S(2)}, u32[]{:S(2)}) %collective-permute-start) | collective-permute-done | bytes 294944 | tf_op jit(solution)/shard_map/ppermute | solution.py:250
  5.3 13.5 %all_to_all.17 = f32[8,72,128]{2,1,0:T(8,128)S(1)} all-to-all(f32[8,72,128]{2,1,0:T(8,128)S(1)} %bitcast.5), channel_id=1, replica_groups={{0,2,4,6,8,10,12,14},{16,18,20,22,24,26,28,30},{1,3,5,7,9,11,13,15},{17..., dimensions={0} | all-to-all | bytes 589824 | tf_op jit(solution)/shard_map/all_to_all | solution.py:270
  18.8 2.7 %collective-permute-start.1 = (f32[72,128]{1,0:T(8,128)S(1)}, f32[72,128]{1,0:T(8,128)S(1)}, u32[]{:S(2)}, u32[]{:S(2)}) collective-permute-start(f32[72,128]{1,0:T(8,128)S(1)} %reduce_sum.9), channel_id=1, source_target_pairs={{0,16},{1,17},{2,18},{3,19},{4,20},{5,21},{6,22},{7,23},{8,24},{9,... | collective-permute-start | bytes 110600 | tf_op jit(solution)/shard_map/ppermute | solution.py:259
  21.4 2.7 %collective-permute-done.1 = f32[72,128]{1,0:T(8,128)S(1)} collective-permute-done((f32[72,128]{1,0:T(8,128)S(1)}, f32[72,128]{1,0:T(8,128)S(1)}, u32[]{:S(2)}, u32[]{:S(2)}) %collective-permute-start.1) | collective-permute-done | bytes 36896 | tf_op jit(solution)/shard_map/ppermute | solution.py:259
  24.1 9.5 %all_to_all.18 = f32[8,72,128]{2,1,0:T(8,128)S(1)} all-to-all(f32[8,72,128]{2,1,0:T(8,128)S(1)} %tile.2), channel_id=1, replica_groups={{0,2,4,6,8,10,12,14},{16,18,20,22,24,26,28,30},{1,3,5,7,9,11,13,15},{17..., dimensions={0} | all-to-all | bytes 589824 | tf_op jit(solution)/shard_map/all_to_all | solution.py:270
  33.6 0.0 copy-start.2
  33.6 0.0 copy-start.3
  33.6 0.0 copy-start
  33.6 0.0 copy-start.1
  33.6 0.1 collective-permute-start.2
  33.7 1.6 %collective-permute-done.2.other_ref = f32[576,128]{1,0:T(8,128)S(1)} collective-permute-done((f32[576,128]{1,0:T(8,128)S(1)}, f32[576,128]{1,0:T(8,128)S(1)}, u32[]{:S(2)}, u32[]{:S(2)}) %collective-permute-start.2) | collective-permute-done | bytes 294944 | tf_op jit(solution)/shard_map/ppermute | solution.py:250
  35.3 0.0 copy-done.2
  35.3 0.0 copy-done.3
  35.3 16.3 %shard_map.47 = (f32[256,256]{1,0:T(8,128)S(1)}, f32[256,256]{1,0:T(8,128)S(1)}) custom-call(s32[1]{0:T(128)} %bitcast.where_ref, f32[16]{0:T(128)S(1)} %copy-done.3, f32[16]{0:T(128)S(1)} %copy-done.2, f32[576,128]{1,0:T(8,128)S(1)} %bitcast.4, f32[576,128]{1,0:T(8,128)S(1)} %collective-permute-done.2.other_ref), custom_call_target="tpu_custom_call" | custom-call | flops 99999997952 | bytes 1000000 | tf_op jit(solution)/shard_map/pallas_call | solution.py:309
  51.6 0.2 collective-permute-start.3
  51.8 0.0 copy-done
  51.9 0.0 copy-done.1
  51.9 0.6 %shard_map.48 = (bf16[1024,256]{1,0:T(8,128)(2,1)S(1)}, bf16[1024,256]{1,0:T(8,128)(2,1)S(1)}) custom-call(f32[256,256]{1,0:T(8,128)S(1)} %get-tuple-element.14.cross_ref, f32[1024,256]{1,0:T(8,128)S(1)} %copy-done, f32[1024,256]{1,0:T(8,128)S(1)} %copy-done.1), custom_call_target="tpu_custom_call" | custom-call | flops 1000000000 | bytes 3000000 | tf_op jit(solution)/shard_map/pallas_call | solution.py:325
  52.5 0.8 %collective-permute-done.3.other_ref = f32[256,256]{1,0:T(8,128)S(1)} collective-permute-done((f32[256,256]{1,0:T(8,128)S(1)}, f32[256,256]{1,0:T(8,128)S(1)}, u32[]{:S(2)}, u32[]{:S(2)}) %collective-permute-start.3) | collective-permute-done | bytes 262176 | tf_op jit(solution)/shard_map/ppermute | solution.py:250
  53.2 1.7 %shard_map.49 = f32[1024,256]{1,0:T(8,128)} custom-call(f32[256,256]{1,0:T(8,128)S(1)} %get-tuple-element.13.mine_ref, f32[256,256]{1,0:T(8,128)S(1)} %collective-permute-done.3.other_ref, f32[256,256]{1,0:T(8,128)S(1)} %get-tuple-element.14.cross_ref, bf16[1024,256]{1,0:T(8,128)(2,1)S(1)} %get-tuple-element.15.high_ref, ...), custom_call_target="tpu_custom_call" | custom-call | tf_op jit(solution)/shard_map/pallas_call | solution.py:333
  (4 shorter events, 0.1 us)
Async XLA Ops:
  3.5 1.7 %collective-permute-start = (f32[576,128]{1,0:T(8,128)S(1)}, f32[576,128]{1,0:T(8,128)S(1)}, u32[]{:S(2)}, u32[]{:S(2)}) collective-permute-start(f32[576,128]{1,0:T(8,128)S(1)} %get-tuple-element.12), channel_id=1, source_target_pairs={{0,1},{1,0},{2,3},{3,2},{4,5},{5,4},{6,7},{7,6},{8,9},{9,8},{10,11... | collective-permute-start | bytes 884744 | tf_op jit(solution)/shard_map/ppermute | solution.py:250
  18.8 5.3 %collective-permute-start.1 = (f32[72,128]{1,0:T(8,128)S(1)}, f32[72,128]{1,0:T(8,128)S(1)}, u32[]{:S(2)}, u32[]{:S(2)}) collective-permute-start(f32[72,128]{1,0:T(8,128)S(1)} %reduce_sum.9), channel_id=1, source_target_pairs={{0,16},{1,17},{2,18},{3,19},{4,20},{5,21},{6,22},{7,23},{8,24},{9,... | collective-permute-start | bytes 110600 | tf_op jit(solution)/shard_map/ppermute | solution.py:259
  33.6 1.7 %copy-start.2 = (f32[16]{0:T(128)S(1)}, f32[16]{0:T(128)}, u32[]{:S(2)}) copy-start(f32[16]{0:T(128)} %constant.11.clone.weight_ref) | copy-start | bytes 196
  33.6 1.7 %copy-start.3 = (f32[16]{0:T(128)S(1)}, f32[16]{0:T(128)}, u32[]{:S(2)}) copy-start(f32[16]{0:T(128)} %constant.10.clone.shift_ref) | copy-start | bytes 196
  33.6 18.2 %copy-start = (f32[1024,256]{1,0:T(8,128)S(1)}, f32[1024,256]{1,0:T(8,128)}, u32[]{:S(2)}) copy-start(f32[1024,256]{1,0:T(8,128)} %b_ref.1) | copy-start | bytes 3145732
  33.6 18.2 %copy-start.1 = (f32[1024,256]{1,0:T(8,128)S(1)}, f32[1024,256]{1,0:T(8,128)}, u32[]{:S(2)}) copy-start(f32[1024,256]{1,0:T(8,128)} %t_ref.1) | copy-start | bytes 3145732
  33.6 1.6 %collective-permute-start.2 = (f32[576,128]{1,0:T(8,128)S(1)}, f32[576,128]{1,0:T(8,128)S(1)}, u32[]{:S(2)}, u32[]{:S(2)}) collective-permute-start(f32[576,128]{1,0:T(8,128)S(1)} %bitcast.3), channel_id=1, source_target_pairs={{0,1},{1,0},{2,3},{3,2},{4,5},{5,4},{6,7},{7,6},{8,9},{9,8},{10,11... | collective-permute-start | bytes 884744 | tf_op jit(solution)/shard_map/ppermute | solution.py:250
  51.6 1.6 %collective-permute-start.3 = (f32[256,256]{1,0:T(8,128)S(1)}, f32[256,256]{1,0:T(8,128)S(1)}, u32[]{:S(2)}, u32[]{:S(2)}) collective-permute-start(f32[256,256]{1,0:T(8,128)S(1)} %get-tuple-element.13.mine_ref), channel_id=1, source_target_pairs={{0,1},{1,0},{2,3},{3,2},{4,5},{5,4},{6,7},{7,6},{8,9},{9,8},{10,11... | collective-permute-start | bytes 786440 | tf_op jit(solution)/shard_map/ppermute | solution.py:250

commit v10 on v9

--- a/solution.py
+++ b/solution.py
@@ -116,7 +116,9 @@
             index = node + (first + p) * NODES
             pan.append([jnp.take_along_axis(x, index, axis=1) for x in v[q]])
         for p in range(8):
-            recip = 1.0 / pan[p][g][p : p + 1, :]
+            pivot = pan[p][g][p : p + 1, :]
+            recip = pl.reciprocal(pivot, approx=True)
+            recip = recip * (2.0 - pivot * recip)
             new = [x for x in pan[p]]
             new[g] = jnp.where(row == p, 1.0, new[g])
             new = [x * recip for x in new]

time: 55.2 us -> 56.7 us (1.027)
  Pallas kernels: 22.2 us -> 23.7 us
    pallas_call x1, Pallas kernels: 16.3 us -> 17.9 us  [on_device(): pl.pallas_call(resolvent_kernel, out_shape=(square, square), in_specs=[sm...]
where the time goes in v10:
time: 56.7 us; the launch traced here: 56.5 us
  Pallas kernels  23.7 us (42%)
  blocking collectives  23 us (41%)
  waiting for transfers between devices  6.24 us (11%)
  starting transfers between devices  3.45 us (6%)
    all_to_all x2, blocking collectives, cube(): lax.all_to_all(pieces, ('gx', 'gy'), 0, 0, axis_index_groups=groups, tile...  23 us
    pallas_call x1, Pallas kernels, on_device(): pl.pallas_call(resolvent_kernel, out_shape=(square, square), in_specs=[sm...  17.9 us
    ppermute x3, waiting for transfers between devices, swap_cores(): return lax.ppermute(x, 'gz', [(0, 1), (1, 0)])  3.58 us
    pallas_call x1, Pallas kernels, on_device(): pl.pallas_call(gram_kernel, out_shape=(half, half), in_specs=[smem, hbm,...  3.52 us
    ppermute x1, waiting for transfers between devices, swap_bits(): return lax.ppermute(x, ('gx', 'gy', 'gz'), perm)  2.66 us
    ppermute x1, starting transfers between devices, swap_bits(): return lax.ppermute(x, ('gx', 'gy', 'gz'), perm)  2.65 us
    pallas_call x1, Pallas kernels, on_device(): pl.pallas_call(functools.partial(lift_kernel, float(np.sqrt(total_rows)))...  1.74 us
  transfers between devices with their start and end apart: 4, of which 4 were waited for; matrix products, arithmetic and copies ran while one was open for 0% of the time, Pallas kernels for 1%

profile of v10, /device:TPU:0, one launch (start us, length us, event | category | flops | bytes accessed | tf_op | source)
XLA Modules:
  0.0 56.5 jit_solution(1065037152108067748)
XLA Ops:
  0.0 3.5 %shard_map.46 = (f32[576,128]{1,0:T(8,128)S(1)}, f32[576,128]{1,0:T(8,128)S(1)}) custom-call(s32[1]{0:T(128)} %bitcast.where_ref, f32[1024,256]{1,0:T(8,128)} %b_ref.1, f32[1024,256]{1,0:T(8,128)} %t_ref.1), custom_call_target="tpu_custom_call" | custom-call | tf_op jit(solution)/shard_map/pallas_call | solution.py:295
  3.5 0.5 collective-permute-start
  4.1 1.2 %collective-permute-done = f32[576,128]{1,0:T(8,128)S(1)} collective-permute-done((f32[576,128]{1,0:T(8,128)S(1)}, f32[576,128]{1,0:T(8,128)S(1)}, u32[]{:S(2)}, u32[]{:S(2)}) %collective-permute-start) | collective-permute-done | bytes 294944 | tf_op jit(solution)/shard_map/ppermute | solution.py:252
  5.3 13.5 %all_to_all.17 = f32[8,72,128]{2,1,0:T(8,128)S(1)} all-to-all(f32[8,72,128]{2,1,0:T(8,128)S(1)} %bitcast.5), channel_id=1, replica_groups={{0,2,4,6,8,10,12,14},{16,18,20,22,24,26,28,30},{1,3,5,7,9,11,13,15},{17..., dimensions={0} | all-to-all | bytes 589824 | tf_op jit(solution)/shard_map/all_to_all | solution.py:272
  18.8 2.7 %collective-permute-start.1 = (f32[72,128]{1,0:T(8,128)S(1)}, f32[72,128]{1,0:T(8,128)S(1)}, u32[]{:S(2)}, u32[]{:S(2)}) collective-permute-start(f32[72,128]{1,0:T(8,128)S(1)} %reduce_sum.9), channel_id=1, source_target_pairs={{0,16},{1,17},{2,18},{3,19},{4,20},{5,21},{6,22},{7,23},{8,24},{9,... | collective-permute-start | bytes 110600 | tf_op jit(solution)/shard_map/ppermute | solution.py:261
  21.4 2.7 %collective-permute-done.1 = f32[72,128]{1,0:T(8,128)S(1)} collective-permute-done((f32[72,128]{1,0:T(8,128)S(1)}, f32[72,128]{1,0:T(8,128)S(1)}, u32[]{:S(2)}, u32[]{:S(2)}) %collective-permute-start.1) | collective-permute-done | bytes 36896 | tf_op jit(solution)/shard_map/ppermute | solution.py:261
  24.1 9.5 %all_to_all.18 = f32[8,72,128]{2,1,0:T(8,128)S(1)} all-to-all(f32[8,72,128]{2,1,0:T(8,128)S(1)} %tile.2), channel_id=1, replica_groups={{0,2,4,6,8,10,12,14},{16,18,20,22,24,26,28,30},{1,3,5,7,9,11,13,15},{17..., dimensions={0} | all-to-all | bytes 589824 | tf_op jit(solution)/shard_map/all_to_all | solution.py:272
  33.6 0.0 copy-start.2
  33.6 0.0 copy-start.3
  33.6 0.0 copy-start
  33.6 0.0 copy-start.1
  33.6 0.1 collective-permute-start.2
  33.7 1.6 %collective-permute-done.2.other_ref = f32[576,128]{1,0:T(8,128)S(1)} collective-permute-done((f32[576,128]{1,0:T(8,128)S(1)}, f32[576,128]{1,0:T(8,128)S(1)}, u32[]{:S(2)}, u32[]{:S(2)}) %collective-permute-start.2) | collective-permute-done | bytes 294944 | tf_op jit(solution)/shard_map/ppermute | solution.py:252
  35.3 0.0 copy-done.2
  35.3 0.0 copy-done.3
  35.3 17.9 %shard_map.47 = (f32[256,256]{1,0:T(8,128)S(1)}, f32[256,256]{1,0:T(8,128)S(1)}) custom-call(s32[1]{0:T(128)} %bitcast.where_ref, f32[16]{0:T(128)S(1)} %copy-done.3, f32[16]{0:T(128)S(1)} %copy-done.2, f32[576,128]{1,0:T(8,128)S(1)} %bitcast.4, f32[576,128]{1,0:T(8,128)S(1)} %collective-permute-done.2.other_ref), custom_call_target="tpu_custom_call" | custom-call | flops 99999997952 | bytes 1000000 | tf_op jit(solution)/shard_map/pallas_call | solution.py:311
  53.2 0.2 collective-permute-start.3
  53.4 0.0 copy-done
  53.4 0.0 copy-done.1
  53.4 0.6 %shard_map.48 = (bf16[1024,256]{1,0:T(8,128)(2,1)S(1)}, bf16[1024,256]{1,0:T(8,128)(2,1)S(1)}) custom-call(f32[256,256]{1,0:T(8,128)S(1)} %get-tuple-element.14.cross_ref, f32[1024,256]{1,0:T(8,128)S(1)} %copy-done, f32[1024,256]{1,0:T(8,128)S(1)} %copy-done.1), custom_call_target="tpu_custom_call" | custom-call | flops 1000000000 | bytes 3000000 | tf_op jit(solution)/shard_map/pallas_call | solution.py:327
  54.0 0.8 %collective-permute-done.3.other_ref = f32[256,256]{1,0:T(8,128)S(1)} collective-permute-done((f32[256,256]{1,0:T(8,128)S(1)}, f32[256,256]{1,0:T(8,128)S(1)}, u32[]{:S(2)}, u32[]{:S(2)}) %collective-permute-start.3) | collective-permute-done | bytes 262176 | tf_op jit(solution)/shard_map/ppermute | solution.py:252
  54.8 1.7 %shard_map.49 = f32[1024,256]{1,0:T(8,128)} custom-call(f32[256,256]{1,0:T(8,128)S(1)} %get-tuple-element.13.mine_ref, f32[256,256]{1,0:T(8,128)S(1)} %collective-permute-done.3.other_ref, f32[256,256]{1,0:T(8,128)S(1)} %get-tuple-element.14.cross_ref, bf16[1024,256]{1,0:T(8,128)(2,1)S(1)} %get-tuple-element.15.high_ref, ...), custom_call_target="tpu_custom_call" | custom-call | tf_op jit(solution)/shard_map/pallas_call | solution.py:335
  (4 shorter events, 0.1 us)
Async XLA Ops:
  3.5 1.7 %collective-permute-start = (f32[576,128]{1,0:T(8,128)S(1)}, f32[576,128]{1,0:T(8,128)S(1)}, u32[]{:S(2)}, u32[]{:S(2)}) collective-permute-start(f32[576,128]{1,0:T(8,128)S(1)} %get-tuple-element.12), channel_id=1, source_target_pairs={{0,1},{1,0},{2,3},{3,2},{4,5},{5,4},{6,7},{7,6},{8,9},{9,8},{10,11... | collective-permute-start | bytes 884744 | tf_op jit(solution)/shard_map/ppermute | solution.py:252
  18.8 5.3 %collective-permute-start.1 = (f32[72,128]{1,0:T(8,128)S(1)}, f32[72,128]{1,0:T(8,128)S(1)}, u32[]{:S(2)}, u32[]{:S(2)}) collective-permute-start(f32[72,128]{1,0:T(8,128)S(1)} %reduce_sum.9), channel_id=1, source_target_pairs={{0,16},{1,17},{2,18},{3,19},{4,20},{5,21},{6,22},{7,23},{8,24},{9,... | collective-permute-start | bytes 110600 | tf_op jit(solution)/shard_map/ppermute | solution.py:261
  33.6 1.7 %copy-start.2 = (f32[16]{0:T(128)S(1)}, f32[16]{0:T(128)}, u32[]{:S(2)}) copy-start(f32[16]{0:T(128)} %constant.11.clone.weight_ref) | copy-start | bytes 196
  33.6 1.7 %copy-start.3 = (f32[16]{0:T(128)S(1)}, f32[16]{0:T(128)}, u32[]{:S(2)}) copy-start(f32[16]{0:T(128)} %constant.10.clone.shift_ref) | copy-start | bytes 196
  33.6 19.7 %copy-start = (f32[1024,256]{1,0:T(8,128)S(1)}, f32[1024,256]{1,0:T(8,128)}, u32[]{:S(2)}) copy-start(f32[1024,256]{1,0:T(8,128)} %b_ref.1) | copy-start | bytes 3145732
  33.6 19.7 %copy-start.1 = (f32[1024,256]{1,0:T(8,128)S(1)}, f32[1024,256]{1,0:T(8,128)}, u32[]{:S(2)}) copy-start(f32[1024,256]{1,0:T(8,128)} %t_ref.1) | copy-start | bytes 3145732
  33.6 1.6 %collective-permute-start.2 = (f32[576,128]{1,0:T(8,128)S(1)}, f32[576,128]{1,0:T(8,128)S(1)}, u32[]{:S(2)}, u32[]{:S(2)}) collective-permute-start(f32[576,128]{1,0:T(8,128)S(1)} %bitcast.3), channel_id=1, source_target_pairs={{0,1},{1,0},{2,3},{3,2},{4,5},{5,4},{6,7},{7,6},{8,9},{9,8},{10,11... | collective-permute-start | bytes 884744 | tf_op jit(solution)/shard_map/ppermute | solution.py:252
  53.2 1.6 %collective-permute-start.3 = (f32[256,256]{1,0:T(8,128)S(1)}, f32[256,256]{1,0:T(8,128)S(1)}, u32[]{:S(2)}, u32[]{:S(2)}) collective-permute-start(f32[256,256]{1,0:T(8,128)S(1)} %get-tuple-element.13.mine_ref), channel_id=1, source_target_pairs={{0,1},{1,0},{2,3},{3,2},{4,5},{5,4},{6,7},{7,6},{8,9},{9,8},{10,11... | collective-permute-start | bytes 786440 | tf_op jit(solution)/shard_map/ppermute | solution.py:252

commit v11 on v7

--- a/solution.py
+++ b/solution.py
@@ -116,9 +116,7 @@
             index = node + (first + p) * NODES
             pan.append([jnp.take_along_axis(x, index, axis=1) for x in v[q]])
         for p in range(8):
-            pivot = pan[p][g][p : p + 1, :]
-            recip = pl.reciprocal(pivot, approx=True)
-            recip = recip * (2.0 - pivot * recip)
+            recip = 1.0 / pan[p][g][p : p + 1, :]
             new = [x for x in pan[p]]
             new[g] = jnp.where(row == p, 1.0, new[g])
             new = [x * recip for x in new]

time: 56.2 us -> 55.6 us (0.989)
  Pallas kernels: 23.2 us -> 22.6 us
    pallas_call x1, Pallas kernels: 17.3 us -> 16.7 us  [on_device(): pl.pallas_call(resolvent_kernel, out_shape=(square, square), in_specs=[sm...]
where the time goes in v11:
time: 55.6 us; the launch traced here: 55.4 us
  blocking collectives  23 us (41%)
  Pallas kernels  22.6 us (41%)
  waiting for transfers between devices  6.24 us (11%)
  starting transfers between devices  3.45 us (6%)
    all_to_all x2, blocking collectives, cube(): lax.all_to_all(pieces, ('gx', 'gy'), 0, 0, axis_index_groups=groups, tile...  23 us
    pallas_call x1, Pallas kernels, on_device(): pl.pallas_call(resolvent_kernel, out_shape=(square, square), in_specs=[sm...  16.7 us
    ppermute x3, waiting for transfers between devices, swap_cores(): return lax.ppermute(x, 'gz', [(0, 1), (1, 0)])  3.58 us
    pallas_call x1, Pallas kernels, on_device(): pl.pallas_call(gram_kernel, out_shape=(half, half), in_specs=[smem, hbm,...  3.52 us
    ppermute x1, waiting for transfers between devices, swap_bits(): return lax.ppermute(x, ('gx', 'gy', 'gz'), perm)  2.66 us
    ppermute x1, starting transfers between devices, swap_bits(): return lax.ppermute(x, ('gx', 'gy', 'gz'), perm)  2.65 us
    pallas_call x1, Pallas kernels, on_device(): pl.pallas_call(functools.partial(lift_kernel, float(np.sqrt(total_rows)))...  1.74 us
  transfers between devices with their start and end apart: 4, of which 4 were waited for; matrix products, arithmetic and copies ran while one was open for 0% of the time, Pallas kernels for 1%

profile of v11, /device:TPU:0, one launch (start us, length us, event | category | flops | bytes accessed | tf_op | source)
XLA Modules:
  0.0 55.4 jit_solution(8658449402593444919)
XLA Ops:
  0.0 3.5 %shard_map.46 = (f32[576,128]{1,0:T(8,128)S(1)}, f32[576,128]{1,0:T(8,128)S(1)}) custom-call(s32[1]{0:T(128)} %bitcast.where_ref, f32[1024,256]{1,0:T(8,128)} %b_ref.1, f32[1024,256]{1,0:T(8,128)} %t_ref.1), custom_call_target="tpu_custom_call" | custom-call | tf_op jit(solution)/shard_map/pallas_call | solution.py:315
  3.5 0.5 collective-permute-start
  4.1 1.2 %collective-permute-done = f32[576,128]{1,0:T(8,128)S(1)} collective-permute-done((f32[576,128]{1,0:T(8,128)S(1)}, f32[576,128]{1,0:T(8,128)S(1)}, u32[]{:S(2)}, u32[]{:S(2)}) %collective-permute-start) | collective-permute-done | bytes 294944 | tf_op jit(solution)/shard_map/ppermute | solution.py:272
  5.3 13.5 %all_to_all.17 = f32[8,72,128]{2,1,0:T(8,128)S(1)} all-to-all(f32[8,72,128]{2,1,0:T(8,128)S(1)} %bitcast.5), channel_id=1, replica_groups={{0,2,4,6,8,10,12,14},{16,18,20,22,24,26,28,30},{1,3,5,7,9,11,13,15},{17..., dimensions={0} | all-to-all | bytes 589824 | tf_op jit(solution)/shard_map/all_to_all | solution.py:292
  18.8 2.7 %collective-permute-start.1 = (f32[72,128]{1,0:T(8,128)S(1)}, f32[72,128]{1,0:T(8,128)S(1)}, u32[]{:S(2)}, u32[]{:S(2)}) collective-permute-start(f32[72,128]{1,0:T(8,128)S(1)} %reduce_sum.9), channel_id=1, source_target_pairs={{0,16},{1,17},{2,18},{3,19},{4,20},{5,21},{6,22},{7,23},{8,24},{9,... | collective-permute-start | bytes 110600 | tf_op jit(solution)/shard_map/ppermute | solution.py:281
  21.4 2.7 %collective-permute-done.1 = f32[72,128]{1,0:T(8,128)S(1)} collective-permute-done((f32[72,128]{1,0:T(8,128)S(1)}, f32[72,128]{1,0:T(8,128)S(1)}, u32[]{:S(2)}, u32[]{:S(2)}) %collective-permute-start.1) | collective-permute-done | bytes 36896 | tf_op jit(solution)/shard_map/ppermute | solution.py:281
  24.1 9.5 %all_to_all.18 = f32[8,72,128]{2,1,0:T(8,128)S(1)} all-to-all(f32[8,72,128]{2,1,0:T(8,128)S(1)} %tile.2), channel_id=1, replica_groups={{0,2,4,6,8,10,12,14},{16,18,20,22,24,26,28,30},{1,3,5,7,9,11,13,15},{17..., dimensions={0} | all-to-all | bytes 589824 | tf_op jit(solution)/shard_map/all_to_all | solution.py:292
  33.6 0.0 copy-start.2
  33.6 0.0 copy-start.3
  33.6 0.0 copy-start
  33.6 0.0 copy-start.1
  33.6 0.1 collective-permute-start.2
  33.7 1.6 %collective-permute-done.2.other_ref = f32[576,128]{1,0:T(8,128)S(1)} collective-permute-done((f32[576,128]{1,0:T(8,128)S(1)}, f32[576,128]{1,0:T(8,128)S(1)}, u32[]{:S(2)}, u32[]{:S(2)}) %collective-permute-start.2) | collective-permute-done | bytes 294944 | tf_op jit(solution)/shard_map/ppermute | solution.py:272
  35.3 0.0 copy-done.2
  35.3 0.0 copy-done.3
  35.3 16.7 %shard_map.47 = (f32[256,256]{1,0:T(8,128)S(1)}, f32[256,256]{1,0:T(8,128)S(1)}) custom-call(s32[1]{0:T(128)} %bitcast.where_ref, f32[16]{0:T(128)S(1)} %copy-done.3, f32[16]{0:T(128)S(1)} %copy-done.2, f32[576,128]{1,0:T(8,128)S(1)} %bitcast.4, f32[576,128]{1,0:T(8,128)S(1)} %collective-permute-done.2.other_ref), custom_call_target="tpu_custom_call" | custom-call | flops 99999997952 | bytes 1000000 | tf_op jit(solution)/shard_map/pallas_call | solution.py:331
  52.0 0.2 collective-permute-start.3
  52.2 0.0 copy-done
  52.2 0.0 copy-done.1
  52.2 0.6 %shard_map.48 = (bf16[1024,256]{1,0:T(8,128)(2,1)S(1)}, bf16[1024,256]{1,0:T(8,128)(2,1)S(1)}) custom-call(f32[256,256]{1,0:T(8,128)S(1)} %get-tuple-element.14.cross_ref, f32[1024,256]{1,0:T(8,128)S(1)} %copy-done, f32[1024,256]{1,0:T(8,128)S(1)} %copy-done.1), custom_call_target="tpu_custom_call" | custom-call | flops 1000000000 | bytes 3000000 | tf_op jit(solution)/shard_map/pallas_call | solution.py:349
  52.8 0.8 %collective-permute-done.3.other_ref = f32[256,256]{1,0:T(8,128)S(1)} collective-permute-done((f32[256,256]{1,0:T(8,128)S(1)}, f32[256,256]{1,0:T(8,128)S(1)}, u32[]{:S(2)}, u32[]{:S(2)}) %collective-permute-start.3) | collective-permute-done | bytes 262176 | tf_op jit(solution)/shard_map/ppermute | solution.py:272
  53.6 1.7 %shard_map.49 = f32[1024,256]{1,0:T(8,128)} custom-call(f32[256,256]{1,0:T(8,128)S(1)} %get-tuple-element.13.mine_ref, f32[256,256]{1,0:T(8,128)S(1)} %collective-permute-done.3.other_ref, f32[256,256]{1,0:T(8,128)S(1)} %get-tuple-element.14.cross_ref, bf16[1024,256]{1,0:T(8,128)(2,1)S(1)} %get-tuple-element.15.high_ref, ...), custom_call_target="tpu_custom_call" | custom-call | tf_op jit(solution)/shard_map/pallas_call | solution.py:357
  (4 shorter events, 0.1 us)
Async XLA Ops:
  3.5 1.7 %collective-permute-start = (f32[576,128]{1,0:T(8,128)S(1)}, f32[576,128]{1,0:T(8,128)S(1)}, u32[]{:S(2)}, u32[]{:S(2)}) collective-permute-start(f32[576,128]{1,0:T(8,128)S(1)} %get-tuple-element.12), channel_id=1, source_target_pairs={{0,1},{1,0},{2,3},{3,2},{4,5},{5,4},{6,7},{7,6},{8,9},{9,8},{10,11... | collective-permute-start | bytes 884744 | tf_op jit(solution)/shard_map/ppermute | solution.py:272
  18.8 5.3 %collective-permute-start.1 = (f32[72,128]{1,0:T(8,128)S(1)}, f32[72,128]{1,0:T(8,128)S(1)}, u32[]{:S(2)}, u32[]{:S(2)}) collective-permute-start(f32[72,128]{1,0:T(8,128)S(1)} %reduce_sum.9), channel_id=1, source_target_pairs={{0,16},{1,17},{2,18},{3,19},{4,20},{5,21},{6,22},{7,23},{8,24},{9,... | collective-permute-start | bytes 110600 | tf_op jit(solution)/shard_map/ppermute | solution.py:281
  33.6 1.7 %copy-start.2 = (f32[16]{0:T(128)S(1)}, f32[16]{0:T(128)}, u32[]{:S(2)}) copy-start(f32[16]{0:T(128)} %constant.11.clone.weight_ref) | copy-start | bytes 196
  33.6 1.7 %copy-start.3 = (f32[16]{0:T(128)S(1)}, f32[16]{0:T(128)}, u32[]{:S(2)}) copy-start(f32[16]{0:T(128)} %constant.10.clone.shift_ref) | copy-start | bytes 196
  33.6 18.6 %copy-start = (f32[1024,256]{1,0:T(8,128)S(1)}, f32[1024,256]{1,0:T(8,128)}, u32[]{:S(2)}) copy-start(f32[1024,256]{1,0:T(8,128)} %b_ref.1) | copy-start | bytes 3145732
  33.6 18.6 %copy-start.1 = (f32[1024,256]{1,0:T(8,128)S(1)}, f32[1024,256]{1,0:T(8,128)}, u32[]{:S(2)}) copy-start(f32[1024,256]{1,0:T(8,128)} %t_ref.1) | copy-start | bytes 3145732
  33.6 1.6 %collective-permute-start.2 = (f32[576,128]{1,0:T(8,128)S(1)}, f32[576,128]{1,0:T(8,128)S(1)}, u32[]{:S(2)}, u32[]{:S(2)}) collective-permute-start(f32[576,128]{1,0:T(8,128)S(1)} %bitcast.3), channel_id=1, source_target_pairs={{0,1},{1,0},{2,3},{3,2},{4,5},{5,4},{6,7},{7,6},{8,9},{9,8},{10,11... | collective-permute-start | bytes 884744 | tf_op jit(solution)/shard_map/ppermute | solution.py:272
  52.0 1.6 %collective-permute-start.3 = (f32[256,256]{1,0:T(8,128)S(1)}, f32[256,256]{1,0:T(8,128)S(1)}, u32[]{:S(2)}, u32[]{:S(2)}) collective-permute-start(f32[256,256]{1,0:T(8,128)S(1)} %get-tuple-element.13.mine_ref), channel_id=1, source_target_pairs={{0,1},{1,0},{2,3},{3,2},{4,5},{5,4},{6,7},{7,6},{8,9},{9,8},{10,11... | collective-permute-start | bytes 786440 | tf_op jit(solution)/shard_map/ppermute | solution.py:272

commit v12 on v9

--- a/solution.py
+++ b/solution.py
@@ -160,8 +160,9 @@
     tgram = upper + upper.T + jnp.where(row == col, tdiag, 0.0)
     bgram = lower + lower.T + jnp.where(row == col, bdiag, 0.0)
     crosst = cross.T
-    square = dot(crosst, cross)
-    normal = tgram - 2.0 * square + dot(crosst, dot(bgram, cross))
+    left, right = halves(crosst), halves(cross)
+    square = dot3(left, right)
+    normal = tgram - 2.0 * square + dot3(left, halves(dot3(halves(bgram), right)))
     for m in range(NODES):
         shifted = square + shift_ref[core * NODES + m] * normal
         mats[0, m * n : (m + 1) * n, :] = shifted[:, 0:128]

time: 55.2 us -> 54.7 us (level)
  no operation moved by 1% of the time
where the time goes in v12:
time: 54.7 us; the launch traced here: 54.5 us
  blocking collectives  23 us (42%)
  Pallas kernels  21.7 us (40%)
  waiting for transfers between devices  6.25 us (11%)
  starting transfers between devices  3.44 us (6%)
    all_to_all x2, blocking collectives, cube(): lax.all_to_all(pieces, ('gx', 'gy'), 0, 0, axis_index_groups=groups, tile...  23 us
    pallas_call x1, Pallas kernels, on_device(): pl.pallas_call(resolvent_kernel, out_shape=(square, square), in_specs=[sm...  15.8 us
    ppermute x3, waiting for transfers between devices, swap_cores(): return lax.ppermute(x, 'gz', [(0, 1), (1, 0)])  3.58 us
    pallas_call x1, Pallas kernels, on_device(): pl.pallas_call(gram_kernel, out_shape=(half, half), in_specs=[smem, hbm,...  3.52 us
    ppermute x1, waiting for transfers between devices, swap_bits(): return lax.ppermute(x, ('gx', 'gy', 'gz'), perm)  2.66 us
    ppermute x1, starting transfers between devices, swap_bits(): return lax.ppermute(x, ('gx', 'gy', 'gz'), perm)  2.65 us
    pallas_call x1, Pallas kernels, on_device(): pl.pallas_call(functools.partial(lift_kernel, float(np.sqrt(total_rows)))...  1.74 us
  transfers between devices with their start and end apart: 4, of which 4 were waited for; matrix products, arithmetic and copies ran while one was open for 0% of the time, Pallas kernels for 1%

profile of v12, /device:TPU:0, one launch (start us, length us, event | category | flops | bytes accessed | tf_op | source)
XLA Modules:
  0.0 54.5 jit_solution(343439025625491702)
XLA Ops:
  0.0 3.5 %shard_map.46 = (f32[576,128]{1,0:T(8,128)S(1)}, f32[576,128]{1,0:T(8,128)S(1)}) custom-call(s32[1]{0:T(128)} %bitcast.where_ref, f32[1024,256]{1,0:T(8,128)} %b_ref.1, f32[1024,256]{1,0:T(8,128)} %t_ref.1), custom_call_target="tpu_custom_call" | custom-call | tf_op jit(solution)/shard_map/pallas_call | solution.py:294
  3.5 0.5 collective-permute-start
  4.1 1.2 %collective-permute-done = f32[576,128]{1,0:T(8,128)S(1)} collective-permute-done((f32[576,128]{1,0:T(8,128)S(1)}, f32[576,128]{1,0:T(8,128)S(1)}, u32[]{:S(2)}, u32[]{:S(2)}) %collective-permute-start) | collective-permute-done | bytes 294944 | tf_op jit(solution)/shard_map/ppermute | solution.py:251
  5.3 13.5 %all_to_all.17 = f32[8,72,128]{2,1,0:T(8,128)S(1)} all-to-all(f32[8,72,128]{2,1,0:T(8,128)S(1)} %bitcast.5), channel_id=1, replica_groups={{0,2,4,6,8,10,12,14},{16,18,20,22,24,26,28,30},{1,3,5,7,9,11,13,15},{17..., dimensions={0} | all-to-all | bytes 589824 | tf_op jit(solution)/shard_map/all_to_all | solution.py:271
  18.8 2.7 %collective-permute-start.1 = (f32[72,128]{1,0:T(8,128)S(1)}, f32[72,128]{1,0:T(8,128)S(1)}, u32[]{:S(2)}, u32[]{:S(2)}) collective-permute-start(f32[72,128]{1,0:T(8,128)S(1)} %reduce_sum.9), channel_id=1, source_target_pairs={{0,16},{1,17},{2,18},{3,19},{4,20},{5,21},{6,22},{7,23},{8,24},{9,... | collective-permute-start | bytes 110600 | tf_op jit(solution)/shard_map/ppermute | solution.py:260
  21.4 2.7 %collective-permute-done.1 = f32[72,128]{1,0:T(8,128)S(1)} collective-permute-done((f32[72,128]{1,0:T(8,128)S(1)}, f32[72,128]{1,0:T(8,128)S(1)}, u32[]{:S(2)}, u32[]{:S(2)}) %collective-permute-start.1) | collective-permute-done | bytes 36896 | tf_op jit(solution)/shard_map/ppermute | solution.py:260
  24.1 9.5 %all_to_all.18 = f32[8,72,128]{2,1,0:T(8,128)S(1)} all-to-all(f32[8,72,128]{2,1,0:T(8,128)S(1)} %tile.2), channel_id=1, replica_groups={{0,2,4,6,8,10,12,14},{16,18,20,22,24,26,28,30},{1,3,5,7,9,11,13,15},{17..., dimensions={0} | all-to-all | bytes 589824 | tf_op jit(solution)/shard_map/all_to_all | solution.py:271
  33.6 0.0 copy-start.2
  33.6 0.0 copy-start.3
  33.6 0.0 copy-start
  33.6 0.0 copy-start.1
  33.6 0.1 collective-permute-start.2
  33.7 1.6 %collective-permute-done.2.other_ref = f32[576,128]{1,0:T(8,128)S(1)} collective-permute-done((f32[576,128]{1,0:T(8,128)S(1)}, f32[576,128]{1,0:T(8,128)S(1)}, u32[]{:S(2)}, u32[]{:S(2)}) %collective-permute-start.2) | collective-permute-done | bytes 294944 | tf_op jit(solution)/shard_map/ppermute | solution.py:251
  35.3 0.0 copy-done.2
  35.3 0.0 copy-done.3
  35.3 15.8 %shard_map.47 = (f32[256,256]{1,0:T(8,128)S(1)}, f32[256,256]{1,0:T(8,128)S(1)}) custom-call(s32[1]{0:T(128)} %bitcast.where_ref, f32[16]{0:T(128)S(1)} %copy-done.3, f32[16]{0:T(128)S(1)} %copy-done.2, f32[576,128]{1,0:T(8,128)S(1)} %bitcast.4, f32[576,128]{1,0:T(8,128)S(1)} %collective-permute-done.2.other_ref), custom_call_target="tpu_custom_call" | custom-call | flops 99999997952 | bytes 1000000 | tf_op jit(solution)/shard_map/pallas_call | solution.py:310
  51.1 0.2 collective-permute-start.3
  51.3 0.0 copy-done
  51.3 0.0 copy-done.1
  51.3 0.6 %shard_map.48 = (bf16[1024,256]{1,0:T(8,128)(2,1)S(1)}, bf16[1024,256]{1,0:T(8,128)(2,1)S(1)}) custom-call(f32[256,256]{1,0:T(8,128)S(1)} %get-tuple-element.14.cross_ref, f32[1024,256]{1,0:T(8,128)S(1)} %copy-done, f32[1024,256]{1,0:T(8,128)S(1)} %copy-done.1), custom_call_target="tpu_custom_call" | custom-call | flops 1000000000 | bytes 3000000 | tf_op jit(solution)/shard_map/pallas_call | solution.py:326
  51.9 0.8 %collective-permute-done.3.other_ref = f32[256,256]{1,0:T(8,128)S(1)} collective-permute-done((f32[256,256]{1,0:T(8,128)S(1)}, f32[256,256]{1,0:T(8,128)S(1)}, u32[]{:S(2)}, u32[]{:S(2)}) %collective-permute-start.3) | collective-permute-done | bytes 262176 | tf_op jit(solution)/shard_map/ppermute | solution.py:251
  52.7 1.7 %shard_map.49 = f32[1024,256]{1,0:T(8,128)} custom-call(f32[256,256]{1,0:T(8,128)S(1)} %get-tuple-element.13.mine_ref, f32[256,256]{1,0:T(8,128)S(1)} %collective-permute-done.3.other_ref, f32[256,256]{1,0:T(8,128)S(1)} %get-tuple-element.14.cross_ref, bf16[1024,256]{1,0:T(8,128)(2,1)S(1)} %get-tuple-element.15.high_ref, ...), custom_call_target="tpu_custom_call" | custom-call | tf_op jit(solution)/shard_map/pallas_call | solution.py:334
  (4 shorter events, 0.1 us)
Async XLA Ops:
  3.5 1.7 %collective-permute-start = (f32[576,128]{1,0:T(8,128)S(1)}, f32[576,128]{1,0:T(8,128)S(1)}, u32[]{:S(2)}, u32[]{:S(2)}) collective-permute-start(f32[576,128]{1,0:T(8,128)S(1)} %get-tuple-element.12), channel_id=1, source_target_pairs={{0,1},{1,0},{2,3},{3,2},{4,5},{5,4},{6,7},{7,6},{8,9},{9,8},{10,11... | collective-permute-start | bytes 884744 | tf_op jit(solution)/shard_map/ppermute | solution.py:251
  18.8 5.3 %collective-permute-start.1 = (f32[72,128]{1,0:T(8,128)S(1)}, f32[72,128]{1,0:T(8,128)S(1)}, u32[]{:S(2)}, u32[]{:S(2)}) collective-permute-start(f32[72,128]{1,0:T(8,128)S(1)} %reduce_sum.9), channel_id=1, source_target_pairs={{0,16},{1,17},{2,18},{3,19},{4,20},{5,21},{6,22},{7,23},{8,24},{9,... | collective-permute-start | bytes 110600 | tf_op jit(solution)/shard_map/ppermute | solution.py:260
  33.6 1.7 %copy-start.2 = (f32[16]{0:T(128)S(1)}, f32[16]{0:T(128)}, u32[]{:S(2)}) copy-start(f32[16]{0:T(128)} %constant.11.clone.weight_ref) | copy-start | bytes 196
  33.6 1.7 %copy-start.3 = (f32[16]{0:T(128)S(1)}, f32[16]{0:T(128)}, u32[]{:S(2)}) copy-start(f32[16]{0:T(128)} %constant.10.clone.shift_ref) | copy-start | bytes 196
  33.6 17.7 %copy-start = (f32[1024,256]{1,0:T(8,128)S(1)}, f32[1024,256]{1,0:T(8,128)}, u32[]{:S(2)}) copy-start(f32[1024,256]{1,0:T(8,128)} %b_ref.1) | copy-start | bytes 3145732
  33.6 17.7 %copy-start.1 = (f32[1024,256]{1,0:T(8,128)S(1)}, f32[1024,256]{1,0:T(8,128)}, u32[]{:S(2)}) copy-start(f32[1024,256]{1,0:T(8,128)} %t_ref.1) | copy-start | bytes 3145732
  33.6 1.6 %collective-permute-start.2 = (f32[576,128]{1,0:T(8,128)S(1)}, f32[576,128]{1,0:T(8,128)S(1)}, u32[]{:S(2)}, u32[]{:S(2)}) collective-permute-start(f32[576,128]{1,0:T(8,128)S(1)} %bitcast.3), channel_id=1, source_target_pairs={{0,1},{1,0},{2,3},{3,2},{4,5},{5,4},{6,7},{7,6},{8,9},{9,8},{10,11... | collective-permute-start | bytes 884744 | tf_op jit(solution)/shard_map/ppermute | solution.py:251
  51.1 1.6 %collective-permute-start.3 = (f32[256,256]{1,0:T(8,128)S(1)}, f32[256,256]{1,0:T(8,128)S(1)}, u32[]{:S(2)}, u32[]{:S(2)}) collective-permute-start(f32[256,256]{1,0:T(8,128)S(1)} %get-tuple-element.13.mine_ref), channel_id=1, source_target_pairs={{0,1},{1,0},{2,3},{3,2},{4,5},{5,4},{6,7},{7,6},{8,9},{9,8},{10,11... | collective-permute-start | bytes 786440 | tf_op jit(solution)/shard_map/ppermute | solution.py:251

commit v13 on v12

--- a/solution.py
+++ b/solution.py
@@ -141,7 +141,7 @@
 
 
 def resolvent_kernel(
-    where_ref, shift_ref, weight_ref, mine_ref, other_ref, out_ref, cross_ref, mats, turned, inverses, news, pay
+    where_ref, shift_ref, weight_ref, mine_ref, other_ref, out_ref, cross_ref, mats, turned, inverses, news, stacks, pay
 ):
     n = out_ref.shape[1]
     half, core = mine_ref.shape[0], where_ref[0]
@@ -198,7 +198,9 @@
             here = pl.ds(pl.multiple_of(m * n + start, STEP), STEP)
             panel = jnp.concatenate([mats[0, here, :], mats[1, here, :]], 1)
             panel = jnp.where(inblock, minus, panel)
-            news[m] = jnp.dot(left, stack(panel), preferred_element_type=F32)
+            new = jnp.dot(left, stack(panel), preferred_element_type=F32)
+            news[m] = new
+            stacks[m] = stack(new)
         for m in range(NODES):
             rows = slice(m * n, (m + 1) * n)
             columns = jnp.take_along_axis(mats[tile, rows, :], index, axis=1)
@@ -206,7 +208,7 @@
             one = jnp.where(group == 2, d, h)
             two = jnp.where((group == 0) | (group == 3), l, d)
             lhs = jnp.concatenate([one, two], 1).astype(BF16)
-            change = jnp.dot(lhs, stack(news[m]), preferred_element_type=F32)
+            change = jnp.dot(lhs, stacks[m], preferred_element_type=F32)
             for c in range(2):
                 half = slice(c * 128, (c + 1) * 128)
                 old = mats[c, rows, :]
@@ -317,6 +319,7 @@
             pltpu.VMEM((2, 128, 128), F32),
             pltpu.VMEM((2, 2 * 128, 128), F32),
             pltpu.VMEM((NODES, STEP, n), F32),
+            pltpu.VMEM((NODES, 8 * STEP, n), BF16),
             pltpu.VMEM((2 * pay_half, 128), F32),
         ],
         compiler_params=limit,

time: 54.7 us -> 55 us (level)
  no operation moved by 1% of the time
where the time goes in v13:
time: 55 us; the launch traced here: 54.8 us
  blocking collectives  23 us (42%)
  Pallas kernels  22 us (40%)
  waiting for transfers between devices  6.24 us (11%)
  starting transfers between devices  3.44 us (6%)
    all_to_all x2, blocking collectives, cube(): lax.all_to_all(pieces, ('gx', 'gy'), 0, 0, axis_index_groups=groups, tile...  23 us
    pallas_call x1, Pallas kernels, on_device(): pl.pallas_call(resolvent_kernel, out_shape=(square, square), in_specs=[sm...  16.1 us
    ppermute x3, waiting for transfers between devices, swap_cores(): return lax.ppermute(x, 'gz', [(0, 1), (1, 0)])  3.58 us
    pallas_call x1, Pallas kernels, on_device(): pl.pallas_call(gram_kernel, out_shape=(half, half), in_specs=[smem, hbm,...  3.52 us
    ppermute x1, waiting for transfers between devices, swap_bits(): return lax.ppermute(x, ('gx', 'gy', 'gz'), perm)  2.66 us
    ppermute x1, starting transfers between devices, swap_bits(): return lax.ppermute(x, ('gx', 'gy', 'gz'), perm)  2.65 us
    pallas_call x1, Pallas kernels, on_device(): pl.pallas_call(functools.partial(lift_kernel, float(np.sqrt(total_rows)))...  1.74 us
  transfers between devices with their start and end apart: 4, of which 4 were waited for; matrix products, arithmetic and copies ran while one was open for 0% of the time, Pallas kernels for 1%

profile of v13, /device:TPU:0, one launch (start us, length us, event | category | flops | bytes accessed | tf_op | source)
XLA Modules:
  0.0 54.8 jit_solution(15524451554667866473)
XLA Ops:
  0.0 3.5 %shard_map.46 = (f32[576,128]{1,0:T(8,128)S(1)}, f32[576,128]{1,0:T(8,128)S(1)}) custom-call(s32[1]{0:T(128)} %bitcast.where_ref, f32[1024,256]{1,0:T(8,128)} %b_ref.1, f32[1024,256]{1,0:T(8,128)} %t_ref.1), custom_call_target="tpu_custom_call" | custom-call | tf_op jit(solution)/shard_map/pallas_call | solution.py:296
  3.5 0.5 collective-permute-start
  4.1 1.2 %collective-permute-done = f32[576,128]{1,0:T(8,128)S(1)} collective-permute-done((f32[576,128]{1,0:T(8,128)S(1)}, f32[576,128]{1,0:T(8,128)S(1)}, u32[]{:S(2)}, u32[]{:S(2)}) %collective-permute-start) | collective-permute-done | bytes 294944 | tf_op jit(solution)/shard_map/ppermute | solution.py:253
  5.3 13.5 %all_to_all.17 = f32[8,72,128]{2,1,0:T(8,128)S(1)} all-to-all(f32[8,72,128]{2,1,0:T(8,128)S(1)} %bitcast.5), channel_id=1, replica_groups={{0,2,4,6,8,10,12,14},{16,18,20,22,24,26,28,30},{1,3,5,7,9,11,13,15},{17..., dimensions={0} | all-to-all | bytes 589824 | tf_op jit(solution)/shard_map/all_to_all | solution.py:273
  18.8 2.7 %collective-permute-start.1 = (f32[72,128]{1,0:T(8,128)S(1)}, f32[72,128]{1,0:T(8,128)S(1)}, u32[]{:S(2)}, u32[]{:S(2)}) collective-permute-start(f32[72,128]{1,0:T(8,128)S(1)} %reduce_sum.9), channel_id=1, source_target_pairs={{0,16},{1,17},{2,18},{3,19},{4,20},{5,21},{6,22},{7,23},{8,24},{9,... | collective-permute-start | bytes 110600 | tf_op jit(solution)/shard_map/ppermute | solution.py:262
  21.4 2.7 %collective-permute-done.1 = f32[72,128]{1,0:T(8,128)S(1)} collective-permute-done((f32[72,128]{1,0:T(8,128)S(1)}, f32[72,128]{1,0:T(8,128)S(1)}, u32[]{:S(2)}, u32[]{:S(2)}) %collective-permute-start.1) | collective-permute-done | bytes 36896 | tf_op jit(solution)/shard_map/ppermute | solution.py:262
  24.1 9.5 %all_to_all.18 = f32[8,72,128]{2,1,0:T(8,128)S(1)} all-to-all(f32[8,72,128]{2,1,0:T(8,128)S(1)} %tile.2), channel_id=1, replica_groups={{0,2,4,6,8,10,12,14},{16,18,20,22,24,26,28,30},{1,3,5,7,9,11,13,15},{17..., dimensions={0} | all-to-all | bytes 589824 | tf_op jit(solution)/shard_map/all_to_all | solution.py:273
  33.6 0.0 copy-start.2
  33.6 0.0 copy-start.3
  33.6 0.0 copy-start
  33.6 0.0 copy-start.1
  33.6 0.1 collective-permute-start.2
  33.7 1.6 %collective-permute-done.2.other_ref = f32[576,128]{1,0:T(8,128)S(1)} collective-permute-done((f32[576,128]{1,0:T(8,128)S(1)}, f32[576,128]{1,0:T(8,128)S(1)}, u32[]{:S(2)}, u32[]{:S(2)}) %collective-permute-start.2) | collective-permute-done | bytes 294944 | tf_op jit(solution)/shard_map/ppermute | solution.py:253
  35.3 0.0 copy-done.2
  35.3 0.0 copy-done.3
  35.3 16.1 %shard_map.47 = (f32[256,256]{1,0:T(8,128)S(1)}, f32[256,256]{1,0:T(8,128)S(1)}) custom-call(s32[1]{0:T(128)} %bitcast.where_ref, f32[16]{0:T(128)S(1)} %copy-done.3, f32[16]{0:T(128)S(1)} %copy-done.2, f32[576,128]{1,0:T(8,128)S(1)} %bitcast.4, f32[576,128]{1,0:T(8,128)S(1)} %collective-permute-done.2.other_ref), custom_call_target="tpu_custom_call" | custom-call | flops 99999997952 | bytes 1000000 | tf_op jit(solution)/shard_map/pallas_call | solution.py:312
  51.4 0.2 collective-permute-start.3
  51.6 0.0 copy-done
  51.6 0.0 copy-done.1
  51.6 0.6 %shard_map.48 = (bf16[1024,256]{1,0:T(8,128)(2,1)S(1)}, bf16[1024,256]{1,0:T(8,128)(2,1)S(1)}) custom-call(f32[256,256]{1,0:T(8,128)S(1)} %get-tuple-element.14.cross_ref, f32[1024,256]{1,0:T(8,128)S(1)} %copy-done, f32[1024,256]{1,0:T(8,128)S(1)} %copy-done.1), custom_call_target="tpu_custom_call" | custom-call | flops 1000000000 | bytes 3000000 | tf_op jit(solution)/shard_map/pallas_call | solution.py:329
  52.2 0.8 %collective-permute-done.3.other_ref = f32[256,256]{1,0:T(8,128)S(1)} collective-permute-done((f32[256,256]{1,0:T(8,128)S(1)}, f32[256,256]{1,0:T(8,128)S(1)}, u32[]{:S(2)}, u32[]{:S(2)}) %collective-permute-start.3) | collective-permute-done | bytes 262176 | tf_op jit(solution)/shard_map/ppermute | solution.py:253
  53.0 1.7 %shard_map.49 = f32[1024,256]{1,0:T(8,128)} custom-call(f32[256,256]{1,0:T(8,128)S(1)} %get-tuple-element.13.mine_ref, f32[256,256]{1,0:T(8,128)S(1)} %collective-permute-done.3.other_ref, f32[256,256]{1,0:T(8,128)S(1)} %get-tuple-element.14.cross_ref, bf16[1024,256]{1,0:T(8,128)(2,1)S(1)} %get-tuple-element.15.high_ref, ...), custom_call_target="tpu_custom_call" | custom-call | tf_op jit(solution)/shard_map/pallas_call | solution.py:337
  (4 shorter events, 0.1 us)
Async XLA Ops:
  3.5 1.7 %collective-permute-start = (f32[576,128]{1,0:T(8,128)S(1)}, f32[576,128]{1,0:T(8,128)S(1)}, u32[]{:S(2)}, u32[]{:S(2)}) collective-permute-start(f32[576,128]{1,0:T(8,128)S(1)} %get-tuple-element.12), channel_id=1, source_target_pairs={{0,1},{1,0},{2,3},{3,2},{4,5},{5,4},{6,7},{7,6},{8,9},{9,8},{10,11... | collective-permute-start | bytes 884744 | tf_op jit(solution)/shard_map/ppermute | solution.py:253
  18.8 5.3 %collective-permute-start.1 = (f32[72,128]{1,0:T(8,128)S(1)}, f32[72,128]{1,0:T(8,128)S(1)}, u32[]{:S(2)}, u32[]{:S(2)}) collective-permute-start(f32[72,128]{1,0:T(8,128)S(1)} %reduce_sum.9), channel_id=1, source_target_pairs={{0,16},{1,17},{2,18},{3,19},{4,20},{5,21},{6,22},{7,23},{8,24},{9,... | collective-permute-start | bytes 110600 | tf_op jit(solution)/shard_map/ppermute | solution.py:262
  33.6 1.7 %copy-start.2 = (f32[16]{0:T(128)S(1)}, f32[16]{0:T(128)}, u32[]{:S(2)}) copy-start(f32[16]{0:T(128)} %constant.11.clone.weight_ref) | copy-start | bytes 196
  33.6 1.7 %copy-start.3 = (f32[16]{0:T(128)S(1)}, f32[16]{0:T(128)}, u32[]{:S(2)}) copy-start(f32[16]{0:T(128)} %constant.10.clone.shift_ref) | copy-start | bytes 196
  33.6 18.0 %copy-start = (f32[1024,256]{1,0:T(8,128)S(1)}, f32[1024,256]{1,0:T(8,128)}, u32[]{:S(2)}) copy-start(f32[1024,256]{1,0:T(8,128)} %b_ref.1) | copy-start | bytes 3145732
  33.6 18.0 %copy-start.1 = (f32[1024,256]{1,0:T(8,128)S(1)}, f32[1024,256]{1,0:T(8,128)}, u32[]{:S(2)}) copy-start(f32[1024,256]{1,0:T(8,128)} %t_ref.1) | copy-start | bytes 3145732
  33.6 1.6 %collective-permute-start.2 = (f32[576,128]{1,0:T(8,128)S(1)}, f32[576,128]{1,0:T(8,128)S(1)}, u32[]{:S(2)}, u32[]{:S(2)}) collective-permute-start(f32[576,128]{1,0:T(8,128)S(1)} %bitcast.3), channel_id=1, source_target_pairs={{0,1},{1,0},{2,3},{3,2},{4,5},{5,4},{6,7},{7,6},{8,9},{9,8},{10,11... | collective-permute-start | bytes 884744 | tf_op jit(solution)/shard_map/ppermute | solution.py:253
  51.4 1.6 %collective-permute-start.3 = (f32[256,256]{1,0:T(8,128)S(1)}, f32[256,256]{1,0:T(8,128)S(1)}, u32[]{:S(2)}, u32[]{:S(2)}) collective-permute-start(f32[256,256]{1,0:T(8,128)S(1)} %get-tuple-element.13.mine_ref), channel_id=1, source_target_pairs={{0,1},{1,0},{2,3},{3,2},{4,5},{5,4},{6,7},{7,6},{8,9},{9,8},{10,11... | collective-permute-start | bytes 786440 | tf_op jit(solution)/shard_map/ppermute | solution.py:253
